TPU v7x, 32 devices: a whole 2x2x4 slice. The times are simulated.
32 devices in a mesh: gx: 4 (over z), gy: 8 (over y, x, core).
Axes of the slice: x: 2, y: 2, z: 4, core: 2. Of those that a mesh axis runs over, the one named last changes fastest.
Arguments:
- populations_in: float32 [19, 4, 128, 3072], P(None, None, 'gx', 'gy'), may hold values from 0.02 to 0.1
- marker_force: float32 [2, 3, 16384], P(None, None, ('gx', 'gy')), may hold values from -1.2 to 1.2
- marker_frac: float32 [2, 3, 16384], P(None, None, ('gx', 'gy')), may hold values from 0 to 1
- marker_cell: int32 [2, 3, 16384], P(None, None, ('gx', 'gy')), may hold values from 0 to 382, as said below
- marker_tile: int32 [2, 16384, 1], P(None, ('gx', 'gy')), may hold values from 0 to 31; in each aligned block of 512 rows (0 to 511, 512 to 1023, ..., all dimensions but the last counted through in order) at most 32 rows name the same one
Outputs:
- populations_out: float32 [19, 4, 128, 3072], P(None, None, 'gx', 'gy')
- marker_velocity: float32 [2, 3, 16384], P(None, None, ('gx', 'gy'))
Inputs may be any that keep to these rules, and one draw needn't show every extreme that they name: `marker_cell`: row 0 lies below 31, row 1 below 383, row 2 below 3, so that a marker's 2 x 2 x 2 kernel stays inside the tile that marker_tile names. `marker_tile`: in each step, of the 512 markers that one device holds at most 32 name the same tile.
All inputs are finite; a program needn't handle non-finite values.
Results may differ from a plain program's by a relative error of at most 0.0003.
Values sent between devices are 32-bit elements; how exact they have to be, the bound alone decides.
No kernel may reach another device: no remote copies, remote signals or barrier semaphores. Data moves between devices by JAX's collectives and lax.ppermute only.
A program may use at most 128 MiB of HBM per device.

v0:
```python
import jax
import jax.numpy as jnp
from jax import lax
from jax.experimental import pallas as pl
from jax.experimental.pallas import tpu as pltpu
from jax.sharding import PartitionSpec as P

LATTICE = [
    (0, 0, 0),
    (1, 0, 0),
    (-1, 0, 0),
    (0, 1, 0),
    (0, -1, 0),
    (0, 0, 1),
    (0, 0, -1),
    (1, 1, 0),
    (-1, -1, 0),
    (1, -1, 0),
    (-1, 1, 0),
    (1, 0, 1),
    (-1, 0, -1),
    (1, 0, -1),
    (-1, 0, 1),
    (0, 1, 1),
    (0, -1, -1),
    (0, 1, -1),
    (0, -1, 1),
]
WEIGHTS = [1.0 / 3.0] + [1.0 / 18.0] * 6 + [1.0 / 36.0] * 12
relax_time = 0.8
OMEGA = 1.0 / relax_time
SOURCE = 1.0 - 0.5 / relax_time
LANES = 128

X_UP = [i for i in range(19) if LATTICE[i][0] == 1]
X_DOWN = [i for i in range(19) if LATTICE[i][0] == -1]
Y_UP = [i for i in range(19) if LATTICE[i][1] == 1]
Y_DOWN = [i for i in range(19) if LATTICE[i][1] == -1]

BF = jnp.bfloat16
F32 = jnp.float32


def split2(x):
    high = x.astype(BF)
    low = (x - high.astype(F32)).astype(BF)
    return high, low


def split3(x):
    high = x.astype(BF)
    rest = x - high.astype(F32)
    middle = rest.astype(BF)
    low = (rest - middle.astype(F32)).astype(BF)
    return high, middle, low


def nt(a, b):
    return lax.dot_general(a, b, (((1,), (1,)), ((), ())), preferred_element_type=F32)


def nn(a, b):
    return lax.dot_general(a, b, (((1,), (0,)), ((), ())), preferred_element_type=F32)


def iota(shape, dim):
    return lax.broadcasted_iota(jnp.int32, shape, dim)


def slot_table(slot, slots):
    owned = slot.shape[1]
    return jnp.where(iota((slots, owned), 0) == slot, 1.0, 0.0).astype(BF)


def pack_kernel(devices, cap, steps, tile_ref, cell_ref, frac_ref, force_ref, out_ref, slot_ref, rows):
    owned = cell_ref.shape[2]
    slots = devices * cap
    lines = owned // LANES
    earlier = jnp.where(iota((owned, owned), 0) < iota((owned, owned), 1), 1.0, 0.0).astype(BF)
    octets = []
    for step in range(steps):
        tiles = jnp.concatenate(
            [tile_ref[step * lines + r : step * lines + r + 1, :] for r in range(lines)], axis=1
        )
        member = jnp.where(iota((devices, owned), 0) == tiles, 1.0, 0.0)
        rank = jnp.sum(nn(member.astype(BF), earlier) * member, axis=0, keepdims=True)
        slot = tiles * cap + rank.astype(jnp.int32)
        slot_ref[step : step + 1, :] = slot
        rows[...] = jnp.zeros_like(rows)
        for number in range(3):
            rows[number : number + 1, :] = cell_ref[number, step : step + 1, :].astype(F32)
            rows[3 + number : 4 + number, :] = frac_ref[number, step : step + 1, :]
            rows[6 + number : 7 + number, :] = force_ref[number, step : step + 1, :]
        parts = jnp.concatenate(split3(rows[...]), axis=0)
        packed = nt(parts, slot_table(slot, slots))
        packed = packed[0:16] + packed[16:32] + packed[32:48]
        octets += [packed[0:8], packed[8:16]]
    group = iota((8, LANES), 1) // cap
    per = LANES // cap
    for device in range(devices):
        line, place = device // per, device % per
        block = jnp.zeros((8, LANES), F32)
        for number, octet in enumerate(octets):
            piece = octet[:, line * LANES : (line + 1) * LANES]
            shift = (number - place) * cap % LANES
            if shift:
                piece = pltpu.roll(piece, shift, 1)
            block = jnp.where(group == number, piece, block)
        out_ref[device] = block


def gather_octet(recv_ref, cap, number):
    devices = recv_ref.shape[0]
    per = LANES // cap
    group = iota((8, LANES), 1) // cap
    pieces = []
    for line in range(devices // per):
        total = jnp.zeros((8, LANES), F32)
        for place in range(per):
            piece = recv_ref[line * per + place]
            shift = (place - number) * cap % LANES
            if shift:
                piece = pltpu.roll(piece, shift, 1)
            total = jnp.where(group == place, piece, total)
        pieces.append(total)
    return jnp.concatenate(pieces, axis=1)


def unpack_kernel(cap, steps, recv_ref, slot_ref, out_ref):
    rows = gather_octet(recv_ref, cap, 0)
    slots = rows.shape[1]
    parts = jnp.concatenate(split3(jnp.concatenate([rows, rows], axis=0)), axis=0)
    for step in range(steps):
        found = nn(parts, slot_table(slot_ref[step : step + 1, :], slots))
        found = found[0:8] + found[16:24] + found[32:40]
        for number in range(3):
            out_ref[number, step : step + 1, :] = found[step * 3 + number : step * 3 + number + 1]


def line_weights(cell, frac, extent):
    grid = iota((extent, cell.shape[1]), 0).astype(F32)
    return jnp.where(grid == cell, 1.0 - frac, jnp.where(grid == cell + 1.0, frac, 0.0))


def y_table(cell, frac, extent):
    grid = iota((extent, cell.shape[1]), 0).astype(F32)
    lower, upper = grid == cell, grid == cell + 1.0
    tables = []
    for low, high in zip(split2(1.0 - frac), split2(frac)):
        low, high = low.astype(F32), high.astype(F32)
        tables.append(jnp.where(lower, low, jnp.where(upper, high, 0.0)).astype(BF))
    return tables


def plane_table(rows, planes, width_x):
    kernel_x = line_weights(rows[0:1], rows[3:4], width_x)
    kernel_z = line_weights(rows[2:3], rows[5:6], 8)
    return [kernel_z[z : z + 1] * kernel_x for z in range(planes)]


def spread(first, second, planes, width_x, width_y, force_ref):
    table = jnp.concatenate(plane_table(first, planes, width_x), axis=0)
    along_y = y_table(first[1:2], first[4:5], width_y)
    size = planes * width_x
    for number, strength in enumerate((first[6:7], first[7:8], second[0:1])):
        high, low = split2(table * strength)
        force_ref[number * size : (number + 1) * size, :] = (
            nt(high, along_y[0]) + nt(high, along_y[1]) + nt(low, along_y[0])
        )


def sample(first, planes, width_x, width_y, probe_ref):
    table = jnp.concatenate(plane_table(first, planes, width_x), axis=0)
    along_y = y_table(first[1:2], first[4:5], width_y)
    size = planes * width_x
    rows = []
    for number in range(3):
        high, low = split2(probe_ref[number * size : (number + 1) * size, :])
        found = nn(high, along_y[0]) + nn(high, along_y[1]) + nn(low, along_y[0])
        rows.append(jnp.sum(found * table, axis=0, keepdims=True))
    return rows


def moments(f):
    density = f[0]
    diff = {}
    for member in range(1, 19, 2):
        density = density + (f[member] + f[member + 1])
        diff[member] = f[member] - f[member + 1]
    momenta = []
    for number in range(3):
        total = None
        for member in range(1, 19, 2):
            sign = LATTICE[member][number]
            if sign == 0:
                continue
            if total is None:
                total = diff[member] if sign == 1 else -diff[member]
            else:
                total = total + diff[member] if sign == 1 else total - diff[member]
        momenta.append(total)
    return density, momenta


def dot_c(vector, comps):
    total = None
    for number in range(3):
        if vector[number] == 0:
            continue
        if total is None:
            total = comps[number] if vector[number] == 1 else -comps[number]
        else:
            total = total + comps[number] if vector[number] == 1 else total - comps[number]
    return total


def collide(f, density, momenta, force):
    inverse = 1.0 / density
    speed = [(momenta[n] + 0.5 * force[n]) * inverse for n in range(3)]
    scaled = OMEGA * density
    speed_sq = speed[0] * speed[0] + speed[1] * speed[1] + speed[2] * speed[2]
    along = speed[0] * force[0] + speed[1] * force[1] + speed[2] * force[2]
    base = scaled * (1.0 - 1.5 * speed_sq) - (3.0 * SOURCE) * along
    flow = [scaled * speed[n] for n in range(3)]
    pull = [(3.0 * SOURCE) * force[n] for n in range(3)]
    linear = [3.0 * flow[n] + pull[n] for n in range(3)]
    square = [4.5 * flow[n] + 3.0 * pull[n] for n in range(3)]
    posts = [(1.0 - OMEGA) * f[0] + WEIGHTS[0] * base]
    for member in range(1, 19, 2):
        vector = LATTICE[member]
        even = WEIGHTS[member] * (base + dot_c(vector, speed) * dot_c(vector, square))
        odd = WEIGHTS[member] * dot_c(vector, linear)
        posts.append((1.0 - OMEGA) * f[member] + (even + odd))
        posts.append((1.0 - OMEGA) * f[member + 1] + (even - odd))
    return posts


def send_faces(post_ref, x_up, x_down, y_up, y_down):
    planes, width_x, width_y = post_ref.shape[1], post_ref.shape[2], post_ref.shape[3]
    for out, members, row in ((x_up, X_UP, width_x - 1), (x_down, X_DOWN, 0)):
        out[...] = jnp.zeros_like(out)
        for place, member in enumerate(members):
            for z in range(planes):
                number = place * planes + z
                out[number : number + 1, :] = post_ref[member, z, row : row + 1, :]
    lane = iota((width_x, LANES), 1)
    count = 5 * planes
    for out, members, start, at in ((y_up, Y_UP, width_y - LANES, LANES - 1), (y_down, Y_DOWN, 0, 0)):
        total = jnp.zeros((width_x, LANES), F32)
        for place, member in enumerate(members):
            for z in range(planes):
                number = place * planes + z
                block = post_ref[member, z, :, start : start + LANES]
                if LATTICE[member][0]:
                    block = pltpu.roll(block, LATTICE[member][0] % width_x, 0)
                if (number - at) % LANES:
                    block = pltpu.roll(block, (number - at) % LANES, 1)
                total = jnp.where(lane == number, block, total)
        packed = jnp.zeros((8, LANES), F32)
        group = iota((8, LANES), 1) // count
        for number in range(width_x // 8):
            piece = total[number * 8 : number * 8 + 8]
            if number:
                piece = pltpu.roll(piece, number * count, 1)
            packed = jnp.where(group == number, piece, packed)
        out[...] = packed


def corner_kernel(planes, width_x, y_up, y_down, x_low, x_high, out_up, out_down):
    count = 5 * planes
    width_y = x_low.shape[1]
    lane, row = iota((8, LANES), 1), iota((8, LANES), 0)
    for source, out, members, start, at in (
        (y_up, out_up, Y_UP, width_y - LANES, LANES - 1),
        (y_down, out_down, Y_DOWN, 0, 0),
    ):
        block = source[...]
        for place, member in enumerate(members):
            along = LATTICE[member][0]
            if along == 0:
                continue
            halo, order = (x_low, X_UP) if along == 1 else (x_high, X_DOWN)
            group, sub = (0, 0) if along == 1 else (width_x // 8 - 1, 7)
            for z in range(planes):
                number = order.index(member) * planes + z
                target = group * count + place * planes + z
                piece = jnp.broadcast_to(halo[number : number + 1, start : start + LANES], (8, LANES))
                if (target - at) % LANES:
                    piece = pltpu.roll(piece, (target - at) % LANES, 1)
                block = jnp.where((lane == target) & (row == sub), piece, block)
        out[...] = block


def stream(post_ref, x_low, x_high, y_low, y_high, out_ref):
    planes, width_x, width_y = post_ref.shape[1], post_ref.shape[2], post_ref.shape[3]
    count = 5 * planes
    rows = iota((width_x, width_y), 0)
    lane = iota((width_x, LANES), 1)
    low, high = y_low[...], y_high[...]
    for member in range(19):
        along_x, along_y, along_z = LATTICE[member]
        for z in range(planes):
            block = post_ref[member, z]
            if along_x == 1:
                number = X_UP.index(member) * planes + z
                block = jnp.where(rows == 0, x_low[number : number + 1, :], pltpu.roll(block, 1, 0))
            elif along_x == -1:
                number = X_DOWN.index(member) * planes + z
                block = jnp.where(
                    rows == width_x - 1,
                    x_high[number : number + 1, :],
                    pltpu.roll(block, width_x - 1, 0),
                )
            to = (z + along_z) % planes
            if along_y == 0:
                out_ref[member, to] = block
                continue
            halo, order, at = (low, Y_UP, 0) if along_y == 1 else (high, Y_DOWN, LANES - 1)
            number = order.index(member) * planes + z
            edge = []
            for group in range(width_x // 8):
                shift = (at - group * count - number) % LANES
                edge.append(pltpu.roll(halo, shift, 1) if shift else halo)
            edge = jnp.concatenate(edge, axis=0)
            block = pltpu.roll(block, along_y % width_y, 1)
            start = 0 if along_y == 1 else width_y - LANES
            first = jnp.where(lane == at, edge, block[:, start : start + LANES])
            if along_y == 1:
                block = jnp.concatenate([first, block[:, LANES:]], axis=1)
            else:
                block = jnp.concatenate([block[:, :start], first], axis=1)
            out_ref[member, to] = block


def blocks(planes, width_x, width_y, body):
    per = width_x // 8

    @pl.loop(0, planes * per)
    def _(index):
        z = index // per
        row = pl.multiple_of((index % per) * 8, 8)
        flat = pl.multiple_of(index * 8, 8)
        for start in range(0, width_y, LANES):
            body(z, pl.ds(row, 8), flat, pl.ds(start, LANES))


def spread_kernel(cap, step, planes, width_x, recv_ref, force_ref):
    first = gather_octet(recv_ref, cap, 2 * step)
    second = gather_octet(recv_ref, cap, 2 * step + 1)
    spread(first, second, planes, width_x, force_ref.shape[1], force_ref)


def first_kernel(cap, recv_ref, f_ref, force_ref, post_ref, x_up, x_down, y_up, y_down):
    planes, width_x, width_y = f_ref.shape[1], f_ref.shape[2], f_ref.shape[3]
    spread_kernel(cap, 0, planes, width_x, recv_ref, force_ref)
    size = planes * width_x

    def body(z, row, flat, lanes):
        f = [f_ref[member, z, row, lanes] for member in range(19)]
        force = [force_ref[pl.ds(number * size + flat, 8), lanes] for number in range(3)]
        density, momenta = moments(f)
        for member, value in enumerate(collide(f, density, momenta, force)):
            post_ref[member, z, row, lanes] = value

    blocks(planes, width_x, width_y, body)
    send_faces(post_ref, x_up, x_down, y_up, y_down)


def middle_kernel(
    post_in, x_low, x_high, y_low, y_high, force_ref, next_ref, probe_ref, post_ref, x_up, x_down, y_up, y_down, f_ref
):
    planes, width_x, width_y = post_in.shape[1], post_in.shape[2], post_in.shape[3]
    size = planes * width_x
    stream(post_in, x_low, x_high, y_low, y_high, f_ref)

    def body(z, row, flat, lanes):
        f = [f_ref[member, z, row, lanes] for member in range(19)]
        density, momenta = moments(f)
        inverse = 1.0 / density
        force = []
        for number in range(3):
            at = pl.ds(number * size + flat, 8)
            probe_ref[at, lanes] = (momenta[number] + 0.5 * force_ref[at, lanes]) * inverse
            force.append(next_ref[at, lanes])
        for member, value in enumerate(collide(f, density, momenta, force)):
            post_ref[member, z, row, lanes] = value

    blocks(planes, width_x, width_y, body)
    send_faces(post_ref, x_up, x_down, y_up, y_down)


def sample_kernel(cap, step, planes, width_x, recv_ref, probe_ref, out_ref):
    first = gather_octet(recv_ref, cap, 2 * step)
    out_ref[...] = jnp.zeros_like(out_ref)
    for number, row in enumerate(sample(first, planes, width_x, probe_ref.shape[1], probe_ref)):
        out_ref[number : number + 1, :] = row


def last_kernel(
    cap, step, post_in, x_low, x_high, y_low, y_high, force_ref, recv_ref, sampled_ref, f_ref, out_ref, probe_ref, rows
):
    planes, width_x, width_y = post_in.shape[1], post_in.shape[2], post_in.shape[3]
    size = planes * width_x
    stream(post_in, x_low, x_high, y_low, y_high, f_ref)

    def body(z, row, flat, lanes):
        f = [f_ref[member, z, row, lanes] for member in range(19)]
        density, momenta = moments(f)
        inverse = 1.0 / density
        for number in range(3):
            at = pl.ds(number * size + flat, 8)
            probe_ref[at, lanes] = (momenta[number] + 0.5 * force_ref[at, lanes]) * inverse

    blocks(planes, width_x, width_y, body)
    first = gather_octet(recv_ref, cap, 2 * step)
    rows[...] = sampled_ref[...]
    for number, row in enumerate(sample(first, planes, width_x, width_y, probe_ref)):
        rows[3 * step + number : 3 * step + number + 1, :] = row
    per = LANES // cap
    for device in range(out_ref.shape[0]):
        line, place = device // per, device % per
        piece = rows[:, line * LANES : (line + 1) * LANES]
        if place:
            piece = pltpu.roll(piece, LANES - place * cap, 1)
        out_ref[device] = piece


def call(kernel, outs, scratch=(), flops=0, moved=0, limit=40):
    shapes = [jax.ShapeDtypeStruct(shape, kind) for shape, kind in outs]
    return pl.pallas_call(
        kernel,
        out_shape=shapes,
        scratch_shapes=list(scratch),
        cost_estimate=pl.CostEstimate(flops=flops, bytes_accessed=moved, transcendentals=0),
        compiler_params=pltpu.CompilerParams(vmem_limit_bytes=limit * 1024 * 1024),
    )


def pair(up, down, axis):
    count = lax.axis_size(axis)
    forward = [(i, (i + 1) % count) for i in range(count)]
    backward = [(target, source) for source, target in forward]
    return lax.ppermute(up, axis, forward), lax.ppermute(down, axis, backward)


def exchange(faces, planes, width_x):
    x_up, x_down, y_up, y_down = faces
    x_low, x_high = pair(x_up, x_down, "gx")

    def kernel(*refs):
        corner_kernel(planes, width_x, *refs)

    y_up, y_down = call(kernel, [((8, LANES), F32)] * 2, moved=300000)(y_up, y_down, x_low, x_high)
    y_low, y_high = pair(y_up, y_down, "gy")
    return x_low, x_high, y_low, y_high


def local(populations_in, marker_force, marker_frac, marker_cell, marker_tile):
    devices = lax.axis_size("gx") * lax.axis_size("gy")
    steps, owned = marker_force.shape[0], marker_force.shape[2]
    cap = max(2, 2 * owned // devices)
    slots = devices * cap
    planes, width_x, width_y = populations_in.shape[1:]
    size = planes * width_x
    by_comp = lambda x: jnp.transpose(x, (1, 0, 2))

    def pack(*refs):
        pack_kernel(devices, cap, steps, *refs)

    outgoing, slot = call(
        pack,
        [((devices, 8, LANES), F32), ((steps, owned), jnp.int32)],
        [pltpu.VMEM((16, owned), F32)],
    )(
        marker_tile.reshape(steps * owned // LANES, LANES),
        by_comp(marker_cell),
        by_comp(marker_frac),
        by_comp(marker_force),
    )
    arrived = lax.all_to_all(outgoing, ("gx", "gy"), split_axis=0, concat_axis=0, tiled=True)

    field = ((3 * size, width_y), F32)
    pops = (populations_in.shape, F32)
    rows_x = -(-5 * planes // 8) * 8
    faces = [((rows_x, width_y), F32)] * 2 + [((8, LANES), F32)] * 2

    def first(*refs):
        first_kernel(cap, *refs)

    force_0, post, *sent = call(first, [field, pops] + faces)(arrived, populations_in)
    halos = exchange(sent, planes, width_x)

    def second_spread(*refs):
        spread_kernel(cap, 1, planes, width_x, *refs)

    (force_1,) = call(second_spread, [field], flops=10**9, moved=10**6)(arrived)

    probe, post, *sent = call(middle_kernel, [field, pops] + faces, [pltpu.VMEM(pops[0], F32)])(
        post, *halos, force_0, force_1
    )
    halos = exchange(sent, planes, width_x)

    def first_sample(*refs):
        sample_kernel(cap, 0, planes, width_x, *refs)

    (sampled,) = call(first_sample, [((8, slots), F32)], flops=10**9, moved=10**6)(arrived, probe)

    def last(*refs):
        last_kernel(cap, 1, *refs)

    fields, back = call(
        last,
        [pops, ((devices, 8, LANES), F32)],
        [pltpu.VMEM(field[0], F32), pltpu.VMEM((8, slots), F32)],
    )(post, *halos, force_1, arrived, sampled)
    returned = lax.all_to_all(back, ("gx", "gy"), split_axis=0, concat_axis=0, tiled=True)

    def unpack(*refs):
        unpack_kernel(cap, steps, *refs)

    (velocity,) = call(unpack, [((3, steps, owned), F32)])(returned, slot)
    return fields, by_comp(velocity)


def solution(mesh):
    return jax.shard_map(
        local,
        mesh=mesh,
        in_specs=(
            P(None, None, "gx", "gy"),
            P(None, None, ("gx", "gy")),
            P(None, None, ("gx", "gy")),
            P(None, None, ("gx", "gy")),
            P(None, ("gx", "gy"), None),
        ),
        out_specs=(P(None, None, "gx", "gy"), P(None, None, ("gx", "gy"))),
        check_vma=False,
    )
```

profile of v0, /device:TPU:0, one launch (start us, length us, event | category | flops | bytes accessed | tf_op | source)
XLA Modules:
  0.0 68.5 jit_solution(3722649406988242195)
XLA Ops:
  0.6 0.0 copy-start.1
  0.6 0.7 %copy-done.1 = s32[2,3,512]{2,0,1:T(2,128)S(1)} copy-done((s32[2,3,512]{2,0,1:T(2,128)S(1)}, s32[2,3,512]{2,0,1:T(2,128)}, u32[]{:S(2)}) %copy-start.1) | copy-done | bytes 12312
  1.3 0.0 copy-start.2
  1.3 0.7 %copy-done.2 = f32[2,3,512]{2,0,1:T(2,128)S(1)} copy-done((f32[2,3,512]{2,0,1:T(2,128)S(1)}, f32[2,3,512]{2,0,1:T(2,128)}, u32[]{:S(2)}) %copy-start.2) | copy-done | bytes 12312
  2.0 0.0 copy-start.3
  2.0 0.7 %copy-done.3 = f32[2,3,512]{2,0,1:T(2,128)S(1)} copy-done((f32[2,3,512]{2,0,1:T(2,128)S(1)}, f32[2,3,512]{2,0,1:T(2,128)}, u32[]{:S(2)}) %copy-start.3) | copy-done | bytes 12312
  2.8 0.0 copy-start.4
  2.8 0.7 copy-done.4
  3.4 1.2 %shard_map.68 = (f32[32,8,128]{2,1,0:T(8,128)S(1)}, s32[2,512]{1,0:T(2,128)S(1)}) custom-call(s32[8,128]{1,0:T(8,128)S(1)} %bitcast.8, s32[3,2,512]{2,1,0:T(2,128)S(1)} %bitcast.5, f32[3,2,512]{2,1,0:T(2,128)S(1)} %bitcast.6, f32[3,2,512]{2,1,0:T(2,128)S(1)} %bitcast.7), custom_call_target="tpu_custom_call" | custom-call | tf_op jit(solution)/shard_map/pallas_call | solution.py:470
  4.6 15.3 %all_to_all.10.refs_0_.refs_6_ = f32[32,8,128]{2,1,0:T(8,128)S(1)} all-to-all(f32[32,8,128]{2,1,0:T(8,128)S(1)} %get-tuple-element.22), channel_id=1, replica_groups=mesh['gx'=4,'gy'=8] {'gx','gy'}, dimensions={0} | all-to-all | bytes 262144 | tf_op jit(solution)/shard_map/all_to_all | solution.py:480
  20.0 0.0 copy-start
  20.0 2.1 %copy-done = f32[19,4,32,384]{3,2,1,0:T(8,128)S(1)} copy-done((f32[19,4,32,384]{3,2,1,0:T(8,128)S(1)}, f32[19,4,32,384]{3,2,1,0:T(8,128)}, u32[]{:S(2)}) %copy-start) | copy-done | bytes 3735576
  22.0 4.3 %shard_map.69 = (f32[384,384]{1,0:T(8,128)S(1)}, f32[19,4,32,384]{3,2,1,0:T(8,128)S(1)}, f32[24,384]{1,0:T(8,128)S(1)}, f32[24,384]{1,0:T(8,128)S(1)}, f32[8,128]{1,0:T(8,128)S(1)}, /*index=5*/f32[8,128]{1,0:T(8,128)S(1)}) custom-call(f32[32,8,128]{2,1,0:T(8,128)S(1)} %all_to_all.10.refs_0_.refs_6_, f32[19,4,32,384]{3,2,1,0:T(8,128)S(1)} %copy-done), custom_call_target="tpu_custom_call" | custom-call | tf_op jit(solution)/shard_map/pallas_call | solution.py:490
  26.3 0.7 collective-permute-start
  27.0 3.2 %collective-permute-start.1 = (f32[24,384]{1,0:T(8,128)S(1)}, f32[24,384]{1,0:T(8,128)S(1)}, u32[]{:S(2)}, u32[]{:S(2)}) collective-permute-start(f32[24,384]{1,0:T(8,128)S(1)} %get-tuple-element.25), channel_id=1, source_target_pairs={{8,0},{16,8},{24,16},{0,24},{9,1},{17,9},{25,17},{1,25},{10,2},{18... | collective-permute-start | bytes 110600 | tf_op jit(solution)/shard_map/ppermute | solution.py:443
  30.2 2.0 %collective-permute-done.refs_2_.x_low = f32[24,384]{1,0:T(8,128)S(1)} collective-permute-done((f32[24,384]{1,0:T(8,128)S(1)}, f32[24,384]{1,0:T(8,128)S(1)}, u32[]{:S(2)}, u32[]{:S(2)}) %collective-permute-start) | collective-permute-done | bytes 36896 | tf_op jit(solution)/shard_map/ppermute | solution.py:443
  32.1 0.0 collective-permute-done.1.refs_3_.x_high
  32.1 0.1 shard_map.70
  32.2 0.1 collective-permute-start.2
  32.3 2.6 %collective-permute-start.3 = (f32[8,128]{1,0:T(8,128)S(1)}, f32[8,128]{1,0:T(8,128)S(1)}, u32[]{:S(2)}, u32[]{:S(2)}) collective-permute-start(f32[8,128]{1,0:T(8,128)S(1)} %get-tuple-element.29), channel_id=1, source_target_pairs={{1,0},{2,1},{3,2},{4,3},{5,4},{6,5},{7,6},{0,7},{9,8},{10,9},{11,1... | collective-permute-start | bytes 12296 | tf_op jit(solution)/shard_map/ppermute | solution.py:443
  34.9 2.2 %shard_map.71.next_ref.refs_5_ = f32[384,384]{1,0:T(8,128)S(1)} custom-call(f32[32,8,128]{2,1,0:T(8,128)S(1)} %all_to_all.10.refs_0_.refs_6_), custom_call_target="tpu_custom_call" | custom-call | flops 1000000000 | bytes 1000000 | tf_op jit(solution)/shard_map/pallas_call | solution.py:496
  37.2 0.0 collective-permute-done.2.y_low
  37.2 0.0 collective-permute-done.3.y_high
  37.2 2.7 %shard_map.72 = (f32[384,384]{1,0:T(8,128)S(1)}, f32[19,4,32,384]{3,2,1,0:T(8,128)S(1)}, f32[24,384]{1,0:T(8,128)S(1)}, f32[24,384]{1,0:T(8,128)S(1)}, f32[8,128]{1,0:T(8,128)S(1)}, /*index=5*/f32[8,128]{1,0:T(8,128)S(1)}) custom-call(f32[19,4,32,384]{3,2,1,0:T(8,128)S(1)} %get-tuple-element.23.post_in, f32[24,384]{1,0:T(8,128)S(1)} %collective-permute-done.refs_2_.x_low, ...), custom_call_target="tpu_custom_call" | custom-call | tf_op jit(solution)/shard_map/pallas_call | solution.py:498
  39.9 0.0 collective-permute-start.4
  40.0 3.8 %collective-permute-start.5 = (f32[24,384]{1,0:T(8,128)S(1)}, f32[24,384]{1,0:T(8,128)S(1)}, u32[]{:S(2)}, u32[]{:S(2)}) collective-permute-start(f32[24,384]{1,0:T(8,128)S(1)} %get-tuple-element.33), channel_id=1, source_target_pairs={{8,0},{16,8},{24,16},{0,24},{9,1},{17,9},{25,17},{1,25},{10,2},{18... | collective-permute-start | bytes 110600 | tf_op jit(solution)/shard_map/ppermute | solution.py:443
  43.8 2.0 %collective-permute-done.4.refs_2_.refs_1_ = f32[24,384]{1,0:T(8,128)S(1)} collective-permute-done((f32[24,384]{1,0:T(8,128)S(1)}, f32[24,384]{1,0:T(8,128)S(1)}, u32[]{:S(2)}, u32[]{:S(2)}) %collective-permute-start.4) | collective-permute-done | bytes 36896 | tf_op jit(solution)/shard_map/ppermute | solution.py:443
  45.8 0.0 collective-permute-done.5.refs_3_.refs_2_
  45.8 0.1 shard_map.73
  45.9 0.1 collective-permute-start.6
  46.0 2.6 %collective-permute-start.7 = (f32[8,128]{1,0:T(8,128)S(1)}, f32[8,128]{1,0:T(8,128)S(1)}, u32[]{:S(2)}, u32[]{:S(2)}) collective-permute-start(f32[8,128]{1,0:T(8,128)S(1)} %get-tuple-element.37), channel_id=1, source_target_pairs={{1,0},{2,1},{3,2},{4,3},{5,4},{6,5},{7,6},{0,7},{9,8},{10,9},{11,1... | collective-permute-start | bytes 12296 | tf_op jit(solution)/shard_map/ppermute | solution.py:443
  48.6 1.8 %shard_map.74.refs_7_ = f32[8,1024]{1,0:T(8,128)S(1)} custom-call(f32[32,8,128]{2,1,0:T(8,128)S(1)} %all_to_all.10.refs_0_.refs_6_, f32[384,384]{1,0:T(8,128)S(1)} %get-tuple-element.38.refs_1_), custom_call_target="tpu_custom_call" | custom-call | flops 1000000000 | bytes 1000000 | tf_op jit(solution)/shard_map/pallas_call | solution.py:506
  50.4 0.0 collective-permute-done.6.refs_3_
  50.4 0.0 collective-permute-done.7.refs_4_
  50.4 3.3 %shard_map.75 = (f32[19,4,32,384]{3,2,1,0:T(8,128)}, f32[32,8,128]{2,1,0:T(8,128)S(1)}) custom-call(f32[19,4,32,384]{3,2,1,0:T(8,128)S(1)} %get-tuple-element.31.refs_0_, f32[24,384]{1,0:T(8,128)S(1)} %collective-permute-done.4.refs_2_.refs_1_, f32[24,384]{1,0:T(8,128)S(1)} %collective-permute-done.5.refs_3_.refs_2_, ...), custom_call_target="tpu_custom_call" | custom-call | tf_op jit(solution)/shard_map/pallas_call | solution.py:511
  53.7 13.7 %all_to_all.11.refs_0_ = f32[32,8,128]{2,1,0:T(8,128)S(1)} all-to-all(f32[32,8,128]{2,1,0:T(8,128)S(1)} %get-tuple-element.40), channel_id=1, replica_groups=mesh['gx'=4,'gy'=8] {'gx','gy'}, dimensions={0} | all-to-all | bytes 262144 | tf_op jit(solution)/shard_map/all_to_all | solution.py:516
  67.4 1.1 %shard_map.76 = f32[3,2,512]{2,1,0:T(2,128)} custom-call(f32[32,8,128]{2,1,0:T(8,128)S(1)} %all_to_all.11.refs_0_, s32[2,512]{1,0:T(2,128)S(1)} %get-tuple-element.41.refs_1_), custom_call_target="tpu_custom_call" | custom-call | tf_op jit(solution)/shard_map/pallas_call | solution.py:521
Async XLA Ops:
  0.6 0.7 %copy-start.1 = (s32[2,3,512]{2,0,1:T(2,128)S(1)}, s32[2,3,512]{2,0,1:T(2,128)}, u32[]{:S(2)}) copy-start(s32[2,3,512]{2,0,1:T(2,128)} %param.8) | copy-start | bytes 36868
  1.3 0.7 %copy-start.2 = (f32[2,3,512]{2,0,1:T(2,128)S(1)}, f32[2,3,512]{2,0,1:T(2,128)}, u32[]{:S(2)}) copy-start(f32[2,3,512]{2,0,1:T(2,128)} %param.7) | copy-start | bytes 36868
  2.0 0.7 %copy-start.3 = (f32[2,3,512]{2,0,1:T(2,128)S(1)}, f32[2,3,512]{2,0,1:T(2,128)}, u32[]{:S(2)}) copy-start(f32[2,3,512]{2,0,1:T(2,128)} %param.6) | copy-start | bytes 36868
  2.8 0.7 %copy-start.4 = (s32[2,512,1]{1,2,0:T(1,128)S(1)}, s32[2,512,1]{1,2,0:T(1,128)}, u32[]{:S(2)}) copy-start(s32[2,512,1]{1,2,0:T(1,128)} %param.9) | copy-start | bytes 12292
  20.0 2.1 %copy-start = (f32[19,4,32,384]{3,2,1,0:T(8,128)S(1)}, f32[19,4,32,384]{3,2,1,0:T(8,128)}, u32[]{:S(2)}) copy-start(f32[19,4,32,384]{3,2,1,0:T(8,128)} %refs_1_.1) | copy-start | bytes 11206660
  26.3 5.8 %collective-permute-start = (f32[24,384]{1,0:T(8,128)S(1)}, f32[24,384]{1,0:T(8,128)S(1)}, u32[]{:S(2)}, u32[]{:S(2)}) collective-permute-start(f32[24,384]{1,0:T(8,128)S(1)} %get-tuple-element.24), channel_id=1, source_target_pairs={{0,8},{8,16},{16,24},{24,0},{1,9},{9,17},{17,25},{25,1},{2,10},{10... | collective-permute-start | bytes 110600 | tf_op jit(solution)/shard_map/ppermute | solution.py:443
  27.0 5.1 %collective-permute-start.1 = (f32[24,384]{1,0:T(8,128)S(1)}, f32[24,384]{1,0:T(8,128)S(1)}, u32[]{:S(2)}, u32[]{:S(2)}) collective-permute-start(f32[24,384]{1,0:T(8,128)S(1)} %get-tuple-element.25), channel_id=1, source_target_pairs={{8,0},{16,8},{24,16},{0,24},{9,1},{17,9},{25,17},{1,25},{10,2},{18... | collective-permute-start | bytes 110600 | tf_op jit(solution)/shard_map/ppermute | solution.py:443
  32.2 5.0 %collective-permute-start.2 = (f32[8,128]{1,0:T(8,128)S(1)}, f32[8,128]{1,0:T(8,128)S(1)}, u32[]{:S(2)}, u32[]{:S(2)}) collective-permute-start(f32[8,128]{1,0:T(8,128)S(1)} %get-tuple-element.28), channel_id=1, source_target_pairs={{0,1},{1,2},{2,3},{3,4},{4,5},{5,6},{6,7},{7,0},{8,9},{9,10},{10,1... | collective-permute-start | bytes 12296 | tf_op jit(solution)/shard_map/ppermute | solution.py:443
  32.3 4.9 %collective-permute-start.3 = (f32[8,128]{1,0:T(8,128)S(1)}, f32[8,128]{1,0:T(8,128)S(1)}, u32[]{:S(2)}, u32[]{:S(2)}) collective-permute-start(f32[8,128]{1,0:T(8,128)S(1)} %get-tuple-element.29), channel_id=1, source_target_pairs={{1,0},{2,1},{3,2},{4,3},{5,4},{6,5},{7,6},{0,7},{9,8},{10,9},{11,1... | collective-permute-start | bytes 12296 | tf_op jit(solution)/shard_map/ppermute | solution.py:443
  39.9 5.9 %collective-permute-start.4 = (f32[24,384]{1,0:T(8,128)S(1)}, f32[24,384]{1,0:T(8,128)S(1)}, u32[]{:S(2)}, u32[]{:S(2)}) collective-permute-start(f32[24,384]{1,0:T(8,128)S(1)} %get-tuple-element.32), channel_id=1, source_target_pairs={{0,8},{8,16},{16,24},{24,0},{1,9},{9,17},{17,25},{25,1},{2,10},{10... | collective-permute-start | bytes 110600 | tf_op jit(solution)/shard_map/ppermute | solution.py:443
  40.0 5.8 %collective-permute-start.5 = (f32[24,384]{1,0:T(8,128)S(1)}, f32[24,384]{1,0:T(8,128)S(1)}, u32[]{:S(2)}, u32[]{:S(2)}) collective-permute-start(f32[24,384]{1,0:T(8,128)S(1)} %get-tuple-element.33), channel_id=1, source_target_pairs={{8,0},{16,8},{24,16},{0,24},{9,1},{17,9},{25,17},{1,25},{10,2},{18... | collective-permute-start | bytes 110600 | tf_op jit(solution)/shard_map/ppermute | solution.py:443
  45.9 4.5 %collective-permute-start.6 = (f32[8,128]{1,0:T(8,128)S(1)}, f32[8,128]{1,0:T(8,128)S(1)}, u32[]{:S(2)}, u32[]{:S(2)}) collective-permute-start(f32[8,128]{1,0:T(8,128)S(1)} %get-tuple-element.36), channel_id=1, source_target_pairs={{0,1},{1,2},{2,3},{3,4},{4,5},{5,6},{6,7},{7,0},{8,9},{9,10},{10,1... | collective-permute-start | bytes 12296 | tf_op jit(solution)/shard_map/ppermute | solution.py:443
  46.0 4.4 %collective-permute-start.7 = (f32[8,128]{1,0:T(8,128)S(1)}, f32[8,128]{1,0:T(8,128)S(1)}, u32[]{:S(2)}, u32[]{:S(2)}) collective-permute-start(f32[8,128]{1,0:T(8,128)S(1)} %get-tuple-element.37), channel_id=1, source_target_pairs={{1,0},{2,1},{3,2},{4,3},{5,4},{6,5},{7,6},{0,7},{9,8},{10,9},{11,1... | collective-permute-start | bytes 12296 | tf_op jit(solution)/shard_map/ppermute | solution.py:443
where the time goes:
time: 68.9 us; the launch traced here: 68.5 us
  blocking collectives  29 us (42%)
  Pallas kernels  16.8 us (24%)
  starting transfers between devices  13.1 us (19%)
  local copies, waits for them, and re-layouts  4.86 us (7%)
  waiting for transfers between devices  3.99 us (6%)
  between operations  0.74 us (1%)
    all_to_all x1, blocking collectives, local(): lax.all_to_all(outgoing, ('gx', 'gy'), split_axis=0, concat_axis=0, tiled...  15.3 us
    all_to_all x1, blocking collectives, local(): lax.all_to_all(back, ('gx', 'gy'), split_axis=0, concat_axis=0, tiled=True)  13.7 us
    ppermute x8, starting transfers between devices, pair(): return (lax.ppermute(up, axis, forward), lax.ppermute(down, axis, backward))  13.1 us
    unnamed x10, local copies, waits for them, and re-layouts  4.86 us
    pallas_call x1, Pallas kernels, local(): call(first, [field, pops] + faces)(arrived, populations_in)  4.32 us
    ppermute x8, waiting for transfers between devices, pair(): return (lax.ppermute(up, axis, forward), lax.ppermute(down, axis, backward))  3.99 us
    pallas_call x1, Pallas kernels, local(): call(last, [pops, ((devices, 8, LANES), F32)], [pltpu.VMEM(field[0], F32)...  3.26 us
    pallas_call x1, Pallas kernels, local(): call(middle_kernel, [field, pops] + faces, [pltpu.VMEM(pops[0], F32)])  2.73 us
  transfers between devices with their start and end apart: 8, of which 2 were waited for; matrix products, arithmetic and copies ran while one was open for 0% of the time, Pallas kernels for 6%

commit v1 on v0

--- a/solution.py
+++ b/solution.py
@@ -72,12 +72,24 @@
     return jnp.where(iota((slots, owned), 0) == slot, 1.0, 0.0).astype(BF)
 
 
-def pack_kernel(devices, cap, steps, tile_ref, cell_ref, frac_ref, force_ref, out_ref, slot_ref, rows):
+def fetch(pairs, sems):
+    copies = [pltpu.make_async_copy(source, target, sems.at[n]) for n, (source, target) in enumerate(pairs)]
+    for copy in copies:
+        copy.start()
+    return copies
+
+
+def pack_kernel(
+    devices, cap, steps, tile_in, cell_in, frac_in, force_in, out_ref, slot_ref, rows, tile_ref, cell_ref, frac_ref, force_ref, sems
+):
+    copies = fetch([(tile_in, tile_ref), (cell_in, cell_ref), (frac_in, frac_ref), (force_in, force_ref)], sems)
     owned = cell_ref.shape[2]
     slots = devices * cap
     lines = owned // LANES
     earlier = jnp.where(iota((owned, owned), 0) < iota((owned, owned), 1), 1.0, 0.0).astype(BF)
     octets = []
+    for copy in copies:
+        copy.wait()
     for step in range(steps):
         tiles = jnp.concatenate(
             [tile_ref[step * lines + r : step * lines + r + 1, :] for r in range(lines)], axis=1
@@ -127,14 +139,29 @@
 
 
 def unpack_kernel(cap, steps, recv_ref, slot_ref, out_ref):
-    rows = gather_octet(recv_ref, cap, 0)
-    slots = rows.shape[1]
-    parts = jnp.concatenate(split3(jnp.concatenate([rows, rows], axis=0)), axis=0)
+    devices = recv_ref.shape[0]
+    per = LANES // cap
+    group = iota((steps, LANES), 1) // cap
+    comps = []
+    for number in range(3):
+        pieces = []
+        for line in range(devices // per):
+            total = jnp.zeros((steps, LANES), F32)
+            for place in range(per):
+                piece = recv_ref[line * per + place]
+                shift = (place - number) * cap % LANES
+                if shift:
+                    piece = pltpu.roll(piece, shift, 1)
+                total = jnp.where(group == place, piece, total)
+            pieces.append(total)
+        comps.append(jnp.concatenate(pieces, axis=1))
+    slots = devices * cap
     for step in range(steps):
-        found = nn(parts, slot_table(slot_ref[step : step + 1, :], slots))
+        rows = jnp.concatenate([comp[step : step + 1] for comp in comps] + [jnp.zeros((13, slots), F32)], axis=0)
+        found = nn(jnp.concatenate(split3(rows), axis=0), slot_table(slot_ref[step : step + 1, :], slots))
         found = found[0:8] + found[16:24] + found[32:40]
         for number in range(3):
-            out_ref[number, step : step + 1, :] = found[step * 3 + number : step * 3 + number + 1]
+            out_ref[number, step : step + 1, :] = found[number : number + 1]
 
 
 def line_weights(cell, frac, extent):
@@ -350,10 +377,13 @@
     spread(first, second, planes, width_x, force_ref.shape[1], force_ref)
 
 
-def first_kernel(cap, recv_ref, f_ref, force_ref, post_ref, x_up, x_down, y_up, y_down):
+def first_kernel(cap, recv_ref, f_in, force_ref, post_ref, x_up, x_down, y_up, y_down, f_ref, sems):
+    copies = fetch([(f_in, f_ref)], sems)
     planes, width_x, width_y = f_ref.shape[1], f_ref.shape[2], f_ref.shape[3]
     spread_kernel(cap, 0, planes, width_x, recv_ref, force_ref)
     size = planes * width_x
+    for copy in copies:
+        copy.wait()
 
     def body(z, row, flat, lanes):
         f = [f_ref[member, z, row, lanes] for member in range(19)]
@@ -396,6 +426,22 @@
         out_ref[number : number + 1, :] = row
 
 
+def send_back(cap, rows, out_ref):
+    devices, steps = out_ref.shape[0], out_ref.shape[1]
+    per = LANES // cap
+    group = iota((steps, LANES), 1) // cap
+    for device in range(devices):
+        line, place = device // per, device % per
+        total = jnp.zeros((steps, LANES), F32)
+        for number in range(3):
+            piece = rows[number * steps : (number + 1) * steps, line * LANES : (line + 1) * LANES]
+            shift = (number - place) * cap % LANES
+            if shift:
+                piece = pltpu.roll(piece, shift, 1)
+            total = jnp.where(group == number, piece, total)
+        out_ref[device] = total
+
+
 def last_kernel(
     cap, step, post_in, x_low, x_high, y_low, y_high, force_ref, recv_ref, sampled_ref, f_ref, out_ref, probe_ref, rows
 ):
@@ -413,24 +459,22 @@
 
     blocks(planes, width_x, width_y, body)
     first = gather_octet(recv_ref, cap, 2 * step)
-    rows[...] = sampled_ref[...]
+    steps = out_ref.shape[1]
     for number, row in enumerate(sample(first, planes, width_x, width_y, probe_ref)):
-        rows[3 * step + number : 3 * step + number + 1, :] = row
-    per = LANES // cap
-    for device in range(out_ref.shape[0]):
-        line, place = device // per, device % per
-        piece = rows[:, line * LANES : (line + 1) * LANES]
-        if place:
-            piece = pltpu.roll(piece, LANES - place * cap, 1)
-        out_ref[device] = piece
-
-
-def call(kernel, outs, scratch=(), flops=0, moved=0, limit=40):
+        for other in range(step):
+            rows[steps * number + other : steps * number + other + 1, :] = sampled_ref[number : number + 1, :]
+        rows[steps * number + step : steps * number + step + 1, :] = row
+    send_back(cap, rows, out_ref)
+
+
+def call(kernel, outs, scratch=(), flops=0, moved=0, limit=40, fetched=(False,)):
     shapes = [jax.ShapeDtypeStruct(shape, kind) for shape, kind in outs]
+    specs = [pl.BlockSpec(memory_space=pltpu.HBM if own else pltpu.VMEM) for own in fetched]
     return pl.pallas_call(
         kernel,
         out_shape=shapes,
         scratch_shapes=list(scratch),
+        **({"in_specs": specs} if any(fetched) else {}),
         cost_estimate=pl.CostEstimate(flops=flops, bytes_accessed=moved, transcendentals=0),
         compiler_params=pltpu.CompilerParams(vmem_limit_bytes=limit * 1024 * 1024),
     )
@@ -470,7 +514,16 @@
     outgoing, slot = call(
         pack,
         [((devices, 8, LANES), F32), ((steps, owned), jnp.int32)],
-        [pltpu.VMEM((16, owned), F32)],
+        [
+            pltpu.VMEM((16, owned), F32),
+            pltpu.VMEM((steps * owned // LANES, LANES), jnp.int32),
+            pltpu.VMEM((3, steps, owned), jnp.int32),
+            pltpu.VMEM((3, steps, owned), F32),
+            pltpu.VMEM((3, steps, owned), F32),
+            pltpu.SemaphoreType.DMA((4,)),
+        ],
+        fetched=(True,) * 4,
+        limit=63,
     )(
         marker_tile.reshape(steps * owned // LANES, LANES),
         by_comp(marker_cell),
@@ -487,7 +540,12 @@
     def first(*refs):
         first_kernel(cap, *refs)
 
-    force_0, post, *sent = call(first, [field, pops] + faces)(arrived, populations_in)
+    force_0, post, *sent = call(
+        first,
+        [field, pops] + faces,
+        [pltpu.VMEM(pops[0], F32), pltpu.SemaphoreType.DMA((1,))],
+        fetched=(False, True),
+    )(arrived, populations_in)
     halos = exchange(sent, planes, width_x)
 
     def second_spread(*refs):
@@ -510,7 +568,7 @@
 
     fields, back = call(
         last,
-        [pops, ((devices, 8, LANES), F32)],
+        [pops, ((devices, steps, LANES), F32)],
         [pltpu.VMEM(field[0], F32), pltpu.VMEM((8, slots), F32)],
     )(post, *halos, force_1, arrived, sampled)
     returned = lax.all_to_all(back, ("gx", "gy"), split_axis=0, concat_axis=0, tiled=True)

time: 68.9 us -> 67.2 us (0.975)
  local copies, waits for them, and re-layouts: 4.86 us -> 2.06 us
  Pallas kernels: 16.8 us -> 18.7 us
  blocking collectives: 29 us -> 28.3 us
    unnamed x10 -> x4, local copies, waits for them, and re-layouts: 4.86 us -> 2.06 us
    pallas_call x1, Pallas kernels: 1.18 us -> 2.62 us  [local(): call(pack, [((devices, 8, LANES), F32), ((steps, owned), jnp.int32)], [pl...]
    all_to_all x1, blocking collectives: 13.7 us -> 12.7 us  [local(): lax.all_to_all(back, ('gx', 'gy'), split_axis=0, concat_axis=0, tiled=True)]
where the time goes in v1:
time: 67.2 us; the launch traced here: 66.8 us
  blocking collectives  28.3 us (42%)
  Pallas kernels  18.7 us (28%)
  starting transfers between devices  13.1 us (19%)
  waiting for transfers between devices  3.98 us (6%)
  local copies, waits for them, and re-layouts  2.06 us (3%)
  between operations  0.74 us (1%)
    all_to_all x1, blocking collectives, local(): lax.all_to_all(outgoing, ('gx', 'gy'), split_axis=0, concat_axis=0, tiled...  15.5 us
    ppermute x8, starting transfers between devices, pair(): return (lax.ppermute(up, axis, forward), lax.ppermute(down, axis, backward))  13.1 us
    all_to_all x1, blocking collectives, local(): lax.all_to_all(back, ('gx', 'gy'), split_axis=0, concat_axis=0, tiled=True)  12.7 us
    pallas_call x1, Pallas kernels, local(): call(first, [field, pops] + faces, [pltpu.VMEM(pops[0], F32), pltpu.Semap...  4.63 us
    ppermute x8, waiting for transfers between devices, pair(): return (lax.ppermute(up, axis, forward), lax.ppermute(down, axis, backward))  3.98 us
    pallas_call x1, Pallas kernels, local(): call(last, [pops, ((devices, steps, LANES), F32)], [pltpu.VMEM(field[0],...  3.27 us
    pallas_call x1, Pallas kernels, local(): call(middle_kernel, [field, pops] + faces, [pltpu.VMEM(pops[0], F32)])  2.73 us
    pallas_call x1, Pallas kernels, local(): call(pack, [((devices, 8, LANES), F32), ((steps, owned), jnp.int32)], [pl...  2.62 us
  transfers between devices with their start and end apart: 8, of which 2 were waited for; matrix products, arithmetic and copies ran while one was open for 0% of the time, Pallas kernels for 6%

profile of v1, /device:TPU:0, one launch (start us, length us, event | category | flops | bytes accessed | tf_op | source)
XLA Modules:
  0.0 66.8 jit_solution(16153373068287781249)
XLA Ops:
  0.6 2.6 %shard_map.68 = (f32[32,8,128]{2,1,0:T(8,128)}, s32[2,512]{1,0:T(2,128)}) custom-call(s32[8,128]{1,0:T(8,128)} %bitcast.9, s32[3,2,512]{2,1,0:T(2,128)} %bitcast.5, f32[3,2,512]{2,1,0:T(2,128)} %bitcast.6, f32[3,2,512]{2,1,0:T(2,128)} %bitcast.7), custom_call_target="tpu_custom_call" | custom-call | tf_op jit(solution)/shard_map/pallas_call | solution.py:514
  3.3 15.5 %all_to_all.10.refs_0_.refs_6_ = f32[32,8,128]{2,1,0:T(8,128)S(1)} all-to-all(f32[32,8,128]{2,1,0:T(8,128)} %get-tuple-element.22), channel_id=1, replica_groups=mesh['gx'=4,'gy'=8] {'gx','gy'}, dimensions={0} | all-to-all | bytes 262144 | tf_op jit(solution)/shard_map/all_to_all | solution.py:533
  18.8 0.0 copy-start
  18.8 2.1 %copy-done = f32[19,4,32,384]{3,2,1,0:T(8,128)S(1)} copy-done((f32[19,4,32,384]{3,2,1,0:T(8,128)S(1)}, f32[19,4,32,384]{3,2,1,0:T(8,128)}, u32[]{:S(2)}) %copy-start) | copy-done | bytes 3735576
  20.9 4.6 %shard_map.69 = (f32[384,384]{1,0:T(8,128)S(1)}, f32[19,4,32,384]{3,2,1,0:T(8,128)S(1)}, f32[24,384]{1,0:T(8,128)S(1)}, f32[24,384]{1,0:T(8,128)S(1)}, f32[8,128]{1,0:T(8,128)S(1)}, /*index=5*/f32[8,128]{1,0:T(8,128)S(1)}) custom-call(f32[32,8,128]{2,1,0:T(8,128)S(1)} %all_to_all.10.refs_0_.refs_6_, f32[19,4,32,384]{3,2,1,0:T(8,128)S(1)} %copy-done), custom_call_target="tpu_custom_call" | custom-call | tf_op jit(solution)/shard_map/pallas_call | solution.py:543
  25.5 0.7 %collective-permute-start = (f32[24,384]{1,0:T(8,128)S(1)}, f32[24,384]{1,0:T(8,128)S(1)}, u32[]{:S(2)}, u32[]{:S(2)}) collective-permute-start(f32[24,384]{1,0:T(8,128)S(1)} %get-tuple-element.24), channel_id=1, source_target_pairs={{0,8},{8,16},{16,24},{24,0},{1,9},{9,17},{17,25},{25,1},{2,10},{10... | collective-permute-start | bytes 110600 | tf_op jit(solution)/shard_map/ppermute | solution.py:487
  26.2 3.2 %collective-permute-start.1 = (f32[24,384]{1,0:T(8,128)S(1)}, f32[24,384]{1,0:T(8,128)S(1)}, u32[]{:S(2)}, u32[]{:S(2)}) collective-permute-start(f32[24,384]{1,0:T(8,128)S(1)} %get-tuple-element.25), channel_id=1, source_target_pairs={{8,0},{16,8},{24,16},{0,24},{9,1},{17,9},{25,17},{1,25},{10,2},{18... | collective-permute-start | bytes 110600 | tf_op jit(solution)/shard_map/ppermute | solution.py:487
  29.4 2.0 %collective-permute-done.refs_2_.x_low = f32[24,384]{1,0:T(8,128)S(1)} collective-permute-done((f32[24,384]{1,0:T(8,128)S(1)}, f32[24,384]{1,0:T(8,128)S(1)}, u32[]{:S(2)}, u32[]{:S(2)}) %collective-permute-start) | collective-permute-done | bytes 36896 | tf_op jit(solution)/shard_map/ppermute | solution.py:487
  31.3 0.0 collective-permute-done.1.refs_3_.x_high
  31.3 0.1 shard_map.70
  31.4 0.1 collective-permute-start.2
  31.5 2.6 %collective-permute-start.3 = (f32[8,128]{1,0:T(8,128)S(1)}, f32[8,128]{1,0:T(8,128)S(1)}, u32[]{:S(2)}, u32[]{:S(2)}) collective-permute-start(f32[8,128]{1,0:T(8,128)S(1)} %get-tuple-element.29), channel_id=1, source_target_pairs={{1,0},{2,1},{3,2},{4,3},{5,4},{6,5},{7,6},{0,7},{9,8},{10,9},{11,1... | collective-permute-start | bytes 12296 | tf_op jit(solution)/shard_map/ppermute | solution.py:487
  34.1 2.2 %shard_map.71.next_ref.refs_5_ = f32[384,384]{1,0:T(8,128)S(1)} custom-call(f32[32,8,128]{2,1,0:T(8,128)S(1)} %all_to_all.10.refs_0_.refs_6_), custom_call_target="tpu_custom_call" | custom-call | flops 1000000000 | bytes 1000000 | tf_op jit(solution)/shard_map/pallas_call | solution.py:554
  36.4 0.0 collective-permute-done.2.y_low
  36.4 0.0 collective-permute-done.3.y_high
  36.4 2.7 %shard_map.72 = (f32[384,384]{1,0:T(8,128)S(1)}, f32[19,4,32,384]{3,2,1,0:T(8,128)S(1)}, f32[24,384]{1,0:T(8,128)S(1)}, f32[24,384]{1,0:T(8,128)S(1)}, f32[8,128]{1,0:T(8,128)S(1)}, /*index=5*/f32[8,128]{1,0:T(8,128)S(1)}) custom-call(f32[19,4,32,384]{3,2,1,0:T(8,128)S(1)} %get-tuple-element.23.post_in, f32[24,384]{1,0:T(8,128)S(1)} %collective-permute-done.refs_2_.x_low, ...), custom_call_target="tpu_custom_call" | custom-call | tf_op jit(solution)/shard_map/pallas_call | solution.py:556
  39.1 0.0 collective-permute-start.4
  39.2 3.8 %collective-permute-start.5 = (f32[24,384]{1,0:T(8,128)S(1)}, f32[24,384]{1,0:T(8,128)S(1)}, u32[]{:S(2)}, u32[]{:S(2)}) collective-permute-start(f32[24,384]{1,0:T(8,128)S(1)} %get-tuple-element.33), channel_id=1, source_target_pairs={{8,0},{16,8},{24,16},{0,24},{9,1},{17,9},{25,17},{1,25},{10,2},{18... | collective-permute-start | bytes 110600 | tf_op jit(solution)/shard_map/ppermute | solution.py:487
  43.0 2.0 %collective-permute-done.4.refs_2_.refs_1_ = f32[24,384]{1,0:T(8,128)S(1)} collective-permute-done((f32[24,384]{1,0:T(8,128)S(1)}, f32[24,384]{1,0:T(8,128)S(1)}, u32[]{:S(2)}, u32[]{:S(2)}) %collective-permute-start.4) | collective-permute-done | bytes 36896 | tf_op jit(solution)/shard_map/ppermute | solution.py:487
  45.0 0.0 collective-permute-done.5.refs_3_.refs_2_
  45.0 0.1 shard_map.73
  45.1 0.1 collective-permute-start.6
  45.2 2.6 %collective-permute-start.7 = (f32[8,128]{1,0:T(8,128)S(1)}, f32[8,128]{1,0:T(8,128)S(1)}, u32[]{:S(2)}, u32[]{:S(2)}) collective-permute-start(f32[8,128]{1,0:T(8,128)S(1)} %get-tuple-element.37), channel_id=1, source_target_pairs={{1,0},{2,1},{3,2},{4,3},{5,4},{6,5},{7,6},{0,7},{9,8},{10,9},{11,1... | collective-permute-start | bytes 12296 | tf_op jit(solution)/shard_map/ppermute | solution.py:487
  47.8 0.0 copy-start.1
  47.8 1.8 %shard_map.74.refs_7_ = f32[8,1024]{1,0:T(8,128)S(1)} custom-call(f32[32,8,128]{2,1,0:T(8,128)S(1)} %all_to_all.10.refs_0_.refs_6_, f32[384,384]{1,0:T(8,128)S(1)} %get-tuple-element.38.refs_1_), custom_call_target="tpu_custom_call" | custom-call | flops 1000000000 | bytes 1000000 | tf_op jit(solution)/shard_map/pallas_call | solution.py:564
  49.6 0.0 collective-permute-done.6.refs_3_
  49.6 0.0 collective-permute-done.7.refs_4_
  49.6 3.3 %shard_map.75 = (f32[19,4,32,384]{3,2,1,0:T(8,128)}, f32[32,2,128]{2,1,0:T(2,128)S(1)}) custom-call(f32[19,4,32,384]{3,2,1,0:T(8,128)S(1)} %get-tuple-element.31.refs_0_, f32[24,384]{1,0:T(8,128)S(1)} %collective-permute-done.4.refs_2_.refs_1_, f32[24,384]{1,0:T(8,128)S(1)} %collective-permute-done.5.refs_3_.refs_2_, ...), custom_call_target="tpu_custom_call" | custom-call | tf_op jit(solution)/shard_map/pallas_call | solution.py:569
  52.9 12.7 %all_to_all.11.refs_0_ = f32[32,2,128]{2,1,0:T(2,128)S(1)} all-to-all(f32[32,2,128]{2,1,0:T(2,128)S(1)} %get-tuple-element.40), channel_id=1, replica_groups=mesh['gx'=4,'gy'=8] {'gx','gy'}, dimensions={0} | all-to-all | bytes 65536 | tf_op jit(solution)/shard_map/all_to_all | solution.py:574
  65.6 0.0 copy-done.1
  65.6 1.2 %shard_map.76 = f32[3,2,512]{2,1,0:T(2,128)} custom-call(f32[32,2,128]{2,1,0:T(2,128)S(1)} %all_to_all.11.refs_0_, s32[2,512]{1,0:T(2,128)S(1)} %copy-done.1), custom_call_target="tpu_custom_call" | custom-call | tf_op jit(solution)/shard_map/pallas_call | solution.py:579
Async XLA Ops:
  18.8 2.1 %copy-start = (f32[19,4,32,384]{3,2,1,0:T(8,128)S(1)}, f32[19,4,32,384]{3,2,1,0:T(8,128)}, u32[]{:S(2)}) copy-start(f32[19,4,32,384]{3,2,1,0:T(8,128)} %refs_1_.1) | copy-start | bytes 11206660
  25.5 5.8 %collective-permute-start = (f32[24,384]{1,0:T(8,128)S(1)}, f32[24,384]{1,0:T(8,128)S(1)}, u32[]{:S(2)}, u32[]{:S(2)}) collective-permute-start(f32[24,384]{1,0:T(8,128)S(1)} %get-tuple-element.24), channel_id=1, source_target_pairs={{0,8},{8,16},{16,24},{24,0},{1,9},{9,17},{17,25},{25,1},{2,10},{10... | collective-permute-start | bytes 110600 | tf_op jit(solution)/shard_map/ppermute | solution.py:487
  26.2 5.1 %collective-permute-start.1 = (f32[24,384]{1,0:T(8,128)S(1)}, f32[24,384]{1,0:T(8,128)S(1)}, u32[]{:S(2)}, u32[]{:S(2)}) collective-permute-start(f32[24,384]{1,0:T(8,128)S(1)} %get-tuple-element.25), channel_id=1, source_target_pairs={{8,0},{16,8},{24,16},{0,24},{9,1},{17,9},{25,17},{1,25},{10,2},{18... | collective-permute-start | bytes 110600 | tf_op jit(solution)/shard_map/ppermute | solution.py:487
  31.4 5.0 %collective-permute-start.2 = (f32[8,128]{1,0:T(8,128)S(1)}, f32[8,128]{1,0:T(8,128)S(1)}, u32[]{:S(2)}, u32[]{:S(2)}) collective-permute-start(f32[8,128]{1,0:T(8,128)S(1)} %get-tuple-element.28), channel_id=1, source_target_pairs={{0,1},{1,2},{2,3},{3,4},{4,5},{5,6},{6,7},{7,0},{8,9},{9,10},{10,1... | collective-permute-start | bytes 12296 | tf_op jit(solution)/shard_map/ppermute | solution.py:487
  31.5 4.9 %collective-permute-start.3 = (f32[8,128]{1,0:T(8,128)S(1)}, f32[8,128]{1,0:T(8,128)S(1)}, u32[]{:S(2)}, u32[]{:S(2)}) collective-permute-start(f32[8,128]{1,0:T(8,128)S(1)} %get-tuple-element.29), channel_id=1, source_target_pairs={{1,0},{2,1},{3,2},{4,3},{5,4},{6,5},{7,6},{0,7},{9,8},{10,9},{11,1... | collective-permute-start | bytes 12296 | tf_op jit(solution)/shard_map/ppermute | solution.py:487
  39.1 5.9 %collective-permute-start.4 = (f32[24,384]{1,0:T(8,128)S(1)}, f32[24,384]{1,0:T(8,128)S(1)}, u32[]{:S(2)}, u32[]{:S(2)}) collective-permute-start(f32[24,384]{1,0:T(8,128)S(1)} %get-tuple-element.32), channel_id=1, source_target_pairs={{0,8},{8,16},{16,24},{24,0},{1,9},{9,17},{17,25},{25,1},{2,10},{10... | collective-permute-start | bytes 110600 | tf_op jit(solution)/shard_map/ppermute | solution.py:487
  39.2 5.8 %collective-permute-start.5 = (f32[24,384]{1,0:T(8,128)S(1)}, f32[24,384]{1,0:T(8,128)S(1)}, u32[]{:S(2)}, u32[]{:S(2)}) collective-permute-start(f32[24,384]{1,0:T(8,128)S(1)} %get-tuple-element.33), channel_id=1, source_target_pairs={{8,0},{16,8},{24,16},{0,24},{9,1},{17,9},{25,17},{1,25},{10,2},{18... | collective-permute-start | bytes 110600 | tf_op jit(solution)/shard_map/ppermute | solution.py:487
  45.1 4.5 %collective-permute-start.6 = (f32[8,128]{1,0:T(8,128)S(1)}, f32[8,128]{1,0:T(8,128)S(1)}, u32[]{:S(2)}, u32[]{:S(2)}) collective-permute-start(f32[8,128]{1,0:T(8,128)S(1)} %get-tuple-element.36), channel_id=1, source_target_pairs={{0,1},{1,2},{2,3},{3,4},{4,5},{5,6},{6,7},{7,0},{8,9},{9,10},{10,1... | collective-permute-start | bytes 12296 | tf_op jit(solution)/shard_map/ppermute | solution.py:487
  45.2 4.4 %collective-permute-start.7 = (f32[8,128]{1,0:T(8,128)S(1)}, f32[8,128]{1,0:T(8,128)S(1)}, u32[]{:S(2)}, u32[]{:S(2)}) collective-permute-start(f32[8,128]{1,0:T(8,128)S(1)} %get-tuple-element.37), channel_id=1, source_target_pairs={{1,0},{2,1},{3,2},{4,3},{5,4},{6,5},{7,6},{0,7},{9,8},{10,9},{11,1... | collective-permute-start | bytes 12296 | tf_op jit(solution)/shard_map/ppermute | solution.py:487
  47.8 17.8 %copy-start.1 = (s32[2,512]{1,0:T(2,128)S(1)}, s32[2,512]{1,0:T(2,128)}, u32[]{:S(2)}) copy-start(s32[2,512]{1,0:T(2,128)} %get-tuple-element.41.refs_1_) | copy-start | bytes 12292

commit v2 on v1

v2 whole, which is shorter than its diff:
```python
import jax
import jax.numpy as jnp
from jax import lax
from jax.experimental import pallas as pl
from jax.experimental.pallas import tpu as pltpu
from jax.sharding import PartitionSpec as P

LATTICE = [
    (0, 0, 0),
    (1, 0, 0),
    (-1, 0, 0),
    (0, 1, 0),
    (0, -1, 0),
    (0, 0, 1),
    (0, 0, -1),
    (1, 1, 0),
    (-1, -1, 0),
    (1, -1, 0),
    (-1, 1, 0),
    (1, 0, 1),
    (-1, 0, -1),
    (1, 0, -1),
    (-1, 0, 1),
    (0, 1, 1),
    (0, -1, -1),
    (0, 1, -1),
    (0, -1, 1),
]
WEIGHTS = [1.0 / 3.0] + [1.0 / 18.0] * 6 + [1.0 / 36.0] * 12
relax_time = 0.8
OMEGA = 1.0 / relax_time
SOURCE = 1.0 - 0.5 / relax_time
LANES = 128

BF = jnp.bfloat16
F32 = jnp.float32


def split2(x):
    high = x.astype(BF)
    low = (x - high.astype(F32)).astype(BF)
    return high, low


def split3(x):
    high = x.astype(BF)
    rest = x - high.astype(F32)
    middle = rest.astype(BF)
    low = (rest - middle.astype(F32)).astype(BF)
    return high, middle, low


def nt(a, b):
    return lax.dot_general(a, b, (((1,), (1,)), ((), ())), preferred_element_type=F32)


def nn(a, b):
    return lax.dot_general(a, b, (((1,), (0,)), ((), ())), preferred_element_type=F32)


def iota(shape, dim):
    return lax.broadcasted_iota(jnp.int32, shape, dim)


RING = 8
SIDE = LANES


def slot_table(slot, slots):
    owned = slot.shape[1]
    return jnp.where(iota((slots, owned), 0) == slot, 1.0, 0.0).astype(BF)


def fetch(pairs, sems):
    copies = [pltpu.make_async_copy(source, target, sems.at[n]) for n, (source, target) in enumerate(pairs)]
    for copy in copies:
        copy.start()
    return copies


def ghosts(step, steps, count_gx, count_gy, width_x, width_y, tiles, cell_x, cell_y):
    reach = steps - step
    along = []
    tiles = tiles.astype(F32)
    gx = jnp.floor((tiles + 0.5) * (1.0 / count_gy))
    for cell, width, place, count in (
        (cell_x, width_x, gx, count_gx),
        (cell_y, width_y, tiles - gx * count_gy, count_gy),
    ):
        above, below = cell >= width - 1 - reach, cell <= reach - 1
        place_up = jnp.where(place == count - 1, 0.0, place + 1.0)
        place_down = jnp.where(place == 0, count - 1.0, place - 1.0)
        along.append(
            (
                jnp.where(above | below, 1.0, 0.0),
                place,
                jnp.where(above, place_up, place_down),
                cell,
                jnp.where(above, cell - width, cell + width),
            )
        )
    (near_x, here_x, there_x, in_x, out_x), (near_y, here_y, there_y, in_y, out_y) = along
    return [
        (jnp.where(near_x > 0, there_x * count_gy + here_y, -1.0), out_x, in_y),
        (jnp.where(near_y > 0, here_x * count_gy + there_y, -1.0), in_x, out_y),
        (jnp.where(near_x * near_y > 0, there_x * count_gy + there_y, -1.0), out_x, out_y),
    ]


def pack(grid, steps, cap, step_rows, out_ref, slot_ref, rows, turn=None):
    count_gx, count_gy, width_x, width_y = grid
    devices, half = count_gx * count_gy, cap // 2
    owned = rows.shape[1]
    slots = devices * cap
    earlier = jnp.where(iota((owned, owned), 0) < iota((owned, owned), 1), 1.0, 0.0).astype(BF)
    column = iota((devices, owned), 0).astype(F32)
    octets, extras, most = [], [], []
    for step in range(steps):
        tiles, values = step_rows(step)
        beside = ghosts(step, steps, *grid, tiles, values[0], values[1])
        member = [jnp.where(column == tile, 1.0, 0.0) for tile in [tiles.astype(F32)] + [b[0] for b in beside]]
        before = nn(jnp.concatenate(member, axis=0).astype(BF), earlier)
        before = [before[n * devices : (n + 1) * devices] for n in range(4)]
        if turn is None:
            rank = jnp.sum(before[0] * member[0], axis=0, keepdims=True)
            slot = tiles * cap + rank.astype(jnp.int32)
            slot_ref[step : step + 1, :] = slot
            rows[...] = jnp.zeros_like(rows)
            for number, value in enumerate(values):
                rows[number : number + 1, :] = value
            packed = nt(jnp.concatenate(split3(rows[...]), axis=0), slot_table(slot, slots))
            packed = packed[0:16] + packed[16:32] + packed[32:48]
            octets.append((packed[0:8], packed[8:16]))
        taken = jnp.zeros((devices, 1), F32)
        extra = jnp.zeros((48, devices * half), F32)
        for number, (tile, cell_x, cell_y) in enumerate(beside):
            rank = jnp.sum((before[number + 1] + taken) * member[number + 1], axis=0, keepdims=True)
            taken = taken + jnp.sum(member[number + 1], axis=1, keepdims=True)
            if turn is not None:
                rank = rank - turn * half
            fits = (tile >= 0) & (rank >= 0) & (rank < half)
            slot = jnp.where(fits, tile * half + rank, -1.0).astype(jnp.int32)
            rows[...] = jnp.zeros_like(rows)
            for place, value in zip((1, 2, 3, 4, 5, 6, 7, 9, 10), [cell_x, cell_y] + values[2:]):
                rows[place : place + 1, :] = value
            extra = extra + nt(jnp.concatenate(split3(rows[...]), axis=0), slot_table(slot, devices * half))
        extra = extra[0:16] + extra[16:32] + extra[32:48]
        extras.append((extra[0:8], extra[8:16]))
        most.append(jnp.max(taken, axis=0, keepdims=True))
    lane, row = iota((8, LANES), 1), iota((8, LANES), 0)

    def placed(octet, device, width, offset):
        line, place = device * width // LANES, device * width % LANES
        piece = octet[:, line * LANES : (line + 1) * LANES]
        shift = (offset - place) % LANES
        if shift:
            piece = pltpu.roll(piece, shift, 1)
        return jnp.where((lane >= offset) & (lane < offset + width), piece, 0.0)

    heading = jnp.zeros((8, LANES), F32)
    for step in range(steps):
        start = (2 * step + 1) * cap + half
        heading = jnp.where((row == 3) & (lane >= start) & (lane < start + half), most[step], heading)
    for device in range(devices):
        block = heading
        for step in range(steps):
            start = 2 * step * cap
            if turn is None:
                block = block + placed(octets[step][0], device, cap, start)
                block = block + placed(octets[step][1], device, cap, start + cap)
            block = block + placed(extras[step][0], device, half, start + cap)
            block = block + placed(extras[step][1], device, half, start + cap + half)
        out_ref[device] = block


def marker_rows(tile_ref, cell_ref, frac_ref, force_ref):
    lines = cell_ref.shape[2] // LANES

    def step_rows(step):
        tiles = jnp.concatenate(
            [tile_ref[step * lines + r : step * lines + r + 1, :] for r in range(lines)], axis=1
        )
        values = [cell_ref[n, step : step + 1, :].astype(F32) for n in range(3)]
        values += [frac_ref[n, step : step + 1, :] for n in range(3)]
        values += [force_ref[n, step : step + 1, :] for n in range(3)]
        return tiles, values

    return step_rows


def pack_kernel(
    grid, steps, cap, tile_in, cell_in, frac_in, force_in, f_in, out_ref, slot_ref, x_up, x_down,
    rows, tile_ref, cell_ref, frac_ref, force_ref, near_ref, far_ref, sems,
):
    width_x = f_in.shape[2]
    copies = fetch(
        [
            (tile_in, tile_ref),
            (cell_in, cell_ref),
            (frac_in, frac_ref),
            (force_in, force_ref),
            (f_in.at[:, :, pl.ds(0, 8), :], near_ref),
            (f_in.at[:, :, pl.ds(width_x - 8, 8), :], far_ref),
        ],
        sems,
    )
    for copy in copies[:4]:
        copy.wait()
    pack(grid, steps, cap, marker_rows(tile_ref, cell_ref, frac_ref, force_ref), out_ref, slot_ref, rows)
    for copy in copies[4:]:
        copy.wait()
    planes = f_in.shape[1]
    for member in range(19):
        for z in range(planes):
            plane = member * planes + z
            x_up[2 * plane : 2 * plane + 2, :] = far_ref[member, z, 6:8, :]
            x_down[2 * plane : 2 * plane + 2, :] = near_ref[member, z, 0:2, :]


def turn_kernel(grid, steps, cap, turn_ref, tile_ref, cell_ref, frac_ref, force_ref, out_ref, rows):
    step_rows = marker_rows(tile_ref, cell_ref, frac_ref, force_ref)
    pack(grid, steps, cap, step_rows, out_ref, None, rows, turn_ref[0].astype(F32))


def gather(recv_ref, offset, width):
    devices = recv_ref.shape[0]
    per = LANES // width
    group = iota((8, LANES), 1) // width
    pieces = []
    for line in range(devices // per):
        total = jnp.zeros((8, LANES), F32)
        for place in range(per):
            piece = recv_ref[line * per + place]
            shift = (place * width - offset) % LANES
            if shift:
                piece = pltpu.roll(piece, shift, 1)
            total = jnp.where(group == place, piece, total)
        pieces.append(total)
    return jnp.concatenate(pieces, axis=1)


def unpack_kernel(cap, steps, recv_ref, slot_ref, out_ref):
    devices = recv_ref.shape[0]
    per = LANES // cap
    group = iota((steps, LANES), 1) // cap
    comps = []
    for number in range(3):
        pieces = []
        for line in range(devices // per):
            total = jnp.zeros((steps, LANES), F32)
            for place in range(per):
                piece = recv_ref[line * per + place]
                shift = (place - number) * cap % LANES
                if shift:
                    piece = pltpu.roll(piece, shift, 1)
                total = jnp.where(group == place, piece, total)
            pieces.append(total)
        comps.append(jnp.concatenate(pieces, axis=1))
    slots = devices * cap
    for step in range(steps):
        rows = jnp.concatenate([comp[step : step + 1] for comp in comps] + [jnp.zeros((13, slots), F32)], axis=0)
        found = nn(jnp.concatenate(split3(rows), axis=0), slot_table(slot_ref[step : step + 1, :], slots))
        found = found[0:8] + found[16:24] + found[32:40]
        for number in range(3):
            out_ref[number, step : step + 1, :] = found[number : number + 1]


def line_weights(cell, frac, extent):
    grid = iota((extent, cell.shape[1]), 0).astype(F32)
    return jnp.where(grid == cell, 1.0 - frac, jnp.where(grid == cell + 1.0, frac, 0.0))


def y_table(cell, frac, extent):
    grid = iota((extent, cell.shape[1]), 0).astype(F32)
    lower, upper = grid == cell, grid == cell + 1.0
    tables = []
    for low, high in zip(split2(1.0 - frac), split2(frac)):
        low, high = low.astype(F32), high.astype(F32)
        tables.append(jnp.where(lower, low, jnp.where(upper, high, 0.0)).astype(BF))
    return tables


def plane_table(rows, planes, width_x):
    kernel_x = line_weights(rows[0:1], rows[3:4], width_x)
    kernel_z = line_weights(rows[2:3], rows[5:6], 8)
    return [kernel_z[z : z + 1] * kernel_x for z in range(planes)]


def product(table, along_y):
    high, low = split2(table)
    return nt(high, along_y[0]) + nt(high, along_y[1]) + nt(low, along_y[0])


def spread_own(first, second, planes, width_x, width_y, force_ref):
    tall = width_x + RING
    table = jnp.concatenate(plane_table(first, planes, width_x), axis=0)
    along_y = y_table(first[1:2], first[4:5], width_y)
    for number, strength in enumerate((first[6:7], first[7:8], second[0:1])):
        found = product(table * strength, along_y)
        for z in range(planes):
            at = (number * planes + z) * tall
            force_ref[at : at + width_x, 0:width_y] = found[z * width_x : (z + 1) * width_x]


def spread_ghosts(first, second, planes, width_x, width_y, force_ref, add):
    tall, wide = width_x + RING, width_y + SIDE
    cell_x = jnp.where(first[1:2] < 0, first[1:2] + tall, first[1:2])
    cell_y = jnp.where(first[2:3] < 0, first[2:3] + wide, first[2:3])
    kernel_x = line_weights(cell_x, first[4:5], tall)
    kernel_z = line_weights(first[3:4], first[6:7], 8)
    along_y = y_table(cell_y, first[5:6], wide)
    side_y = [table[width_y:] for table in along_y]
    ring = [kernel_z[z : z + 1] * kernel_x[width_x:] for z in range(planes)]
    side = [kernel_z[z : z + 1] * kernel_x[0:width_x] for z in range(planes)]
    ring, side = jnp.concatenate(ring, axis=0), jnp.concatenate(side, axis=0)
    for number, strength in enumerate((first[7:8], second[1:2], second[2:3])):
        found_ring = product(ring * strength, along_y)
        found_side = product(side * strength, side_y)
        for z in range(planes):
            at = (number * planes + z) * tall
            part_ring = found_ring[z * RING : (z + 1) * RING]
            part_side = found_side[z * width_x : (z + 1) * width_x]
            if add:
                part_ring = part_ring + force_ref[at + width_x : at + tall, :]
                part_side = part_side + force_ref[at : at + width_x, width_y:]
            force_ref[at + width_x : at + tall, :] = part_ring
            force_ref[at : at + width_x, width_y:] = part_side


def spread_kernel(cap, steps, planes, width_x, width_y, recv_ref, *outs):
    forces, own_ref, most_ref = outs[:steps], outs[steps], outs[steps + 1]
    half = cap // 2
    most = jnp.zeros((1, 1), F32)
    for step in range(steps):
        start = 2 * step * cap
        first = gather(recv_ref, start, cap)
        own_ref[8 * step : 8 * step + 8, :] = first
        second = gather(recv_ref, start + cap, cap)
        spread_own(first, second, planes, width_x, width_y, forces[step])
        first = gather(recv_ref, start + cap, half)
        second = gather(recv_ref, start + cap + half, half)
        spread_ghosts(first, second, planes, width_x, width_y, forces[step], False)
        most = jnp.maximum(most, jnp.max(second[3:4], axis=1, keepdims=True))
    most_ref[...] = jnp.broadcast_to(most, most_ref.shape)


def more_kernel(cap, steps, planes, width_x, width_y, recv_ref, *refs):
    half = cap // 2
    for step in range(steps):
        start = (2 * step + 1) * cap
        force_ref = refs[steps + step]
        force_ref[...] = refs[step][...]
        first, second = gather(recv_ref, start, half), gather(recv_ref, start + half, half)
        spread_ghosts(first, second, planes, width_x, width_y, force_ref, True)


def sample(first, planes, width_x, width_y, probe_ref):
    table = jnp.concatenate(plane_table(first, planes, width_x), axis=0)
    along_y = y_table(first[1:2], first[4:5], width_y)
    size = planes * width_x
    rows = []
    for number in range(3):
        high, low = split2(probe_ref[number * size : (number + 1) * size, :])
        found = nn(high, along_y[0]) + nn(high, along_y[1]) + nn(low, along_y[0])
        rows.append(jnp.sum(found * table, axis=0, keepdims=True))
    return rows


def moments(f):
    density = f[0]
    diff = {}
    for member in range(1, 19, 2):
        density = density + (f[member] + f[member + 1])
        diff[member] = f[member] - f[member + 1]
    momenta = []
    for number in range(3):
        total = None
        for member in range(1, 19, 2):
            sign = LATTICE[member][number]
            if sign == 0:
                continue
            if total is None:
                total = diff[member] if sign == 1 else -diff[member]
            else:
                total = total + diff[member] if sign == 1 else total - diff[member]
        momenta.append(total)
    return density, momenta


def dot_c(vector, comps):
    total = None
    for number in range(3):
        if vector[number] == 0:
            continue
        if total is None:
            total = comps[number] if vector[number] == 1 else -comps[number]
        else:
            total = total + comps[number] if vector[number] == 1 else total - comps[number]
    return total


def collide(f, density, momenta, force):
    inverse = 1.0 / density
    speed = [(momenta[n] + 0.5 * force[n]) * inverse for n in range(3)]
    scaled = OMEGA * density
    speed_sq = speed[0] * speed[0] + speed[1] * speed[1] + speed[2] * speed[2]
    along = speed[0] * force[0] + speed[1] * force[1] + speed[2] * force[2]
    base = scaled * (1.0 - 1.5 * speed_sq) - (3.0 * SOURCE) * along
    flow = [scaled * speed[n] for n in range(3)]
    pull = [(3.0 * SOURCE) * force[n] for n in range(3)]
    linear = [3.0 * flow[n] + pull[n] for n in range(3)]
    square = [4.5 * flow[n] + 3.0 * pull[n] for n in range(3)]
    posts = [(1.0 - OMEGA) * f[0] + WEIGHTS[0] * base]
    for member in range(1, 19, 2):
        vector = LATTICE[member]
        even = WEIGHTS[member] * (base + dot_c(vector, speed) * dot_c(vector, square))
        odd = WEIGHTS[member] * dot_c(vector, linear)
        posts.append((1.0 - OMEGA) * f[member] + (even + odd))
        posts.append((1.0 - OMEGA) * f[member + 1] + (even - odd))
    return posts


def columns_kernel(f_ref, up, down):
    planes, width_x, width_y = f_ref.shape[1], f_ref.shape[2], f_ref.shape[3]
    lane = iota((width_x, LANES), 1)
    for out, start, at in ((up, width_y - LANES, LANES - 2), (down, 0, 0)):
        lines = out.shape[1] // LANES
        totals = [jnp.zeros((width_x, LANES), F32) for _ in range(lines)]
        for plane in range(19 * planes):
            line, target = divmod(2 * plane, LANES)
            block = f_ref[plane // planes, plane % planes, :, start : start + LANES]
            shift = (target - at) % LANES
            if shift:
                block = pltpu.roll(block, shift, 1)
            totals[line] = jnp.where((lane == target) | (lane == target + 1), block, totals[line])
        for line in range(lines):
            out[:, line * LANES : (line + 1) * LANES] = totals[line]


def corner_kernel(up, down, x_low, x_high, out_up, out_down):
    width_x, width_y = up.shape[0], x_low.shape[1]
    count = x_low.shape[0]
    for source, out, start, at in ((up, out_up, width_y - LANES, LANES - 2), (down, out_down, 0, 0)):
        out[0:width_x, :] = source[...]
        out[width_x:, :] = jnp.zeros((out.shape[0] - width_x, out.shape[1]), F32)
        for number, halo in enumerate((x_low, x_high)):
            for line in range(out.shape[1] // LANES):
                last = min(count, (line + 1) * LANES)
                block = halo[line * LANES : last, start : start + LANES]
                if last < (line + 1) * LANES:
                    block = jnp.concatenate([block, jnp.zeros(((line + 1) * LANES - last, LANES), F32)], axis=0)
                turned = jnp.transpose(block)
                row = width_x + 2 * number
                out[row : row + 2, line * LANES : (line + 1) * LANES] = turned[at : at + 2]


def ring_cells(x_low, x_high, y_low, y_high, f_ref):
    planes, tall, wide = f_ref.shape[1], f_ref.shape[2], f_ref.shape[3]
    width_x, width_y = tall - RING, wide - SIDE
    lane = iota((width_x, LANES), 1)
    wide_lane = iota((LANES, LANES), 1)
    for line in range(y_low.shape[1] // LANES):
        at = slice(line * LANES, (line + 1) * LANES)
        pad = jnp.zeros((LANES - 8, LANES), F32)
        low = jnp.transpose(jnp.concatenate([y_low[width_x:, at], pad], axis=0))
        high = jnp.transpose(jnp.concatenate([y_high[width_x:, at], pad], axis=0))
        corner_low = jnp.where(wide_lane >= LANES - 2, pltpu.roll(low, LANES - 2, 1), high)
        corner_high = jnp.where(
            wide_lane >= LANES - 2, pltpu.roll(low, LANES - 4, 1), pltpu.roll(high, LANES - 2, 1)
        )
        for plane in range(line * LANES // 2, min((line + 1) * LANES // 2, 19 * planes)):
            member, z = divmod(plane, planes)
            here = 2 * plane - line * LANES
            f_ref[member, z, tall - 2 : tall, 0:width_y] = x_low[2 * plane : 2 * plane + 2, :]
            f_ref[member, z, width_x : width_x + 2, 0:width_y] = x_high[2 * plane : 2 * plane + 2, :]
            f_ref[member, z, tall - 2 : tall, width_y:] = corner_low[here : here + 2]
            f_ref[member, z, width_x : width_x + 2, width_y:] = corner_high[here : here + 2]
            below, above = y_low[0:width_x, at], y_high[0:width_x, at]
            if (LANES - 2 - here) % LANES:
                below = pltpu.roll(below, (LANES - 2 - here) % LANES, 1)
            if here:
                above = pltpu.roll(above, LANES - here, 1)
            f_ref[member, z, 0:width_x, width_y:] = jnp.where(lane >= LANES - 2, below, above)


def shifted(block, member):
    along_x, along_y, _ = LATTICE[member]
    if along_x:
        block = pltpu.roll(block, along_x % block.shape[0], 0)
    if along_y:
        block = pltpu.roll(block, along_y % block.shape[1], 1)
    return block


MOVED = [i for i in range(19) if LATTICE[i][0] or LATTICE[i][1]]


def main_kernel(
    cap, steps, f_ref, x_low, x_high, y_low, y_high, force_0, force_1, own_ref, out_ref, back_ref, before, after, probe_0, probe_1, rows
):
    planes, width_x, width_y = f_ref.shape[1], f_ref.shape[2], f_ref.shape[3]
    tall, wide = before.shape[2], before.shape[3]
    ring_cells(x_low, x_high, y_low, y_high, before)

    def blocks(body, own_body):
        @pl.loop(0, planes * (width_x // 8))
        def _(index):
            z = index // (width_x // 8)
            row = pl.multiple_of((index % (width_x // 8)) * 8, 8)
            for start in range(0, width_y, LANES):
                own_body(z, row, pl.ds(start, LANES), pl.multiple_of(index * 8, 8))
            body(z, row, pl.ds(width_y, LANES))

        @pl.loop(0, planes)
        def _(z):
            for start in range(0, wide, LANES):
                body(z, width_x, pl.ds(start, LANES))

    def force_at(ref, z, row, lanes):
        return [ref[pl.ds(pl.multiple_of((n * planes + z) * tall + row, 8), 8), lanes] for n in range(3)]

    def first_body(source, z, row, lanes):
        at = pl.ds(row, 8)
        f = [source[member, z, at, lanes] for member in range(19)]
        density, momenta = moments(f)
        for member, value in enumerate(collide(f, density, momenta, force_at(force_0, z, row, lanes))):
            before[member, z, at, lanes] = value

    blocks(
        lambda z, row, lanes: first_body(before, z, row, lanes),
        lambda z, row, lanes, flat: first_body(f_ref, z, row, lanes),
    )
    for member in MOVED:
        for z in range(planes):
            after[member, (z + LATTICE[member][2]) % planes] = shifted(before[member, z], member)

    def second_body(z, row, lanes, flat=None):
        at = pl.ds(row, 8)
        f = []
        for member in range(19):
            if member in MOVED:
                f.append(after[member, z, at, lanes])
            else:
                f.append(before[member, lax.rem(z - LATTICE[member][2] + planes, planes), at, lanes])
        density, momenta = moments(f)
        if flat is not None:
            inverse = 1.0 / density
            for number, force in enumerate(force_at(force_0, z, row, lanes)):
                probe_0[pl.ds(pl.multiple_of(number * planes * width_x + flat, 8), 8), lanes] = (
                    momenta[number] + 0.5 * force
                ) * inverse
        for member, value in enumerate(collide(f, density, momenta, force_at(force_1, z, row, lanes))):
            after[member, z, at, lanes] = value

    blocks(second_body, second_body)
    for member in range(19):
        for z in range(planes):
            to = (z + LATTICE[member][2]) % planes
            out_ref[member, to] = shifted(after[member, z], member)[0:width_x, 0:width_y]

    @pl.loop(0, planes * (width_x // 8))
    def _(index):
        z = index // (width_x // 8)
        row = pl.multiple_of((index % (width_x // 8)) * 8, 8)
        flat = pl.multiple_of(index * 8, 8)
        for start in range(0, width_y, LANES):
            lanes = pl.ds(start, LANES)
            density, momenta = moments([out_ref[member, z, pl.ds(row, 8), lanes] for member in range(19)])
            inverse = 1.0 / density
            for number, force in enumerate(force_at(force_1, z, row, lanes)):
                probe_1[pl.ds(pl.multiple_of(number * planes * width_x + flat, 8), 8), lanes] = (
                    momenta[number] + 0.5 * force
                ) * inverse

    for step, probe_ref in enumerate((probe_0, probe_1)):
        first = own_ref[8 * step : 8 * step + 8, :]
        for number, row in enumerate(sample(first, planes, width_x, width_y, probe_ref)):
            rows[steps * number + step : steps * number + step + 1, :] = row
    send_back(cap, rows, back_ref)


def send_back(cap, rows, out_ref):
    devices, steps = out_ref.shape[0], out_ref.shape[1]
    per = LANES // cap
    group = iota((steps, LANES), 1) // cap
    for device in range(devices):
        line, place = device // per, device % per
        total = jnp.zeros((steps, LANES), F32)
        for number in range(3):
            piece = rows[number * steps : (number + 1) * steps, line * LANES : (line + 1) * LANES]
            shift = (number - place) * cap % LANES
            if shift:
                piece = pltpu.roll(piece, shift, 1)
            total = jnp.where(group == number, piece, total)
        out_ref[device] = total


def call(kernel, outs, scratch=(), flops=0, moved=0, limit=40, fetched=(False,)):
    shapes = [jax.ShapeDtypeStruct(shape, kind) for shape, kind in outs]
    specs = [pl.BlockSpec(memory_space=pltpu.HBM if own else pltpu.VMEM) for own in fetched]
    return pl.pallas_call(
        kernel,
        out_shape=shapes,
        scratch_shapes=list(scratch),
        **({"in_specs": specs} if any(fetched) else {}),
        cost_estimate=pl.CostEstimate(flops=flops, bytes_accessed=moved, transcendentals=0),
        compiler_params=pltpu.CompilerParams(vmem_limit_bytes=limit * 1024 * 1024),
    )


def pair(up, down, axis):
    count = lax.axis_size(axis)
    forward = [(i, (i + 1) % count) for i in range(count)]
    backward = [(target, source) for source, target in forward]
    return lax.ppermute(up, axis, forward), lax.ppermute(down, axis, backward)


def local(populations_in, marker_force, marker_frac, marker_cell, marker_tile):
    count_gx, count_gy = lax.axis_size("gx"), lax.axis_size("gy")
    devices = count_gx * count_gy
    steps, owned = marker_force.shape[0], marker_force.shape[2]
    cap = max(2, 2 * owned // devices)
    half, slots = cap // 2, devices * cap
    planes, width_x, width_y = populations_in.shape[1:]
    tall, wide = width_x + RING, width_y + SIDE
    grid = (count_gx, count_gy, width_x, width_y)
    by_comp = lambda x: jnp.transpose(x, (1, 0, 2))
    markers = (
        marker_tile.reshape(steps * owned // LANES, LANES),
        by_comp(marker_cell),
        by_comp(marker_frac),
        by_comp(marker_force),
    )
    message = ((devices, 8, LANES), F32)
    rows = pltpu.VMEM((16, owned), F32)

    def send(outgoing):
        return lax.all_to_all(outgoing, ("gx", "gy"), split_axis=0, concat_axis=0, tiled=True)

    def pack_markers(*refs):
        pack_kernel(grid, steps, cap, *refs)

    lines = 2 * 19 * planes
    face = ((lines, width_y), F32)
    outgoing, slot, x_up, x_down = call(
        pack_markers,
        [message, ((steps, owned), jnp.int32), face, face],
        [
            rows,
            pltpu.VMEM((steps * owned // LANES, LANES), jnp.int32),
            pltpu.VMEM((3, steps, owned), jnp.int32),
            pltpu.VMEM((3, steps, owned), F32),
            pltpu.VMEM((3, steps, owned), F32),
            pltpu.VMEM((19, planes, 8, width_y), F32),
            pltpu.VMEM((19, planes, 8, width_y), F32),
            pltpu.SemaphoreType.DMA((6,)),
        ],
        fetched=(True,) * 5,
        limit=63,
    )(*markers, populations_in)
    arrived = send(outgoing)

    x_low, x_high = pair(x_up, x_down, "gx")
    packed = -(-lines // LANES) * LANES
    y_up, y_down = call(columns_kernel, [((width_x, packed), F32)] * 2)(populations_in)
    y_up, y_down = call(corner_kernel, [((width_x + 8, packed), F32)] * 2)(y_up, y_down, x_low, x_high)
    y_low, y_high = pair(y_up, y_down, "gy")

    field = ((3 * planes * tall, wide), F32)

    def spread_markers(*refs):
        spread_kernel(cap, steps, planes, width_x, width_y, *refs)

    *forces, own, most = call(
        spread_markers, [field] * steps + [((8 * steps, slots), F32), ((8, LANES), F32)], flops=4 * 10**9, moved=10**6
    )(arrived)
    most = most[0, 0]

    def again(state):
        return (state[0] * half).astype(F32) < most

    def more(state):
        turn, *forces = state

        def turn_markers(*refs):
            turn_kernel(grid, steps, cap, *refs)

        def add_markers(*refs):
            more_kernel(cap, steps, planes, width_x, width_y, *refs)

        spec = [pl.BlockSpec(memory_space=pltpu.SMEM)] + [pl.BlockSpec(memory_space=pltpu.VMEM)] * 4
        (outgoing,) = pl.pallas_call(
            turn_markers,
            out_shape=[jax.ShapeDtypeStruct(*message)],
            in_specs=spec,
            scratch_shapes=[rows],
            compiler_params=pltpu.CompilerParams(vmem_limit_bytes=40 * 1024 * 1024),
        )(turn.reshape(1), *markers)
        return (turn + 1, *call(add_markers, [field] * steps)(send(outgoing), *forces))

    _, force_0, force_1 = lax.while_loop(again, more, (jnp.int32(1), *forces))

    def main(*refs):
        main_kernel(cap, steps, *refs)

    own_field = pltpu.VMEM((3 * planes * width_x, width_y), F32)
    extended = pltpu.VMEM((19, planes, tall, wide), F32)
    fields, back = call(
        main,
        [(populations_in.shape, F32), ((devices, steps, LANES), F32)],
        [extended, extended, own_field, own_field, pltpu.VMEM((8, slots), F32)],
    )(populations_in, x_low, x_high, y_low, y_high, force_0, force_1, own)
    returned = send(back)

    def unpack(*refs):
        unpack_kernel(cap, steps, *refs)

    (velocity,) = call(unpack, [((3, steps, owned), F32)])(returned, slot)
    return fields, by_comp(velocity)


def solution(mesh):
    return jax.shard_map(
        local,
        mesh=mesh,
        in_specs=(
            P(None, None, "gx", "gy"),
            P(None, None, ("gx", "gy")),
            P(None, None, ("gx", "gy")),
            P(None, None, ("gx", "gy")),
            P(None, ("gx", "gy"), None),
        ),
        out_specs=(P(None, None, "gx", "gy"), P(None, None, ("gx", "gy"))),
        check_vma=False,
    )
```

time: 67.2 us -> 68.5 us (1.019)
  blocking collectives: 28.3 us -> 10.2 us
  Pallas kernels: 18.7 us -> 29 us
  waiting for transfers between devices: 3.98 us -> 8.95 us
  local copies, waits for them, and re-layouts: 2.06 us -> 4.68 us
  loops' own time: 0 us -> 0.82 us
  starting transfers between devices: 13.1 us -> 13.9 us
    all_to_all x2 -> x1, blocking collectives: 28.3 us -> 10.2 us  [send(): lax.all_to_all(outgoing, ('gx', 'gy'), split_axis=0, concat_axis=0, tiled...]
    pallas_call x8 -> x5, Pallas kernels: 17.4 us -> 27.7 us  [the longest x1 13.6 us: local(): call(main, [(populations_in.shape, F32), ((devices, steps, LANES), F32)],...]
    all_to_all x0 -> x1, starting transfers between devices: none -> 7.3 us  [send(): lax.all_to_all(outgoing, ('gx', 'gy'), split_axis=0, concat_axis=0, tiled...]
    ppermute x8 -> x4, starting transfers between devices: 13.1 us -> 6.56 us  [pair(): return (lax.ppermute(up, axis, forward), lax.ppermute(down, axis, backward))]
    ppermute x8 -> x4, waiting for transfers between devices: 3.98 us -> 8.95 us  [pair(): return (lax.ppermute(up, axis, forward), lax.ppermute(down, axis, backward))]
    unnamed x4 -> x14, local copies, waits for them, and re-layouts: 2.06 us -> 4.14 us
    another operation x0 -> x1, loops' own time: none -> 0.82 us  [local(): _, force_0, force_1 = lax.while_loop(again, more, (jnp.int32(1), *forces))]
  transfers between devices with their start and end apart: 8 -> 5, of which waited for: 2 -> 2; matrix products, arithmetic and copies ran while one was open for 0% -> 1% of each run, Pallas kernels for 6% -> 15%
where the time goes in v2:
time: 68.5 us; the launch traced here: 68.2 us
  Pallas kernels  29 us (42%)
  starting transfers between devices  13.9 us (20%)
  blocking collectives  10.2 us (15%)
  waiting for transfers between devices  8.95 us (13%)
  local copies, waits for them, and re-layouts  4.68 us (7%)
  loops' own time  0.82 us (1%)
  between operations  0.75 us (1%)
    pallas_call x1, Pallas kernels, local(): call(main, [(populations_in.shape, F32), ((devices, steps, LANES), F32)],...  13.6 us
    all_to_all x1, blocking collectives, send(): lax.all_to_all(outgoing, ('gx', 'gy'), split_axis=0, concat_axis=0, tiled...  10.2 us
    pallas_call x1, Pallas kernels, local(): call(spread_markers, [field] * steps + [((8 * steps, slots), F32), ((8, L...  9.07 us
    ppermute x4, waiting for transfers between devices, pair(): return (lax.ppermute(up, axis, forward), lax.ppermute(down, axis, backward))  8.95 us
    all_to_all x1, starting transfers between devices, send(): lax.all_to_all(outgoing, ('gx', 'gy'), split_axis=0, concat_axis=0, tiled...  7.3 us
    ppermute x4, starting transfers between devices, pair(): return (lax.ppermute(up, axis, forward), lax.ppermute(down, axis, backward))  6.56 us
    unnamed x14, local copies, waits for them, and re-layouts  4.14 us
    pallas_call x1, Pallas kernels, local(): call(pack_markers, [message, ((steps, owned), jnp.int32), face, face], [r...  4.12 us
  transfers between devices with their start and end apart: 5, of which 2 were waited for; matrix products, arithmetic and copies ran while one was open for 1% of the time, Pallas kernels for 15%

profile of v2, /device:TPU:0, one launch (start us, length us, event | category | flops | bytes accessed | tf_op | source)
XLA Modules:
  0.0 68.2 jit_solution(9581068881376227203)
XLA Ops:
  0.6 4.1 %shard_map.68 = (f32[32,8,128]{2,1,0:T(8,128)}, s32[2,512]{1,0:T(2,128)}, f32[152,384]{1,0:T(8,128)}, f32[152,384]{1,0:T(8,128)}) custom-call(s32[8,128]{1,0:T(8,128)} %bitcast.15, s32[3,2,512]{2,1,0:T(2,128)} %bitcast.9, f32[3,2,512]{2,1,0:T(2,128)} %bitcast.11, f32[3,2,512]{2,1,0:T(2,128)} %bitcast.13, f32[19,4,32,384]{3,2,1,0:T(8,128)} %refs_0_.1), custom_call_target="tpu_custom_call" | custom-call | tf_op jit(solution)/shard_map/pallas_call | solution.py:645
  4.8 7.3 %all-to-all-start.1 = ((f32[32,8,128]{2,1,0:T(8,128)}), f32[32,8,128]{2,1,0:T(8,128)S(1)}, u32[]{:S(2)}, u32[]{:S(2)}) async-start(f32[32,8,128]{2,1,0:T(8,128)} %get-tuple-element.68), calls=%async_computation.1 | async-start | bytes 262144 | tf_op jit(solution)/shard_map/all_to_all | solution.py:638
  12.1 1.8 %collective-permute-start = (f32[152,384]{1,0:T(8,128)}, f32[152,384]{1,0:T(8,128)S(1)}, u32[]{:S(2)}, u32[]{:S(2)}) collective-permute-start(f32[152,384]{1,0:T(8,128)} %get-tuple-element.62), channel_id=1, source_target_pairs={{0,8},{8,16},{16,24},{24,0},{1,9},{9,17},{17,25},{25,1},{2,10},{10... | collective-permute-start | bytes 700424 | tf_op jit(solution)/shard_map/ppermute | solution.py:615
  13.9 2.1 %collective-permute-start.1 = (f32[152,384]{1,0:T(8,128)}, f32[152,384]{1,0:T(8,128)S(1)}, u32[]{:S(2)}, u32[]{:S(2)}) collective-permute-start(f32[152,384]{1,0:T(8,128)} %get-tuple-element.63), channel_id=1, source_target_pairs={{8,0},{16,8},{24,16},{0,24},{9,1},{17,9},{25,17},{1,25},{10,2},{18... | collective-permute-start | bytes 700424 | tf_op jit(solution)/shard_map/ppermute | solution.py:615
  16.0 0.0 copy-start
  16.0 2.1 %copy-done = f32[19,4,32,384]{3,2,1,0:T(8,128)S(1)} copy-done((f32[19,4,32,384]{3,2,1,0:T(8,128)S(1)}, f32[19,4,32,384]{3,2,1,0:T(8,128)}, u32[]{:S(2)}) %copy-start) | copy-done | bytes 3735576
  18.0 0.7 %shard_map.69 = (f32[32,256]{1,0:T(8,128)S(1)}, f32[32,256]{1,0:T(8,128)S(1)}) custom-call(f32[19,4,32,384]{3,2,1,0:T(8,128)S(1)} %copy-done), custom_call_target="tpu_custom_call" | custom-call | tf_op jit(solution)/shard_map/pallas_call | solution.py:665
  18.7 5.6 %collective-permute-done.x_low.refs_1_ = f32[152,384]{1,0:T(8,128)S(1)} collective-permute-done((f32[152,384]{1,0:T(8,128)}, f32[152,384]{1,0:T(8,128)S(1)}, u32[]{:S(2)}, u32[]{:S(2)}) %collective-permute-start) | collective-permute-done | bytes 233504 | tf_op jit(solution)/shard_map/ppermute | solution.py:615
  24.4 3.3 %collective-permute-done.1.x_high.refs_2_ = f32[152,384]{1,0:T(8,128)S(1)} collective-permute-done((f32[152,384]{1,0:T(8,128)}, f32[152,384]{1,0:T(8,128)S(1)}, u32[]{:S(2)}, u32[]{:S(2)}) %collective-permute-start.1) | collective-permute-done | bytes 233504 | tf_op jit(solution)/shard_map/ppermute | solution.py:615
  27.7 0.2 shard_map.70
  27.8 0.0 collective-permute-start.2
  27.9 0.0 copy-start.3
  27.9 0.0 copy-start.4
  27.9 0.0 copy-start.5
  27.9 0.0 copy-start.6
  27.9 2.6 %collective-permute-start.3 = (f32[40,256]{1,0:T(8,128)S(1)}, f32[40,256]{1,0:T(8,128)S(1)}, u32[]{:S(2)}, u32[]{:S(2)}) collective-permute-start(f32[40,256]{1,0:T(8,128)S(1)} %get-tuple-element.67), channel_id=1, source_target_pairs={{1,0},{2,1},{3,2},{4,3},{5,4},{6,5},{7,6},{0,7},{9,8},{10,9},{11,1... | collective-permute-start | bytes 122888 | tf_op jit(solution)/shard_map/ppermute | solution.py:615
  30.6 0.0 all-to-all-done.1.refs_0_
  30.6 9.1 %shard_map.71 = (f32[480,512]{1,0:T(8,128)}, f32[480,512]{1,0:T(8,128)}, f32[16,1024]{1,0:T(8,128)S(1)}, f32[8,128]{1,0:T(8,128)S(1)}) custom-call(f32[32,8,128]{2,1,0:T(8,128)S(1)} %all-to-all-done.1.refs_0_), custom_call_target="tpu_custom_call" | custom-call | flops 4000000000 | bytes 1000000 | tf_op jit(solution)/shard_map/pallas_call | solution.py:674
  39.7 0.5 slice.3
  40.2 0.0 copy-done.3
  40.2 0.0 copy-done.4
  40.2 0.0 copy-done.5
  40.2 0.0 copy-done.6
  40.2 0.8 %while.12 = (s32[]{:T(128)}, f32[480,512]{1,0:T(8,128)}, f32[480,512]{1,0:T(8,128)}, f32[]{:T(128)}, s32[8,128]{1,0:T(8,128)S(1)}, /*index=5*/s32[3,2,512]{2,1,0...) while((s32[]{:T(128)}, f32[480,512]{1,0:T(8,128)}, f32[480,512]{1,0:T(8,128)}, ...), condition=%wide.region_1.0_spmd, body=%wide.region_0.0_spmd.sunk | while | flops 4 | bytes 4325521 | solution.py:701
  41.0 0.0 copy-start.2
  41.0 0.0 collective-permute-done.2.refs_3_
  41.1 0.0 collective-permute-done.3.refs_4_
  41.1 0.0 copy-start.1
  41.1 2.0 %copy-done.1 = f32[19,4,32,384]{3,2,1,0:T(8,128)S(1)} copy-done((f32[19,4,32,384]{3,2,1,0:T(8,128)S(1)}, f32[19,4,32,384]{3,2,1,0:T(8,128)}, u32[]{:S(2)}) %copy-start.1) | copy-done | bytes 3735576
  43.1 13.6 %shard_map.72 = (f32[19,4,32,384]{3,2,1,0:T(8,128)}, f32[32,2,128]{2,1,0:T(2,128)S(1)}) custom-call(f32[19,4,32,384]{3,2,1,0:T(8,128)S(1)} %copy-done.1, f32[152,384]{1,0:T(8,128)S(1)} %collective-permute-done.x_low.refs_1_, f32[152,384]{1,0:T(8,128)S(1)} %collective-permute-done.1.x_high.refs_2_, f32[40,256]{1,0:T(8,128)S(1)} %collective-permute-done.2.refs_3_, ...), custom_call_target="tpu_custom_call" | custom-call | tf_op jit(solution)/shard_map/pallas_call | solution.py:708
  56.8 10.2 %all_to_all.16.refs_0_ = f32[32,2,128]{2,1,0:T(2,128)S(1)} all-to-all(f32[32,2,128]{2,1,0:T(2,128)S(1)} %get-tuple-element.76), channel_id=1, replica_groups=mesh['gx'=4,'gy'=8] {'gx','gy'}, dimensions={0} | all-to-all | bytes 65536 | tf_op jit(solution)/shard_map/all_to_all | solution.py:638
  66.9 0.0 copy-done.2
  67.0 1.2 %shard_map.73 = f32[3,2,512]{2,1,0:T(2,128)} custom-call(f32[32,2,128]{2,1,0:T(2,128)S(1)} %all_to_all.16.refs_0_, s32[2,512]{1,0:T(2,128)S(1)} %copy-done.2), custom_call_target="tpu_custom_call" | custom-call | tf_op jit(solution)/shard_map/pallas_call | solution.py:718
Async XLA Ops:
  4.8 25.8 %all-to-all-start.1 = ((f32[32,8,128]{2,1,0:T(8,128)}), f32[32,8,128]{2,1,0:T(8,128)S(1)}, u32[]{:S(2)}, u32[]{:S(2)}) async-start(f32[32,8,128]{2,1,0:T(8,128)} %get-tuple-element.68), calls=%async_computation.1 | async-start | bytes 262144 | tf_op jit(solution)/shard_map/all_to_all | solution.py:638
  12.1 12.3 %collective-permute-start = (f32[152,384]{1,0:T(8,128)}, f32[152,384]{1,0:T(8,128)S(1)}, u32[]{:S(2)}, u32[]{:S(2)}) collective-permute-start(f32[152,384]{1,0:T(8,128)} %get-tuple-element.62), channel_id=1, source_target_pairs={{0,8},{8,16},{16,24},{24,0},{1,9},{9,17},{17,25},{25,1},{2,10},{10... | collective-permute-start | bytes 700424 | tf_op jit(solution)/shard_map/ppermute | solution.py:615
  13.9 13.8 %collective-permute-start.1 = (f32[152,384]{1,0:T(8,128)}, f32[152,384]{1,0:T(8,128)S(1)}, u32[]{:S(2)}, u32[]{:S(2)}) collective-permute-start(f32[152,384]{1,0:T(8,128)} %get-tuple-element.63), channel_id=1, source_target_pairs={{8,0},{16,8},{24,16},{0,24},{9,1},{17,9},{25,17},{1,25},{10,2},{18... | collective-permute-start | bytes 700424 | tf_op jit(solution)/shard_map/ppermute | solution.py:615
  16.0 2.1 %copy-start = (f32[19,4,32,384]{3,2,1,0:T(8,128)S(1)}, f32[19,4,32,384]{3,2,1,0:T(8,128)}, u32[]{:S(2)}) copy-start(f32[19,4,32,384]{3,2,1,0:T(8,128)} %refs_0_.1) | copy-start | bytes 11206660
  27.8 13.2 %collective-permute-start.2 = (f32[40,256]{1,0:T(8,128)S(1)}, f32[40,256]{1,0:T(8,128)S(1)}, u32[]{:S(2)}, u32[]{:S(2)}) collective-permute-start(f32[40,256]{1,0:T(8,128)S(1)} %get-tuple-element.66), channel_id=1, source_target_pairs={{0,1},{1,2},{2,3},{3,4},{4,5},{5,6},{6,7},{7,0},{8,9},{9,10},{10,1... | collective-permute-start | bytes 122888 | tf_op jit(solution)/shard_map/ppermute | solution.py:615
  27.9 12.3 %copy-start.3 = (s32[2,3,512]{2,0,1:T(2,128)S(1)}, s32[2,3,512]{2,0,1:T(2,128)}, u32[]{:S(2)}) copy-start(s32[2,3,512]{2,0,1:T(2,128)} %param.10) | copy-start | bytes 36868
  27.9 12.3 %copy-start.4 = (f32[2,3,512]{2,0,1:T(2,128)S(1)}, f32[2,3,512]{2,0,1:T(2,128)}, u32[]{:S(2)}) copy-start(f32[2,3,512]{2,0,1:T(2,128)} %param.9) | copy-start | bytes 36868
  27.9 12.3 %copy-start.5 = (f32[2,3,512]{2,0,1:T(2,128)S(1)}, f32[2,3,512]{2,0,1:T(2,128)}, u32[]{:S(2)}) copy-start(f32[2,3,512]{2,0,1:T(2,128)} %param.8) | copy-start | bytes 36868
  27.9 12.3 %copy-start.6 = (s32[2,512,1]{1,2,0:T(1,128)S(1)}, s32[2,512,1]{1,2,0:T(1,128)}, u32[]{:S(2)}) copy-start(s32[2,512,1]{1,2,0:T(1,128)} %param.11) | copy-start | bytes 12292
  27.9 13.1 %collective-permute-start.3 = (f32[40,256]{1,0:T(8,128)S(1)}, f32[40,256]{1,0:T(8,128)S(1)}, u32[]{:S(2)}, u32[]{:S(2)}) collective-permute-start(f32[40,256]{1,0:T(8,128)S(1)} %get-tuple-element.67), channel_id=1, source_target_pairs={{1,0},{2,1},{3,2},{4,3},{5,4},{6,5},{7,6},{0,7},{9,8},{10,9},{11,1... | collective-permute-start | bytes 122888 | tf_op jit(solution)/shard_map/ppermute | solution.py:615
  41.0 25.9 %copy-start.2 = (s32[2,512]{1,0:T(2,128)S(1)}, s32[2,512]{1,0:T(2,128)}, u32[]{:S(2)}) copy-start(s32[2,512]{1,0:T(2,128)} %get-tuple-element.77.refs_1_) | copy-start | bytes 12292
  41.1 2.1 %copy-start.1 = (f32[19,4,32,384]{3,2,1,0:T(8,128)S(1)}, f32[19,4,32,384]{3,2,1,0:T(8,128)}, u32[]{:S(2)}) copy-start(f32[19,4,32,384]{3,2,1,0:T(8,128)} %refs_0_.1) | copy-start | bytes 11206660

commit v3 on v2

--- a/solution.py
+++ b/solution.py
@@ -189,32 +189,28 @@
 
 
 def pack_kernel(
-    grid, steps, cap, tile_in, cell_in, frac_in, force_in, f_in, out_ref, slot_ref, x_up, x_down,
-    rows, tile_ref, cell_ref, frac_ref, force_ref, near_ref, far_ref, sems,
+    grid, steps, cap, tile_in, cell_in, frac_in, force_in, after_ref, out_ref, slot_ref,
+    rows, tile_ref, cell_ref, frac_ref, force_ref, sems,
 ):
-    width_x = f_in.shape[2]
+    copies = fetch([(tile_in, tile_ref), (cell_in, cell_ref), (frac_in, frac_ref), (force_in, force_ref)], sems)
+    for copy in copies:
+        copy.wait()
+    pack(grid, steps, cap, marker_rows(tile_ref, cell_ref, frac_ref, force_ref), out_ref, slot_ref, rows)
+
+
+def strips_kernel(f_in, x_up, x_down, near_ref, far_ref, sems):
+    planes, width_x = f_in.shape[1], f_in.shape[2]
     copies = fetch(
         [
-            (tile_in, tile_ref),
-            (cell_in, cell_ref),
-            (frac_in, frac_ref),
-            (force_in, force_ref),
+            (f_in.at[:, :, pl.ds(width_x - 8, 8), :], far_ref),
             (f_in.at[:, :, pl.ds(0, 8), :], near_ref),
-            (f_in.at[:, :, pl.ds(width_x - 8, 8), :], far_ref),
         ],
         sems,
     )
-    for copy in copies[:4]:
+    for copy, out, source, start in ((copies[0], x_up, far_ref, 6), (copies[1], x_down, near_ref, 0)):
         copy.wait()
-    pack(grid, steps, cap, marker_rows(tile_ref, cell_ref, frac_ref, force_ref), out_ref, slot_ref, rows)
-    for copy in copies[4:]:
-        copy.wait()
-    planes = f_in.shape[1]
-    for member in range(19):
-        for z in range(planes):
-            plane = member * planes + z
-            x_up[2 * plane : 2 * plane + 2, :] = far_ref[member, z, 6:8, :]
-            x_down[2 * plane : 2 * plane + 2, :] = near_ref[member, z, 0:2, :]
+        for plane in range(19 * planes):
+            out[2 * plane : 2 * plane + 2, :] = source[plane // planes, plane % planes, start : start + 2, :]
 
 
 def turn_kernel(grid, steps, cap, turn_ref, tile_ref, cell_ref, frac_ref, force_ref, out_ref, rows):
@@ -288,18 +284,20 @@
 
 def product(table, along_y):
     high, low = split2(table)
-    return nt(high, along_y[0]) + nt(high, along_y[1]) + nt(low, along_y[0])
+    high_y, low_y = along_y
+    return nt(
+        jnp.concatenate([high, low, high], axis=1), jnp.concatenate([high_y, high_y, low_y], axis=1)
+    )
 
 
 def spread_own(first, second, planes, width_x, width_y, force_ref):
     tall = width_x + RING
     table = jnp.concatenate(plane_table(first, planes, width_x), axis=0)
     along_y = y_table(first[1:2], first[4:5], width_y)
-    for number, strength in enumerate((first[6:7], first[7:8], second[0:1])):
-        found = product(table * strength, along_y)
-        for z in range(planes):
-            at = (number * planes + z) * tall
-            force_ref[at : at + width_x, 0:width_y] = found[z * width_x : (z + 1) * width_x]
+    strengths = (first[6:7], first[7:8], second[0:1])
+    found = product(jnp.concatenate([table * strength for strength in strengths], axis=0), along_y)
+    for number in range(3 * planes):
+        force_ref[number * tall : number * tall + width_x, 0:width_y] = found[number * width_x : (number + 1) * width_x]
 
 
 def spread_ghosts(first, second, planes, width_x, width_y, force_ref, add):
@@ -313,24 +311,24 @@
     ring = [kernel_z[z : z + 1] * kernel_x[width_x:] for z in range(planes)]
     side = [kernel_z[z : z + 1] * kernel_x[0:width_x] for z in range(planes)]
     ring, side = jnp.concatenate(ring, axis=0), jnp.concatenate(side, axis=0)
-    for number, strength in enumerate((first[7:8], second[1:2], second[2:3])):
-        found_ring = product(ring * strength, along_y)
-        found_side = product(side * strength, side_y)
-        for z in range(planes):
-            at = (number * planes + z) * tall
-            part_ring = found_ring[z * RING : (z + 1) * RING]
-            part_side = found_side[z * width_x : (z + 1) * width_x]
-            if add:
-                part_ring = part_ring + force_ref[at + width_x : at + tall, :]
-                part_side = part_side + force_ref[at : at + width_x, width_y:]
-            force_ref[at + width_x : at + tall, :] = part_ring
-            force_ref[at : at + width_x, width_y:] = part_side
+    strengths = (first[7:8], second[1:2], second[2:3])
+    found_ring = product(jnp.concatenate([ring * strength for strength in strengths], axis=0), along_y)
+    found_side = product(jnp.concatenate([side * strength for strength in strengths], axis=0), side_y)
+    for number in range(3 * planes):
+        at = number * tall
+        part_ring = found_ring[number * RING : (number + 1) * RING]
+        part_side = found_side[number * width_x : (number + 1) * width_x]
+        if add:
+            part_ring = part_ring + force_ref[at + width_x : at + tall, :]
+            part_side = part_side + force_ref[at : at + width_x, width_y:]
+        force_ref[at + width_x : at + tall, :] = part_ring
+        force_ref[at : at + width_x, width_y:] = part_side
 
 
 def spread_kernel(cap, steps, planes, width_x, width_y, recv_ref, *outs):
     forces, own_ref, most_ref = outs[:steps], outs[steps], outs[steps + 1]
     half = cap // 2
-    most = jnp.zeros((1, 1), F32)
+    most = jnp.float32(0)
     for step in range(steps):
         start = 2 * step * cap
         first = gather(recv_ref, start, cap)
@@ -340,8 +338,8 @@
         first = gather(recv_ref, start + cap, half)
         second = gather(recv_ref, start + cap + half, half)
         spread_ghosts(first, second, planes, width_x, width_y, forces[step], False)
-        most = jnp.maximum(most, jnp.max(second[3:4], axis=1, keepdims=True))
-    most_ref[...] = jnp.broadcast_to(most, most_ref.shape)
+        most = jnp.maximum(most, jnp.max(second[3:4]))
+    most_ref[0] = most
 
 
 def more_kernel(cap, steps, planes, width_x, width_y, recv_ref, *refs):
@@ -358,11 +356,10 @@
     table = jnp.concatenate(plane_table(first, planes, width_x), axis=0)
     along_y = y_table(first[1:2], first[4:5], width_y)
     size = planes * width_x
-    rows = []
-    for number in range(3):
-        high, low = split2(probe_ref[number * size : (number + 1) * size, :])
-        found = nn(high, along_y[0]) + nn(high, along_y[1]) + nn(low, along_y[0])
-        rows.append(jnp.sum(found * table, axis=0, keepdims=True))
+    high, low = split2(probe_ref[...])
+    high_y, low_y = along_y
+    found = nn(jnp.concatenate([high, low, high], axis=1), jnp.concatenate([high_y, high_y, low_y], axis=0))
+    rows = [jnp.sum(found[n * size : (n + 1) * size] * table, axis=0, keepdims=True) for n in range(3)]
     return rows
 
 
@@ -420,15 +417,23 @@
     return posts
 
 
-def columns_kernel(f_ref, up, down):
-    planes, width_x, width_y = f_ref.shape[1], f_ref.shape[2], f_ref.shape[3]
+def columns_kernel(f_in, after_ref, up, down, far_ref, near_ref, sems):
+    planes, width_x, width_y = f_in.shape[1], f_in.shape[2], f_in.shape[3]
+    copies = fetch(
+        [
+            (f_in.at[:, :, :, pl.ds(width_y - LANES, LANES)], far_ref),
+            (f_in.at[:, :, :, pl.ds(0, LANES)], near_ref),
+        ],
+        sems,
+    )
     lane = iota((width_x, LANES), 1)
-    for out, start, at in ((up, width_y - LANES, LANES - 2), (down, 0, 0)):
+    for copy, out, source, at in ((copies[0], up, far_ref, LANES - 2), (copies[1], down, near_ref, 0)):
+        copy.wait()
         lines = out.shape[1] // LANES
         totals = [jnp.zeros((width_x, LANES), F32) for _ in range(lines)]
         for plane in range(19 * planes):
             line, target = divmod(2 * plane, LANES)
-            block = f_ref[plane // planes, plane % planes, :, start : start + LANES]
+            block = source[plane // planes, plane % planes]
             shift = (target - at) % LANES
             if shift:
                 block = pltpu.roll(block, shift, 1)
@@ -496,10 +501,18 @@
 
 
 def main_kernel(
-    cap, steps, f_ref, x_low, x_high, y_low, y_high, force_0, force_1, own_ref, out_ref, back_ref, before, after, probe_0, probe_1, rows
+    cap, steps, f_in, x_low, x_high, y_low, y_high, force_0, force_1, own_ref, out_ref, back_ref,
+    before, after, probe_0, probe_1, rows, sems,
 ):
-    planes, width_x, width_y = f_ref.shape[1], f_ref.shape[2], f_ref.shape[3]
+    planes, width_x, width_y = f_in.shape[1], f_in.shape[2], f_in.shape[3]
     tall, wide = before.shape[2], before.shape[3]
+    copies = fetch(
+        [
+            (f_in.at[:, z], before.at[:, z, pl.ds(0, width_x), pl.ds(0, width_y)])
+            for z in range(planes)
+        ],
+        sems,
+    )
     ring_cells(x_low, x_high, y_low, y_high, before)
 
     def blocks(body, own_body):
@@ -519,17 +532,16 @@
     def force_at(ref, z, row, lanes):
         return [ref[pl.ds(pl.multiple_of((n * planes + z) * tall + row, 8), 8), lanes] for n in range(3)]
 
-    def first_body(source, z, row, lanes):
+    def first_body(z, row, lanes, flat=None):
         at = pl.ds(row, 8)
-        f = [source[member, z, at, lanes] for member in range(19)]
+        f = [before[member, z, at, lanes] for member in range(19)]
         density, momenta = moments(f)
         for member, value in enumerate(collide(f, density, momenta, force_at(force_0, z, row, lanes))):
             before[member, z, at, lanes] = value
 
-    blocks(
-        lambda z, row, lanes: first_body(before, z, row, lanes),
-        lambda z, row, lanes, flat: first_body(f_ref, z, row, lanes),
-    )
+    for copy in copies:
+        copy.wait()
+    blocks(first_body, first_body)
     for member in MOVED:
         for z in range(planes):
             after[member, (z + LATTICE[member][2]) % planes] = shifted(before[member, z], member)
@@ -597,10 +609,12 @@
 
 def call(kernel, outs, scratch=(), flops=0, moved=0, limit=40, fetched=(False,)):
     shapes = [jax.ShapeDtypeStruct(shape, kind) for shape, kind in outs]
+    out_specs = [pl.BlockSpec(memory_space=pltpu.SMEM if len(shape) == 1 else pltpu.VMEM) for shape, _ in outs]
     specs = [pl.BlockSpec(memory_space=pltpu.HBM if own else pltpu.VMEM) for own in fetched]
     return pl.pallas_call(
         kernel,
         out_shape=shapes,
+        out_specs=out_specs,
         scratch_shapes=list(scratch),
         **({"in_specs": specs} if any(fetched) else {}),
         cost_estimate=pl.CostEstimate(flops=flops, bytes_accessed=moved, transcendentals=0),
@@ -642,27 +656,46 @@
 
     lines = 2 * 19 * planes
     face = ((lines, width_y), F32)
-    outgoing, slot, x_up, x_down = call(
+    x_up, x_down = call(
+        strips_kernel,
+        [face, face],
+        [
+            pltpu.VMEM((19, planes, 8, width_y), F32),
+            pltpu.VMEM((19, planes, 8, width_y), F32),
+            pltpu.SemaphoreType.DMA((2,)),
+        ],
+        fetched=(True,),
+        limit=63,
+    )(populations_in)
+    outgoing, slot = call(
         pack_markers,
-        [message, ((steps, owned), jnp.int32), face, face],
+        [message, ((steps, owned), jnp.int32)],
         [
             rows,
             pltpu.VMEM((steps * owned // LANES, LANES), jnp.int32),
             pltpu.VMEM((3, steps, owned), jnp.int32),
             pltpu.VMEM((3, steps, owned), F32),
             pltpu.VMEM((3, steps, owned), F32),
-            pltpu.VMEM((19, planes, 8, width_y), F32),
-            pltpu.VMEM((19, planes, 8, width_y), F32),
-            pltpu.SemaphoreType.DMA((6,)),
+            pltpu.SemaphoreType.DMA((4,)),
         ],
         fetched=(True,) * 5,
         limit=63,
-    )(*markers, populations_in)
+    )(*markers, x_up)
     arrived = send(outgoing)
 
     x_low, x_high = pair(x_up, x_down, "gx")
     packed = -(-lines // LANES) * LANES
-    y_up, y_down = call(columns_kernel, [((width_x, packed), F32)] * 2)(populations_in)
+    y_up, y_down = call(
+        columns_kernel,
+        [((width_x, packed), F32)] * 2,
+        [
+            pltpu.VMEM((19, planes, width_x, LANES), F32),
+            pltpu.VMEM((19, planes, width_x, LANES), F32),
+            pltpu.SemaphoreType.DMA((2,)),
+        ],
+        fetched=(True,) * 2,
+        limit=63,
+    )(populations_in, slot)
     y_up, y_down = call(corner_kernel, [((width_x + 8, packed), F32)] * 2)(y_up, y_down, x_low, x_high)
     y_low, y_high = pair(y_up, y_down, "gy")
 
@@ -672,9 +705,9 @@
         spread_kernel(cap, steps, planes, width_x, width_y, *refs)
 
     *forces, own, most = call(
-        spread_markers, [field] * steps + [((8 * steps, slots), F32), ((8, LANES), F32)], flops=4 * 10**9, moved=10**6
+        spread_markers, [field] * steps + [((8 * steps, slots), F32), ((1,), F32)], flops=4 * 10**9, moved=10**6
     )(arrived)
-    most = most[0, 0]
+    most = most.reshape(())
 
     def again(state):
         return (state[0] * half).astype(F32) < most
@@ -708,7 +741,9 @@
     fields, back = call(
         main,
         [(populations_in.shape, F32), ((devices, steps, LANES), F32)],
-        [extended, extended, own_field, own_field, pltpu.VMEM((8, slots), F32)],
+        [extended, extended, own_field, own_field, pltpu.VMEM((8, slots), F32), pltpu.SemaphoreType.DMA((planes,))],
+        fetched=(True,) + (False,) * 7,
+        limit=50,
     )(populations_in, x_low, x_high, y_low, y_high, force_0, force_1, own)
     returned = send(back)
 

time: 68.5 us -> 65.4 us (0.955)
  local copies, waits for them, and re-layouts: 4.68 us -> 1.54 us
  waiting for transfers between devices: 8.95 us -> 10.4 us
  blocking collectives: 10.2 us -> 8.97 us
    unnamed x14, local copies, waits for them, and re-layouts: 4.14 us -> 1.54 us
    ppermute x4, waiting for transfers between devices: 8.95 us -> 10.4 us  [pair(): return (lax.ppermute(up, axis, forward), lax.ppermute(down, axis, backward))]
    all_to_all x1, blocking collectives: 10.2 us -> 8.97 us  [send(): lax.all_to_all(outgoing, ('gx', 'gy'), split_axis=0, concat_axis=0, tiled...]
    pallas_call x3 -> x4, Pallas kernels: 13.9 us -> 13.5 us  [the longest x1 5.41 us: local(): call(spread_markers, [field] * steps + [((8 * steps, slots), F32), ((1,),...]
  transfers between devices with their start and end apart: 5 -> 5, of which waited for: 2 -> 2; matrix products, arithmetic and copies ran while one was open for 1% -> 0% of each run, Pallas kernels for 15% -> 13%
where the time goes in v3:
time: 65.4 us; the launch traced here: 65 us
  Pallas kernels  28.8 us (44%)
  starting transfers between devices  13.6 us (21%)
  waiting for transfers between devices  10.4 us (16%)
  blocking collectives  8.97 us (14%)
  local copies, waits for them, and re-layouts  1.54 us (2%)
  loops' own time  0.79 us (1%)
  between operations  0.79 us (1%)
    pallas_call x1, Pallas kernels, local(): call(main, [(populations_in.shape, F32), ((devices, steps, LANES), F32)],...  13.9 us
    ppermute x4, waiting for transfers between devices, pair(): return (lax.ppermute(up, axis, forward), lax.ppermute(down, axis, backward))  10.4 us
    all_to_all x1, blocking collectives, send(): lax.all_to_all(outgoing, ('gx', 'gy'), split_axis=0, concat_axis=0, tiled...  8.97 us
    all_to_all x1, starting transfers between devices, send(): lax.all_to_all(outgoing, ('gx', 'gy'), split_axis=0, concat_axis=0, tiled...  7.3 us
    ppermute x4, starting transfers between devices, pair(): return (lax.ppermute(up, axis, forward), lax.ppermute(down, axis, backward))  6.35 us
    pallas_call x1, Pallas kernels, local(): call(spread_markers, [field] * steps + [((8 * steps, slots), F32), ((1,),...  5.41 us
    pallas_call x1, Pallas kernels, local(): call(pack_markers, [message, ((steps, owned), jnp.int32)], [rows, pltpu.V...  3.05 us
    pallas_call x1, Pallas kernels, local(): call(columns_kernel, [((width_x, packed), F32)] * 2, [pltpu.VMEM((19, pla...  2.7 us
  transfers between devices with their start and end apart: 5, of which 2 were waited for; matrix products, arithmetic and copies ran while one was open for 0% of the time, Pallas kernels for 13%

profile of v3, /device:TPU:0, one launch (start us, length us, event | category | flops | bytes accessed | tf_op | source)
XLA Modules:
  0.0 65.0 jit_solution(3812283624966876987)
XLA Ops:
  0.6 0.0 copy-start.6
  0.6 0.0 copy-start.3
  0.7 0.0 copy-start.4
  0.7 0.0 copy-start.5
  0.7 2.3 %shard_map.68 = (f32[152,384]{1,0:T(8,128)}, f32[152,384]{1,0:T(8,128)}) custom-call(f32[19,4,32,384]{3,2,1,0:T(8,128)} %refs_0_.1), custom_call_target="tpu_custom_call" | custom-call | tf_op jit(solution)/shard_map/pallas_call | solution.py:659
  3.0 0.0 copy-done.6
  3.0 0.0 copy-done.3
  3.0 0.0 copy-done.4
  3.0 0.0 copy-done.5
  3.0 3.1 %shard_map.69 = (f32[32,8,128]{2,1,0:T(8,128)}, s32[2,512]{1,0:T(2,128)}) custom-call(s32[8,128]{1,0:T(8,128)S(1)} %bitcast.15, s32[3,2,512]{2,1,0:T(2,128)S(1)} %bitcast.9, f32[3,2,512]{2,1,0:T(2,128)S(1)} %bitcast.11, f32[3,2,512]{2,1,0:T(2,128)S(1)} %bitcast.13, f32[152,384]{1,0:T(8,128)} %get-tuple-element.62.refs_4_), custom_call_target="tpu_custom_call" | custom-call | tf_op jit(solution)/shard_map/pallas_call | solution.py:670
  6.1 7.3 %all-to-all-start.1 = ((f32[32,8,128]{2,1,0:T(8,128)}), f32[32,8,128]{2,1,0:T(8,128)S(1)}, u32[]{:S(2)}, u32[]{:S(2)}) async-start(f32[32,8,128]{2,1,0:T(8,128)} %get-tuple-element.69), calls=%async_computation.1 | async-start | bytes 262144 | tf_op jit(solution)/shard_map/all_to_all | solution.py:652
  13.4 3.7 %collective-permute-start.1 = (f32[152,384]{1,0:T(8,128)}, f32[152,384]{1,0:T(8,128)S(1)}, u32[]{:S(2)}, u32[]{:S(2)}) collective-permute-start(f32[152,384]{1,0:T(8,128)} %get-tuple-element.63), channel_id=1, source_target_pairs={{8,0},{16,8},{24,16},{0,24},{9,1},{17,9},{25,17},{1,25},{10,2},{18... | collective-permute-start | bytes 700424 | tf_op jit(solution)/shard_map/ppermute | solution.py:629
  17.1 0.0 collective-permute-start
  17.1 2.7 %shard_map.70 = (f32[32,256]{1,0:T(8,128)}, f32[32,256]{1,0:T(8,128)}) custom-call(f32[19,4,32,384]{3,2,1,0:T(8,128)} %refs_0_.1, s32[2,512]{1,0:T(2,128)} %get-tuple-element.64.after_ref.refs_1_), custom_call_target="tpu_custom_call" | custom-call | tf_op jit(solution)/shard_map/pallas_call | solution.py:688
  19.8 3.7 %collective-permute-done.1.x_high.refs_2_ = f32[152,384]{1,0:T(8,128)S(1)} collective-permute-done((f32[152,384]{1,0:T(8,128)}, f32[152,384]{1,0:T(8,128)S(1)}, u32[]{:S(2)}, u32[]{:S(2)}) %collective-permute-start.1) | collective-permute-done | bytes 233504 | tf_op jit(solution)/shard_map/ppermute | solution.py:629
  23.5 6.7 %collective-permute-done.x_low.refs_1_ = f32[152,384]{1,0:T(8,128)S(1)} collective-permute-done((f32[152,384]{1,0:T(8,128)}, f32[152,384]{1,0:T(8,128)S(1)}, u32[]{:S(2)}, u32[]{:S(2)}) %collective-permute-start) | collective-permute-done | bytes 233504 | tf_op jit(solution)/shard_map/ppermute | solution.py:629
  30.2 0.0 copy-start
  30.2 0.8 %copy-done = f32[32,256]{1,0:T(8,128)S(1)} copy-done((f32[32,256]{1,0:T(8,128)S(1)}, f32[32,256]{1,0:T(8,128)}, u32[]{:S(2)}) %copy-start) | copy-done | bytes 32792
  31.0 0.0 copy-start.1
  31.0 0.8 %copy-done.1 = f32[32,256]{1,0:T(8,128)S(1)} copy-done((f32[32,256]{1,0:T(8,128)S(1)}, f32[32,256]{1,0:T(8,128)}, u32[]{:S(2)}) %copy-start.1) | copy-done | bytes 32792
  31.7 0.2 shard_map.71
  31.9 0.0 collective-permute-start.2
  31.9 2.6 %collective-permute-start.3 = (f32[40,256]{1,0:T(8,128)S(1)}, f32[40,256]{1,0:T(8,128)S(1)}, u32[]{:S(2)}, u32[]{:S(2)}) collective-permute-start(f32[40,256]{1,0:T(8,128)S(1)} %get-tuple-element.68), channel_id=1, source_target_pairs={{1,0},{2,1},{3,2},{4,3},{5,4},{6,5},{7,6},{0,7},{9,8},{10,9},{11,1... | collective-permute-start | bytes 122888 | tf_op jit(solution)/shard_map/ppermute | solution.py:629
  34.6 0.0 all-to-all-done.1.refs_0_
  34.6 5.4 %shard_map.72 = (f32[480,512]{1,0:T(8,128)}, f32[480,512]{1,0:T(8,128)}, f32[16,1024]{1,0:T(8,128)S(1)}, f32[1]{0:T(128)}) custom-call(f32[32,8,128]{2,1,0:T(8,128)S(1)} %all-to-all-done.1.refs_0_), custom_call_target="tpu_custom_call" | custom-call | flops 4000000000 | bytes 1000000 | tf_op jit(solution)/shard_map/pallas_call | solution.py:707
  40.0 0.8 %while.12 = (s32[]{:T(128)}, f32[480,512]{1,0:T(8,128)}, f32[480,512]{1,0:T(8,128)}, f32[]{:T(128)}, s32[8,128]{1,0:T(8,128)S(1)}, /*index=5*/s32[3,2,512]{2,1,0...) while((s32[]{:T(128)}, f32[480,512]{1,0:T(8,128)}, f32[480,512]{1,0:T(8,128)}, ...), condition=%wide.region_1.0_spmd, body=%wide.region_0.0_spmd.sunk | while | flops 4 | bytes 4325521 | solution.py:734
  40.8 0.0 copy-start.2
  40.8 0.0 collective-permute-done.2.refs_3_
  40.8 0.0 collective-permute-done.3.refs_4_
  40.8 13.9 %shard_map.73 = (f32[19,4,32,384]{3,2,1,0:T(8,128)}, f32[32,2,128]{2,1,0:T(2,128)S(1)}) custom-call(f32[19,4,32,384]{3,2,1,0:T(8,128)} %refs_0_.1, f32[152,384]{1,0:T(8,128)S(1)} %collective-permute-done.x_low.refs_1_, f32[152,384]{1,0:T(8,128)S(1)} %collective-permute-done.1.x_high.refs_2_, f32[40,256]{1,0:T(8,128)S(1)} %collective-permute-done.2.refs_3_, ...), custom_call_target="tpu_custom_call" | custom-call | tf_op jit(solution)/shard_map/pallas_call | solution.py:741
  54.7 9.0 %all_to_all.16.refs_0_ = f32[32,2,128]{2,1,0:T(2,128)S(1)} all-to-all(f32[32,2,128]{2,1,0:T(2,128)S(1)} %get-tuple-element.77), channel_id=1, replica_groups=mesh['gx'=4,'gy'=8] {'gx','gy'}, dimensions={0} | all-to-all | bytes 65536 | tf_op jit(solution)/shard_map/all_to_all | solution.py:652
  63.7 0.0 copy-done.2
  63.7 1.2 %shard_map.74 = f32[3,2,512]{2,1,0:T(2,128)} custom-call(f32[32,2,128]{2,1,0:T(2,128)S(1)} %all_to_all.16.refs_0_, s32[2,512]{1,0:T(2,128)S(1)} %copy-done.2), custom_call_target="tpu_custom_call" | custom-call | tf_op jit(solution)/shard_map/pallas_call | solution.py:753
Async XLA Ops:
  0.6 2.4 %copy-start.6 = (s32[2,512,1]{1,2,0:T(1,128)S(1)}, s32[2,512,1]{1,2,0:T(1,128)}, u32[]{:S(2)}) copy-start(s32[2,512,1]{1,2,0:T(1,128)} %param.11) | copy-start | bytes 12292
  0.6 2.4 %copy-start.3 = (s32[2,3,512]{2,0,1:T(2,128)S(1)}, s32[2,3,512]{2,0,1:T(2,128)}, u32[]{:S(2)}) copy-start(s32[2,3,512]{2,0,1:T(2,128)} %param.10) | copy-start | bytes 36868
  0.7 2.4 %copy-start.4 = (f32[2,3,512]{2,0,1:T(2,128)S(1)}, f32[2,3,512]{2,0,1:T(2,128)}, u32[]{:S(2)}) copy-start(f32[2,3,512]{2,0,1:T(2,128)} %param.9) | copy-start | bytes 36868
  0.7 2.4 %copy-start.5 = (f32[2,3,512]{2,0,1:T(2,128)S(1)}, f32[2,3,512]{2,0,1:T(2,128)}, u32[]{:S(2)}) copy-start(f32[2,3,512]{2,0,1:T(2,128)} %param.8) | copy-start | bytes 36868
  6.1 28.5 %all-to-all-start.1 = ((f32[32,8,128]{2,1,0:T(8,128)}), f32[32,8,128]{2,1,0:T(8,128)S(1)}, u32[]{:S(2)}, u32[]{:S(2)}) async-start(f32[32,8,128]{2,1,0:T(8,128)} %get-tuple-element.69), calls=%async_computation.1 | async-start | bytes 262144 | tf_op jit(solution)/shard_map/all_to_all | solution.py:652
  13.4 10.1 %collective-permute-start.1 = (f32[152,384]{1,0:T(8,128)}, f32[152,384]{1,0:T(8,128)S(1)}, u32[]{:S(2)}, u32[]{:S(2)}) collective-permute-start(f32[152,384]{1,0:T(8,128)} %get-tuple-element.63), channel_id=1, source_target_pairs={{8,0},{16,8},{24,16},{0,24},{9,1},{17,9},{25,17},{1,25},{10,2},{18... | collective-permute-start | bytes 700424 | tf_op jit(solution)/shard_map/ppermute | solution.py:629
  17.1 13.2 %collective-permute-start = (f32[152,384]{1,0:T(8,128)}, f32[152,384]{1,0:T(8,128)S(1)}, u32[]{:S(2)}, u32[]{:S(2)}) collective-permute-start(f32[152,384]{1,0:T(8,128)} %get-tuple-element.62.refs_4_), channel_id=1, source_target_pairs={{0,8},{8,16},{16,24},{24,0},{1,9},{9,17},{17,25},{25,1},{2,10},{10... | collective-permute-start | bytes 700424 | tf_op jit(solution)/shard_map/ppermute | solution.py:629
  30.2 0.8 %copy-start = (f32[32,256]{1,0:T(8,128)S(1)}, f32[32,256]{1,0:T(8,128)}, u32[]{:S(2)}) copy-start(f32[32,256]{1,0:T(8,128)} %get-tuple-element.65.up) | copy-start | bytes 98308
  31.0 0.8 %copy-start.1 = (f32[32,256]{1,0:T(8,128)S(1)}, f32[32,256]{1,0:T(8,128)}, u32[]{:S(2)}) copy-start(f32[32,256]{1,0:T(8,128)} %get-tuple-element.66.down) | copy-start | bytes 98308
  31.9 8.9 %collective-permute-start.2 = (f32[40,256]{1,0:T(8,128)S(1)}, f32[40,256]{1,0:T(8,128)S(1)}, u32[]{:S(2)}, u32[]{:S(2)}) collective-permute-start(f32[40,256]{1,0:T(8,128)S(1)} %get-tuple-element.67), channel_id=1, source_target_pairs={{0,1},{1,2},{2,3},{3,4},{4,5},{5,6},{6,7},{7,0},{8,9},{9,10},{10,1... | collective-permute-start | bytes 122888 | tf_op jit(solution)/shard_map/ppermute | solution.py:629
  31.9 8.9 %collective-permute-start.3 = (f32[40,256]{1,0:T(8,128)S(1)}, f32[40,256]{1,0:T(8,128)S(1)}, u32[]{:S(2)}, u32[]{:S(2)}) collective-permute-start(f32[40,256]{1,0:T(8,128)S(1)} %get-tuple-element.68), channel_id=1, source_target_pairs={{1,0},{2,1},{3,2},{4,3},{5,4},{6,5},{7,6},{0,7},{9,8},{10,9},{11,1... | collective-permute-start | bytes 122888 | tf_op jit(solution)/shard_map/ppermute | solution.py:629
  40.8 22.9 %copy-start.2 = (s32[2,512]{1,0:T(2,128)S(1)}, s32[2,512]{1,0:T(2,128)}, u32[]{:S(2)}) copy-start(s32[2,512]{1,0:T(2,128)} %get-tuple-element.64.after_ref.refs_1_) | copy-start | bytes 12292

commit v4 on v3

--- a/solution.py
+++ b/solution.py
@@ -80,9 +80,9 @@
 
 def ghosts(step, steps, count_gx, count_gy, width_x, width_y, tiles, cell_x, cell_y):
     reach = steps - step
-    along = []
     tiles = tiles.astype(F32)
     gx = jnp.floor((tiles + 0.5) * (1.0 / count_gy))
+    along = []
     for cell, width, place, count in (
         (cell_x, width_x, gx, count_gx),
         (cell_y, width_y, tiles - gx * count_gy, count_gy),
@@ -90,20 +90,12 @@
         above, below = cell >= width - 1 - reach, cell <= reach - 1
         place_up = jnp.where(place == count - 1, 0.0, place + 1.0)
         place_down = jnp.where(place == 0, count - 1.0, place - 1.0)
-        along.append(
-            (
-                jnp.where(above | below, 1.0, 0.0),
-                place,
-                jnp.where(above, place_up, place_down),
-                cell,
-                jnp.where(above, cell - width, cell + width),
-            )
-        )
-    (near_x, here_x, there_x, in_x, out_x), (near_y, here_y, there_y, in_y, out_y) = along
+        along.append((jnp.where(above | below, 1.0, 0.0), place, jnp.where(above, place_up, place_down)))
+    (near_x, here_x, there_x), (near_y, here_y, there_y) = along
     return [
-        (jnp.where(near_x > 0, there_x * count_gy + here_y, -1.0), out_x, in_y),
-        (jnp.where(near_y > 0, here_x * count_gy + there_y, -1.0), in_x, out_y),
-        (jnp.where(near_x * near_y > 0, there_x * count_gy + there_y, -1.0), out_x, out_y),
+        jnp.where(near_x > 0, there_x * count_gy + here_y, -1.0),
+        jnp.where(near_y > 0, here_x * count_gy + there_y, -1.0),
+        jnp.where(near_x * near_y > 0, there_x * count_gy + there_y, -1.0),
     ]
 
 
@@ -111,18 +103,20 @@
     count_gx, count_gy, width_x, width_y = grid
     devices, half = count_gx * count_gy, cap // 2
     owned = rows.shape[1]
-    slots = devices * cap
+    slots, spare = devices * cap, devices * half
     earlier = jnp.where(iota((owned, owned), 0) < iota((owned, owned), 1), 1.0, 0.0).astype(BF)
     column = iota((devices, owned), 0).astype(F32)
     octets, extras, most = [], [], []
-    for step in range(steps):
-        tiles, values = step_rows(step)
-        beside = ghosts(step, steps, *grid, tiles, values[0], values[1])
-        member = [jnp.where(column == tile, 1.0, 0.0) for tile in [tiles.astype(F32)] + [b[0] for b in beside]]
-        before = nn(jnp.concatenate(member, axis=0).astype(BF), earlier)
-        before = [before[n * devices : (n + 1) * devices] for n in range(4)]
+    given = [step_rows(step) for step in range(steps)]
+    asked = []
+    for step, (tiles, values) in enumerate(given):
+        asked.append([tiles.astype(F32)] + ghosts(step, steps, *grid, tiles, values[0], values[1]))
+    member = [[jnp.where(column == tile, 1.0, 0.0) for tile in tiles] for tiles in asked]
+    before = nn(jnp.concatenate(sum(member, []), axis=0).astype(BF), earlier)
+    before = [before[n * devices : (n + 1) * devices] for n in range(4 * steps)]
+    for step, (tiles, values) in enumerate(given):
         if turn is None:
-            rank = jnp.sum(before[0] * member[0], axis=0, keepdims=True)
+            rank = jnp.sum(before[4 * step] * member[step][0], axis=0, keepdims=True)
             slot = tiles * cap + rank.astype(jnp.int32)
             slot_ref[step : step + 1, :] = slot
             rows[...] = jnp.zeros_like(rows)
@@ -131,22 +125,37 @@
             packed = nt(jnp.concatenate(split3(rows[...]), axis=0), slot_table(slot, slots))
             packed = packed[0:16] + packed[16:32] + packed[32:48]
             octets.append((packed[0:8], packed[8:16]))
-        taken = jnp.zeros((devices, 1), F32)
-        extra = jnp.zeros((48, devices * half), F32)
-        for number, (tile, cell_x, cell_y) in enumerate(beside):
-            rank = jnp.sum((before[number + 1] + taken) * member[number + 1], axis=0, keepdims=True)
-            taken = taken + jnp.sum(member[number + 1], axis=1, keepdims=True)
+        taken = [jnp.zeros((devices, 1), F32)]
+        places = []
+        for number in range(1, 4):
+            here = member[step][number]
+            rank = jnp.sum((before[4 * step + number] + taken[-1]) * here, axis=0, keepdims=True)
+            taken.append(taken[-1] + jnp.sum(here, axis=1, keepdims=True))
             if turn is not None:
                 rank = rank - turn * half
-            fits = (tile >= 0) & (rank >= 0) & (rank < half)
-            slot = jnp.where(fits, tile * half + rank, -1.0).astype(jnp.int32)
-            rows[...] = jnp.zeros_like(rows)
-            for place, value in zip((1, 2, 3, 4, 5, 6, 7, 9, 10), [cell_x, cell_y] + values[2:]):
-                rows[place : place + 1, :] = value
-            extra = extra + nt(jnp.concatenate(split3(rows[...]), axis=0), slot_table(slot, devices * half))
+            tile = asked[step][number]
+            places.append(jnp.where((tile >= 0) & (rank >= 0) & (rank < half), tile * half + rank, -1.0).astype(jnp.int32))
+        grid_slots = iota((spare, owned), 0)
+        chosen = (grid_slots == places[0]) | (grid_slots == places[1]) | (grid_slots == places[2])
+        rows[...] = jnp.zeros_like(rows)
+        for place, value in zip((1, 2, 3, 4, 5, 6, 7, 9, 10), values):
+            rows[place : place + 1, :] = value
+        extra = nt(jnp.concatenate(split3(rows[...]), axis=0), jnp.where(chosen, 1.0, 0.0).astype(BF))
         extra = extra[0:16] + extra[16:32] + extra[32:48]
-        extras.append((extra[0:8], extra[8:16]))
-        most.append(jnp.max(taken, axis=0, keepdims=True))
+        lanes, sender = iota((devices, spare), 1), iota((devices, spare), 0)
+        ends = [
+            jnp.sum(jnp.where(lanes // half == sender, end, 0.0), axis=0, keepdims=True) for end in (taken[1], taken[2])
+        ]
+        rank = (iota((1, spare), 1) % half).astype(F32)
+        if turn is not None:
+            rank = rank + turn * half
+        in_x = (rank < ends[0]) | (rank >= ends[1])
+        in_y = rank >= ends[0]
+        first = []
+        for cell, width, moved in ((extra[1:2], width_x, in_x), (extra[2:3], width_y, in_y)):
+            first.append(cell + jnp.where(moved, jnp.where(cell * 2 < width, width * 1.0, -1.0 * width), 0.0))
+        extras.append((jnp.concatenate([extra[0:1]] + first + [extra[3:8]], axis=0), extra[8:16]))
+        most.append(jnp.max(taken[3], axis=0, keepdims=True))
     lane, row = iota((8, LANES), 1), iota((8, LANES), 0)
 
     def placed(octet, device, width, offset):
@@ -189,7 +198,7 @@
 
 
 def pack_kernel(
-    grid, steps, cap, tile_in, cell_in, frac_in, force_in, after_ref, out_ref, slot_ref,
+    grid, steps, cap, tile_in, cell_in, frac_in, force_in, out_ref, slot_ref,
     rows, tile_ref, cell_ref, frac_ref, force_ref, sems,
 ):
     copies = fetch([(tile_in, tile_ref), (cell_in, cell_ref), (frac_in, frac_ref), (force_in, force_ref)], sems)
@@ -198,7 +207,27 @@
     pack(grid, steps, cap, marker_rows(tile_ref, cell_ref, frac_ref, force_ref), out_ref, slot_ref, rows)
 
 
-def strips_kernel(f_in, x_up, x_down, near_ref, far_ref, sems):
+def columns_kernel(f_in, after_ref, up, down, far_ref, near_ref, sems):
+    width_y = f_in.shape[3]
+    copies = fetch(
+        [
+            (f_in.at[:, :, :, pl.ds(width_y - LANES, LANES)], far_ref),
+            (f_in.at[:, :, :, pl.ds(0, LANES)], near_ref),
+        ],
+        sems,
+    )
+    for copy, out, source, at in ((copies[0], up, far_ref, LANES - 2), (copies[1], down, near_ref, 0)):
+        copy.wait()
+        columns(source, out, at)
+
+
+def face_rows(members, planes):
+    first = 19 * planes
+    second = {member: first + n * planes for n, member in enumerate(members)}
+    return first, second, first + len(members) * planes
+
+
+def strips_kernel(f_in, after_ref, x_up, x_down, near_ref, far_ref, sems):
     planes, width_x = f_in.shape[1], f_in.shape[2]
     copies = fetch(
         [
@@ -207,10 +236,22 @@
         ],
         sems,
     )
-    for copy, out, source, start in ((copies[0], x_up, far_ref, 6), (copies[1], x_down, near_ref, 0)):
+    for copy, out, source, members, row, inner in (
+        (copies[0], x_up, far_ref, X_UP, 7, 6),
+        (copies[1], x_down, near_ref, X_DOWN, 0, 1),
+    ):
         copy.wait()
-        for plane in range(19 * planes):
-            out[2 * plane : 2 * plane + 2, :] = source[plane // planes, plane % planes, start : start + 2, :]
+        _, second, third = face_rows(members, planes)
+        for z in range(planes):
+            for member in range(19):
+                at = member * planes + z
+                out[at : at + 1, :] = source[member, z, row : row + 1, :]
+            for member, at in second.items():
+                out[at + z : at + z + 1, :] = source[member, z, inner : inner + 1, :]
+            density, momenta = moments([source[member, z] for member in range(19)])
+            for number, value in enumerate([density] + momenta):
+                at = third + number * planes + z
+                out[at : at + 1, :] = value[inner : inner + 1]
 
 
 def turn_kernel(grid, steps, cap, turn_ref, tile_ref, cell_ref, frac_ref, force_ref, out_ref, rows):
@@ -325,21 +366,18 @@
         force_ref[at : at + width_x, width_y:] = part_side
 
 
-def spread_kernel(cap, steps, planes, width_x, width_y, recv_ref, *outs):
-    forces, own_ref, most_ref = outs[:steps], outs[steps], outs[steps + 1]
-    half = cap // 2
-    most = jnp.float32(0)
-    for step in range(steps):
-        start = 2 * step * cap
-        first = gather(recv_ref, start, cap)
-        own_ref[8 * step : 8 * step + 8, :] = first
-        second = gather(recv_ref, start + cap, cap)
-        spread_own(first, second, planes, width_x, width_y, forces[step])
-        first = gather(recv_ref, start + cap, half)
-        second = gather(recv_ref, start + cap + half, half)
-        spread_ghosts(first, second, planes, width_x, width_y, forces[step], False)
-        most = jnp.maximum(most, jnp.max(second[3:4]))
-    most_ref[0] = most
+def spread_kernel(cap, step, planes, width_x, width_y, recv_ref, *refs):
+    force_ref, own_ref, turns_ref = refs[-3:]
+    start, half = 2 * step * cap, cap // 2
+    first = gather(recv_ref, start, cap)
+    own_ref[...] = first
+    second = gather(recv_ref, start + cap, cap)
+    spread_own(first, second, planes, width_x, width_y, force_ref)
+    first = gather(recv_ref, start + cap, half)
+    second = gather(recv_ref, start + cap + half, half)
+    spread_ghosts(first, second, planes, width_x, width_y, force_ref, False)
+    turns = (jnp.max(second[3:4]).astype(jnp.int32) + half - 1) // half
+    turns_ref[0] = jnp.maximum(turns, refs[0][0]) if step else turns
 
 
 def more_kernel(cap, steps, planes, width_x, width_y, recv_ref, *refs):
@@ -417,75 +455,76 @@
     return posts
 
 
-def columns_kernel(f_in, after_ref, up, down, far_ref, near_ref, sems):
-    planes, width_x, width_y = f_in.shape[1], f_in.shape[2], f_in.shape[3]
-    copies = fetch(
-        [
-            (f_in.at[:, :, :, pl.ds(width_y - LANES, LANES)], far_ref),
-            (f_in.at[:, :, :, pl.ds(0, LANES)], near_ref),
-        ],
-        sems,
-    )
+def columns(source, out, at):
+    planes, width_x = source.shape[1], source.shape[2]
     lane = iota((width_x, LANES), 1)
-    for copy, out, source, at in ((copies[0], up, far_ref, LANES - 2), (copies[1], down, near_ref, 0)):
-        copy.wait()
-        lines = out.shape[1] // LANES
-        totals = [jnp.zeros((width_x, LANES), F32) for _ in range(lines)]
-        for plane in range(19 * planes):
-            line, target = divmod(2 * plane, LANES)
-            block = source[plane // planes, plane % planes]
-            shift = (target - at) % LANES
-            if shift:
-                block = pltpu.roll(block, shift, 1)
-            totals[line] = jnp.where((lane == target) | (lane == target + 1), block, totals[line])
-        for line in range(lines):
-            out[:, line * LANES : (line + 1) * LANES] = totals[line]
-
-
-def corner_kernel(up, down, x_low, x_high, out_up, out_down):
+    lines = out.shape[1] // LANES
+    totals = [jnp.zeros((width_x, LANES), F32) for _ in range(lines)]
+    for plane in range(19 * planes):
+        line, target = divmod(2 * plane, LANES)
+        block = source[plane // planes, plane % planes]
+        shift = (target - at) % LANES
+        if shift:
+            block = pltpu.roll(block, shift, 1)
+        totals[line] = jnp.where((lane == target) | (lane == target + 1), block, totals[line])
+    for line in range(lines):
+        out[:, line * LANES : (line + 1) * LANES] = totals[line]
+
+
+def corner_kernel(up, down, x_low, x_high, after_0, after_1, out_up, out_down):
     width_x, width_y = up.shape[0], x_low.shape[1]
     count = x_low.shape[0]
+    pad = jnp.zeros((LANES - count, LANES), F32)
     for source, out, start, at in ((up, out_up, width_y - LANES, LANES - 2), (down, out_down, 0, 0)):
         out[0:width_x, :] = source[...]
         out[width_x:, :] = jnp.zeros((out.shape[0] - width_x, out.shape[1]), F32)
         for number, halo in enumerate((x_low, x_high)):
-            for line in range(out.shape[1] // LANES):
-                last = min(count, (line + 1) * LANES)
-                block = halo[line * LANES : last, start : start + LANES]
-                if last < (line + 1) * LANES:
-                    block = jnp.concatenate([block, jnp.zeros(((line + 1) * LANES - last, LANES), F32)], axis=0)
-                turned = jnp.transpose(block)
-                row = width_x + 2 * number
-                out[row : row + 2, line * LANES : (line + 1) * LANES] = turned[at : at + 2]
-
-
-def ring_cells(x_low, x_high, y_low, y_high, f_ref):
-    planes, tall, wide = f_ref.shape[1], f_ref.shape[2], f_ref.shape[3]
-    width_x, width_y = tall - RING, wide - SIDE
+            turned = jnp.transpose(jnp.concatenate([halo[:, start : start + LANES], pad], axis=0))
+            row = width_x + 2 * number
+            out[row : row + 2, 0:LANES] = turned[at : at + 2]
+
+
+def ring_rows(x_low, x_high, f_ref, ring_ref):
+    planes, tall = f_ref.shape[1], f_ref.shape[2]
+    for halo, members, row, inner in ((x_low, X_UP, RING - 1, RING - 2), (x_high, X_DOWN, 0, 1)):
+        _, second, third = face_rows(members, planes)
+        for z in range(planes):
+            for member in range(19):
+                places = [(row, member * planes + z)]
+                if member in second:
+                    places.append((inner, second[member] + z))
+                for line, at in places:
+                    line += tall - RING
+                    f_ref[member, z, line : line + 1, :] = halo[at : at + 1, :]
+            for number in range(4):
+                at = third + number * planes + z
+                ring_ref[number, z, inner : inner + 1, :] = halo[at : at + 1, :]
+
+
+def side_cells(y_low, y_high, f_ref, ring_ref):
+    planes, tall = f_ref.shape[1], f_ref.shape[2]
+    width_x = tall - RING
     lane = iota((width_x, LANES), 1)
     wide_lane = iota((LANES, LANES), 1)
-    for line in range(y_low.shape[1] // LANES):
-        at = slice(line * LANES, (line + 1) * LANES)
-        pad = jnp.zeros((LANES - 8, LANES), F32)
-        low = jnp.transpose(jnp.concatenate([y_low[width_x:, at], pad], axis=0))
-        high = jnp.transpose(jnp.concatenate([y_high[width_x:, at], pad], axis=0))
-        corner_low = jnp.where(wide_lane >= LANES - 2, pltpu.roll(low, LANES - 2, 1), high)
-        corner_high = jnp.where(
-            wide_lane >= LANES - 2, pltpu.roll(low, LANES - 4, 1), pltpu.roll(high, LANES - 2, 1)
-        )
-        for plane in range(line * LANES // 2, min((line + 1) * LANES // 2, 19 * planes)):
-            member, z = divmod(plane, planes)
-            here = 2 * plane - line * LANES
-            f_ref[member, z, tall - 2 : tall, 0:width_y] = x_low[2 * plane : 2 * plane + 2, :]
-            f_ref[member, z, width_x : width_x + 2, 0:width_y] = x_high[2 * plane : 2 * plane + 2, :]
-            f_ref[member, z, tall - 2 : tall, width_y:] = corner_low[here : here + 2]
-            f_ref[member, z, width_x : width_x + 2, width_y:] = corner_high[here : here + 2]
-            below, above = y_low[0:width_x, at], y_high[0:width_x, at]
-            if (LANES - 2 - here) % LANES:
-                below = pltpu.roll(below, (LANES - 2 - here) % LANES, 1)
-            if here:
-                above = pltpu.roll(above, LANES - here, 1)
-            f_ref[member, z, 0:width_x, width_y:] = jnp.where(lane >= LANES - 2, below, above)
+    pad = jnp.zeros((LANES - 8, LANES), F32)
+    low = jnp.transpose(jnp.concatenate([y_low[width_x:, 0:LANES], pad], axis=0))
+    high = jnp.transpose(jnp.concatenate([y_high[width_x:, 0:LANES], pad], axis=0))
+    near = wide_lane >= LANES - 2
+    ring_rows(
+        jnp.where(near, pltpu.roll(low, LANES - 2, 1), high),
+        jnp.where(near, pltpu.roll(low, LANES - 4, 1), pltpu.roll(high, LANES - 2, 1)),
+        f_ref,
+        ring_ref,
+    )
+    for plane in range(19 * planes):
+        line, here = divmod(2 * plane, LANES)
+        below = y_low[0:width_x, line * LANES : (line + 1) * LANES]
+        above = y_high[0:width_x, line * LANES : (line + 1) * LANES]
+        if (LANES - 2 - here) % LANES:
+            below = pltpu.roll(below, (LANES - 2 - here) % LANES, 1)
+        if here:
+            above = pltpu.roll(above, LANES - here, 1)
+        f_ref[plane // planes, plane % planes, 0:width_x, :] = jnp.where(lane >= LANES - 2, below, above)
 
 
 def shifted(block, member):
@@ -497,98 +536,142 @@
     return block
 
 
+X_UP = [i for i in range(19) if LATTICE[i][0] == 1]
+X_DOWN = [i for i in range(19) if LATTICE[i][0] == -1]
 MOVED = [i for i in range(19) if LATTICE[i][0] or LATTICE[i][1]]
 
 
+def force_at(ref, planes, tall, z, row, lanes):
+    return [ref[pl.ds(pl.multiple_of((n * planes + z) * tall + row, 8), 8), lanes] for n in range(3)]
+
+
+def for_rows(planes, width_x, body):
+    @pl.loop(0, planes * (width_x // 8))
+    def _(index):
+        row = pl.multiple_of((index % (width_x // 8)) * 8, 8)
+        body(index // (width_x // 8), row, pl.multiple_of(index * 8, 8))
+
+
+def collide_block(f_ref, ring_ref, force_ref, z, row, lanes, force_lanes):
+    planes, tall = f_ref.shape[1], f_ref.shape[2]
+    at = pl.ds(row, 8)
+    f = [f_ref[member, z, at, lanes] for member in range(19)]
+    density, momenta = moments(f)
+    if ring_ref is not None:
+        outer = (iota((8, LANES), 0) == 1) | (iota((8, LANES), 0) == RING - 2)
+        density = jnp.where(outer, ring_ref[0, z, :, lanes], density)
+        momenta = [jnp.where(outer, ring_ref[n + 1, z, :, lanes], momenta[n]) for n in range(3)]
+    force = force_at(force_ref, planes, tall, z, row, force_lanes)
+    for member, value in enumerate(collide(f, density, momenta, force)):
+        f_ref[member, z, at, lanes] = value
+
+
+def first_kernel(f_in, x_low, x_high, force_ref, f_ref, ring_ref, sems):
+    planes, width_x, width_y = f_in.shape[1], f_in.shape[2], f_in.shape[3]
+    copies = fetch([(f_in.at[:, z], f_ref.at[:, z, pl.ds(0, width_x), :]) for z in range(planes)], sems)
+    ring_rows(x_low, x_high, f_ref, ring_ref)
+
+    @pl.loop(0, planes)
+    def _(z):
+        for start in range(0, width_y, LANES):
+            lanes = pl.ds(start, LANES)
+            collide_block(f_ref, ring_ref, force_ref, z, width_x, lanes, lanes)
+
+    for z in range(planes):
+        copies[z].wait()
+
+        @pl.loop(0, width_x // 8)
+        def _(index):
+            row = pl.multiple_of(index * 8, 8)
+            for start in range(0, width_y, LANES):
+                lanes = pl.ds(start, LANES)
+                collide_block(f_ref, None, force_ref, z, row, lanes, lanes)
+
+
 def main_kernel(
-    cap, steps, f_in, x_low, x_high, y_low, y_high, force_0, force_1, own_ref, out_ref, back_ref,
-    before, after, probe_0, probe_1, rows, sems,
+    cap, steps, before, y_low, y_high, force_0, force_1, own_0, own_1, out_hbm, back_ref,
+    side, after, ring_ref, probe_0, probe_1, rows, out_ref, sems,
 ):
-    planes, width_x, width_y = f_in.shape[1], f_in.shape[2], f_in.shape[3]
-    tall, wide = before.shape[2], before.shape[3]
-    copies = fetch(
-        [
-            (f_in.at[:, z], before.at[:, z, pl.ds(0, width_x), pl.ds(0, width_y)])
-            for z in range(planes)
-        ],
-        sems,
-    )
-    ring_cells(x_low, x_high, y_low, y_high, before)
-
-    def blocks(body, own_body):
-        @pl.loop(0, planes * (width_x // 8))
-        def _(index):
-            z = index // (width_x // 8)
-            row = pl.multiple_of((index % (width_x // 8)) * 8, 8)
-            for start in range(0, width_y, LANES):
-                own_body(z, row, pl.ds(start, LANES), pl.multiple_of(index * 8, 8))
-            body(z, row, pl.ds(width_y, LANES))
-
-        @pl.loop(0, planes)
-        def _(z):
-            for start in range(0, wide, LANES):
-                body(z, width_x, pl.ds(start, LANES))
-
-    def force_at(ref, z, row, lanes):
-        return [ref[pl.ds(pl.multiple_of((n * planes + z) * tall + row, 8), 8), lanes] for n in range(3)]
-
-    def first_body(z, row, lanes, flat=None):
-        at = pl.ds(row, 8)
-        f = [before[member, z, at, lanes] for member in range(19)]
-        density, momenta = moments(f)
-        for member, value in enumerate(collide(f, density, momenta, force_at(force_0, z, row, lanes))):
-            before[member, z, at, lanes] = value
-
-    for copy in copies:
-        copy.wait()
-    blocks(first_body, first_body)
+    planes, tall, width_y = before.shape[1], before.shape[2], before.shape[3]
+    width_x, wide = tall - RING, after.shape[3]
+    side_cells(y_low, y_high, side, ring_ref)
+    far, all_lanes = pl.ds(width_y, LANES), pl.ds(0, LANES)
+
+    def side_body(z, row, flat):
+        collide_block(side, None, force_0, z, row, all_lanes, far)
+
+    for_rows(planes, width_x, side_body)
+
+    @pl.loop(0, planes)
+    def _(z):
+        collide_block(side, ring_ref, force_0, z, width_x, all_lanes, far)
+
     for member in MOVED:
         for z in range(planes):
-            after[member, (z + LATTICE[member][2]) % planes] = shifted(before[member, z], member)
-
-    def second_body(z, row, lanes, flat=None):
-        at = pl.ds(row, 8)
+            block = jnp.concatenate([before[member, z], side[member, z]], axis=1)
+            after[member, (z + LATTICE[member][2]) % planes] = shifted(block, member)
+
+    def second_block(z, row, start, flat=None, kept=range(19)):
+        at, lanes = pl.ds(row, 8), pl.ds(start, LANES)
         f = []
         for member in range(19):
             if member in MOVED:
                 f.append(after[member, z, at, lanes])
-            else:
-                f.append(before[member, lax.rem(z - LATTICE[member][2] + planes, planes), at, lanes])
+                continue
+            other = lax.rem(z - LATTICE[member][2] + planes, planes)
+            f.append(before[member, other, at, lanes] if start < width_y else side[member, other, at, all_lanes])
         density, momenta = moments(f)
         if flat is not None:
             inverse = 1.0 / density
-            for number, force in enumerate(force_at(force_0, z, row, lanes)):
+            for number, force in enumerate(force_at(force_0, planes, tall, z, row, lanes)):
                 probe_0[pl.ds(pl.multiple_of(number * planes * width_x + flat, 8), 8), lanes] = (
                     momenta[number] + 0.5 * force
                 ) * inverse
-        for member, value in enumerate(collide(f, density, momenta, force_at(force_1, z, row, lanes))):
-            after[member, z, at, lanes] = value
-
-    blocks(second_body, second_body)
+        values = collide(f, density, momenta, force_at(force_1, planes, tall, z, row, lanes))
+        for member in kept:
+            after[member, z, at, lanes] = values[member]
+
+    def second_body(z, row, flat):
+        for start in range(0, width_y, LANES):
+            second_block(z, row, start, flat)
+        second_block(z, row, width_y, kept=[i for i in range(19) if LATTICE[i][1]])
+
+    for_rows(planes, width_x, second_body)
+
+    @pl.loop(0, planes)
+    def _(z):
+        for start in range(0, wide, LANES):
+            second_block(z, width_x, start, kept=[i for i in range(19) if LATTICE[i][0]])
+
+    def sample_step(step, own_ref, probe_ref):
+        for number, row in enumerate(sample(own_ref[...], planes, width_x, width_y, probe_ref)):
+            rows[steps * number + step : steps * number + step + 1, :] = row
+
+    sample_step(0, own_0, probe_0)
+    copies = []
     for member in range(19):
         for z in range(planes):
             to = (z + LATTICE[member][2]) % planes
             out_ref[member, to] = shifted(after[member, z], member)[0:width_x, 0:width_y]
-
-    @pl.loop(0, planes * (width_x // 8))
-    def _(index):
-        z = index // (width_x // 8)
-        row = pl.multiple_of((index % (width_x // 8)) * 8, 8)
-        flat = pl.multiple_of(index * 8, 8)
+        copies.append(pltpu.make_async_copy(out_ref.at[member], out_hbm.at[member], sems.at[member]))
+        copies[-1].start()
+
+    def last_body(z, row, flat):
         for start in range(0, width_y, LANES):
             lanes = pl.ds(start, LANES)
             density, momenta = moments([out_ref[member, z, pl.ds(row, 8), lanes] for member in range(19)])
             inverse = 1.0 / density
-            for number, force in enumerate(force_at(force_1, z, row, lanes)):
+            for number, force in enumerate(force_at(force_1, planes, tall, z, row, lanes)):
                 probe_1[pl.ds(pl.multiple_of(number * planes * width_x + flat, 8), 8), lanes] = (
                     momenta[number] + 0.5 * force
                 ) * inverse
 
-    for step, probe_ref in enumerate((probe_0, probe_1)):
-        first = own_ref[8 * step : 8 * step + 8, :]
-        for number, row in enumerate(sample(first, planes, width_x, width_y, probe_ref)):
-            rows[steps * number + step : steps * number + step + 1, :] = row
+    for_rows(planes, width_x, last_body)
+
+    sample_step(1, own_1, probe_1)
     send_back(cap, rows, back_ref)
+    for copy in copies:
+        copy.wait()
 
 
 def send_back(cap, rows, out_ref):
@@ -607,18 +690,26 @@
         out_ref[device] = total
 
 
-def call(kernel, outs, scratch=(), flops=0, moved=0, limit=40, fetched=(False,)):
+def call(kernel, outs, scratch=(), flops=0, moved=0, limit=24, fetched=(False,), stored=None):
     shapes = [jax.ShapeDtypeStruct(shape, kind) for shape, kind in outs]
     out_specs = [pl.BlockSpec(memory_space=pltpu.SMEM if len(shape) == 1 else pltpu.VMEM) for shape, _ in outs]
-    specs = [pl.BlockSpec(memory_space=pltpu.HBM if own else pltpu.VMEM) for own in fetched]
-    return pl.pallas_call(
+    if stored:
+        out_specs = [pl.BlockSpec(memory_space=pltpu.HBM if own else pltpu.VMEM) for own in stored]
+    places = {True: pltpu.HBM, False: pltpu.VMEM, None: pltpu.SMEM}
+    specs = [pl.BlockSpec(memory_space=places[own]) for own in fetched]
+    made = pl.pallas_call(
         kernel,
         out_shape=shapes,
         out_specs=out_specs,
         scratch_shapes=list(scratch),
-        **({"in_specs": specs} if any(fetched) else {}),
+        **({"in_specs": specs} if fetched != (False,) else {}),
         cost_estimate=pl.CostEstimate(flops=flops, bytes_accessed=moved, transcendentals=0),
         compiler_params=pltpu.CompilerParams(vmem_limit_bytes=limit * 1024 * 1024),
+    )
+    if not any(fetched):
+        return made
+    return lambda *args: made(
+        *[pltpu.with_memory_space_constraint(x, pltpu.HBM) if own else x for x, own in zip(args, fetched)]
     )
 
 
@@ -654,19 +745,8 @@
     def pack_markers(*refs):
         pack_kernel(grid, steps, cap, *refs)
 
-    lines = 2 * 19 * planes
-    face = ((lines, width_y), F32)
-    x_up, x_down = call(
-        strips_kernel,
-        [face, face],
-        [
-            pltpu.VMEM((19, planes, 8, width_y), F32),
-            pltpu.VMEM((19, planes, 8, width_y), F32),
-            pltpu.SemaphoreType.DMA((2,)),
-        ],
-        fetched=(True,),
-        limit=63,
-    )(populations_in)
+    face = (((19 + len(X_UP) + 4) * planes, width_y), F32)
+    packed = -(-2 * 19 * planes // LANES) * LANES
     outgoing, slot = call(
         pack_markers,
         [message, ((steps, owned), jnp.int32)],
@@ -678,13 +758,18 @@
             pltpu.VMEM((3, steps, owned), F32),
             pltpu.SemaphoreType.DMA((4,)),
         ],
-        fetched=(True,) * 5,
-        limit=63,
-    )(*markers, x_up)
-    arrived = send(outgoing)
-
-    x_low, x_high = pair(x_up, x_down, "gx")
-    packed = -(-lines // LANES) * LANES
+        fetched=(True,) * 4,
+    )(*markers)
+    x_up, x_down = call(
+        strips_kernel,
+        [face, face],
+        [
+            pltpu.VMEM((19, planes, 8, width_y), F32),
+            pltpu.VMEM((19, planes, 8, width_y), F32),
+            pltpu.SemaphoreType.DMA((2,)),
+        ],
+        fetched=(True, False),
+    )(populations_in, slot)
     y_up, y_down = call(
         columns_kernel,
         [((width_x, packed), F32)] * 2,
@@ -693,24 +778,29 @@
             pltpu.VMEM((19, planes, width_x, LANES), F32),
             pltpu.SemaphoreType.DMA((2,)),
         ],
-        fetched=(True,) * 2,
-        limit=63,
-    )(populations_in, slot)
-    y_up, y_down = call(corner_kernel, [((width_x + 8, packed), F32)] * 2)(y_up, y_down, x_low, x_high)
+        fetched=(True, False),
+    )(populations_in, x_up)
+    arrived = send(outgoing)
+
+    x_low, x_high = pair(x_up, x_down, "gx")
+    field = ((3 * planes * tall, wide), F32)
+    parts = []
+    for step in range(steps):
+
+        def spread_markers(*refs, step=step):
+            spread_kernel(cap, step, planes, width_x, width_y, *refs)
+
+        outs = [field, ((8, slots), F32), ((1,), jnp.int32)]
+        scalars = (False, None)[: step + 1]
+        parts.append(call(spread_markers, outs, fetched=scalars)(arrived, *[part[2] for part in parts[-1:]]))
+    (force_0, own_0, _), (force_1, own_1, turns) = parts
+    turns = turns.reshape(())
+
+    y_up, y_down = call(corner_kernel, [((width_x + 8, packed), F32)] * 2)(y_up, y_down, x_low, x_high, own_0, own_1)
     y_low, y_high = pair(y_up, y_down, "gy")
 
-    field = ((3 * planes * tall, wide), F32)
-
-    def spread_markers(*refs):
-        spread_kernel(cap, steps, planes, width_x, width_y, *refs)
-
-    *forces, own, most = call(
-        spread_markers, [field] * steps + [((8 * steps, slots), F32), ((1,), F32)], flops=4 * 10**9, moved=10**6
-    )(arrived)
-    most = most.reshape(())
-
     def again(state):
-        return (state[0] * half).astype(F32) < most
+        return state[0] < turns
 
     def more(state):
         turn, *forces = state
@@ -727,24 +817,38 @@
             out_shape=[jax.ShapeDtypeStruct(*message)],
             in_specs=spec,
             scratch_shapes=[rows],
-            compiler_params=pltpu.CompilerParams(vmem_limit_bytes=40 * 1024 * 1024),
+            compiler_params=pltpu.CompilerParams(vmem_limit_bytes=24 * 1024 * 1024),
         )(turn.reshape(1), *markers)
         return (turn + 1, *call(add_markers, [field] * steps)(send(outgoing), *forces))
 
-    _, force_0, force_1 = lax.while_loop(again, more, (jnp.int32(1), *forces))
+    _, force_0, force_1 = lax.while_loop(again, more, (jnp.int32(1), force_0, force_1))
+
+    (before,) = call(
+        first_kernel,
+        [((19, planes, tall, width_y), F32)],
+        [pltpu.VMEM((4, planes, RING, width_y), F32), pltpu.SemaphoreType.DMA((planes,))],
+        fetched=(True,) + (False,) * 3,
+    )(populations_in, x_low, x_high, force_0)
 
     def main(*refs):
         main_kernel(cap, steps, *refs)
 
     own_field = pltpu.VMEM((3 * planes * width_x, width_y), F32)
-    extended = pltpu.VMEM((19, planes, tall, wide), F32)
     fields, back = call(
         main,
         [(populations_in.shape, F32), ((devices, steps, LANES), F32)],
-        [extended, extended, own_field, own_field, pltpu.VMEM((8, slots), F32), pltpu.SemaphoreType.DMA((planes,))],
-        fetched=(True,) + (False,) * 7,
-        limit=50,
-    )(populations_in, x_low, x_high, y_low, y_high, force_0, force_1, own)
+        [
+            pltpu.VMEM((19, planes, tall, LANES), F32),
+            pltpu.VMEM((19, planes, tall, wide), F32),
+            pltpu.VMEM((4, planes, RING, LANES), F32),
+            own_field,
+            own_field,
+            pltpu.VMEM((8, slots), F32),
+            pltpu.VMEM(populations_in.shape, F32),
+            pltpu.SemaphoreType.DMA((19,)),
+        ],
+        stored=(True, False),
+    )(before, y_low, y_high, force_0, force_1, own_0, own_1)
     returned = send(back)
 
     def unpack(*refs):

time: 65.4 us -> 58.1 us (0.89)
  waiting for transfers between devices: 10.4 us -> 0.79 us
  blocking collectives: 8.97 us -> 11.4 us
  local copies, waits for them, and re-layouts: 1.54 us -> 0.03 us
  Pallas kernels: 28.8 us -> 30.2 us
    ppermute x4, waiting for transfers between devices: 10.4 us -> 0.01 us  [pair(): return (lax.ppermute(up, axis, forward), lax.ppermute(down, axis, backward))]
    pallas_call x4 -> x6, Pallas kernels: 13.5 us -> 18.6 us  [the longest x4 11.4 us: call(): made(*[pltpu.with_memory_space_constraint(x, pltpu.HBM) if own else x for...]
    pallas_call x1, Pallas kernels: 13.9 us -> 10.2 us  [local(): call(main, [(populations_in.shape, F32), ((devices, steps, LANES), F32)],...]
    all_to_all x1, blocking collectives: 8.97 us -> 11.4 us  [send(): lax.all_to_all(outgoing, ('gx', 'gy'), split_axis=0, concat_axis=0, tiled...]
    unnamed x14 -> x10, local copies, waits for them, and re-layouts: 1.54 us -> 0.03 us
    all_to_all x1, waiting for transfers between devices: 0.01 us -> 0.78 us  [send(): lax.all_to_all(outgoing, ('gx', 'gy'), split_axis=0, concat_axis=0, tiled...]
  transfers between devices with their start and end apart: 5 -> 5, of which waited for: 2 -> 1; matrix products, arithmetic and copies ran while one was open for 0% -> 0% of each run, Pallas kernels for 13% -> 26%
where the time goes in v4:
time: 58.1 us; the launch traced here: 57.7 us
  Pallas kernels  30.2 us (52%)
  starting transfers between devices  13.7 us (24%)
  blocking collectives  11.4 us (20%)
  loops' own time  0.81 us (1%)
  between operations  0.8 us (1%)
  waiting for transfers between devices  0.79 us (1%)
    all_to_all x1, blocking collectives, send(): lax.all_to_all(outgoing, ('gx', 'gy'), split_axis=0, concat_axis=0, tiled...  11.4 us
    pallas_call x4, Pallas kernels, call(): made(*[pltpu.with_memory_space_constraint(x, pltpu.HBM) if own else x for...  11.4 us
    pallas_call x1, Pallas kernels, local(): call(main, [(populations_in.shape, F32), ((devices, steps, LANES), F32)],...  10.2 us
    all_to_all x1, starting transfers between devices, send(): lax.all_to_all(outgoing, ('gx', 'gy'), split_axis=0, concat_axis=0, tiled...  7.3 us
    pallas_call x2, Pallas kernels, local(): call(spread_markers, outs, fetched=scalars)  7.23 us
    ppermute x4, starting transfers between devices, pair(): return (lax.ppermute(up, axis, forward), lax.ppermute(down, axis, backward))  6.37 us
    pallas_call x1, Pallas kernels, local(): velocity, = call(unpack, [((3, steps, owned), F32)])(returned, slot)  1.23 us
  transfers between devices with their start and end apart: 5, of which 1 were waited for; matrix products, arithmetic and copies ran while one was open for 0% of the time, Pallas kernels for 26%

profile of v4, /device:TPU:0, one launch (start us, length us, event | category | flops | bytes accessed | tf_op | source)
XLA Modules:
  0.0 57.7 jit_solution(4672442957480470860)
XLA Ops:
  0.6 3.5 %shard_map.68 = (f32[32,8,128]{2,1,0:T(8,128)}, s32[2,512]{1,0:T(2,128)S(1)}) custom-call(s32[8,128]{1,0:T(8,128)} %bitcast.15, s32[3,2,512]{2,1,0:T(2,128)} %bitcast.9, f32[3,2,512]{2,1,0:T(2,128)} %bitcast.11, f32[3,2,512]{2,1,0:T(2,128)} %bitcast.13), custom_call_target="tpu_custom_call" | custom-call | tf_op jit(solution)/shard_map/pallas_call | solution.py:711
  4.1 7.3 %all-to-all-start.1 = ((f32[32,8,128]{2,1,0:T(8,128)}), f32[32,8,128]{2,1,0:T(8,128)S(1)}, u32[]{:S(2)}, u32[]{:S(2)}) async-start(f32[32,8,128]{2,1,0:T(8,128)} %get-tuple-element.67), calls=%async_computation.1 | async-start | bytes 262144 | tf_op jit(solution)/shard_map/all_to_all | solution.py:743
  11.4 0.0 copy-start.1
  11.5 0.0 copy-start.2
  11.5 0.0 copy-start.3
  11.5 0.0 copy-start.4
  11.5 1.6 %shard_map.69 = (f32[112,384]{1,0:T(8,128)S(1)}, f32[112,384]{1,0:T(8,128)S(1)}) custom-call(f32[19,4,32,384]{3,2,1,0:T(8,128)} %f_in.5, s32[2,512]{1,0:T(2,128)S(1)} %get-tuple-element.64.after_ref.refs_1_), custom_call_target="tpu_custom_call" | custom-call | tf_op jit(solution)/shard_map/pallas_call | solution.py:711
  13.1 3.7 %collective-permute-start.1 = (f32[112,384]{1,0:T(8,128)S(1)}, f32[112,384]{1,0:T(8,128)S(1)}, u32[]{:S(2)}, u32[]{:S(2)}) collective-permute-start(f32[112,384]{1,0:T(8,128)S(1)} %get-tuple-element.66), channel_id=1, source_target_pairs={{8,0},{16,8},{24,16},{0,24},{9,1},{17,9},{25,17},{1,25},{10,2},{18... | collective-permute-start | bytes 516104 | tf_op jit(solution)/shard_map/ppermute | solution.py:720
  16.8 0.0 collective-permute-start
  16.8 2.1 %shard_map.73 = (f32[32,256]{1,0:T(8,128)S(1)}, f32[32,256]{1,0:T(8,128)S(1)}) custom-call(f32[19,4,32,384]{3,2,1,0:T(8,128)} %f_in.5, f32[112,384]{1,0:T(8,128)S(1)} %get-tuple-element.65.after_ref), custom_call_target="tpu_custom_call" | custom-call | tf_op jit(solution)/shard_map/pallas_call | solution.py:711
  18.9 0.8 %all-to-all-done.1.refs_0_ = f32[32,8,128]{2,1,0:T(8,128)S(1)} async-done(((f32[32,8,128]{2,1,0:T(8,128)}), f32[32,8,128]{2,1,0:T(8,128)S(1)}, u32[]{:S(2)}, u32[]{:S(2)}) %all-to-all-start.1) | async-done | bytes 131104 | tf_op jit(solution)/shard_map/all_to_all | solution.py:743
  19.7 3.3 %shard_map.70 = (f32[480,512]{1,0:T(8,128)}, f32[8,1024]{1,0:T(8,128)S(1)}, s32[1]{0:T(128)}) custom-call(f32[32,8,128]{2,1,0:T(8,128)S(1)} %all-to-all-done.1.refs_0_), custom_call_target="tpu_custom_call" | custom-call | tf_op jit(solution)/shard_map/pallas_call | solution.py:795
  23.0 3.9 %shard_map.71 = (f32[480,512]{1,0:T(8,128)}, f32[8,1024]{1,0:T(8,128)S(1)}, s32[1]{0:T(128)}) custom-call(f32[32,8,128]{2,1,0:T(8,128)S(1)} %all-to-all-done.1.refs_0_, s32[1]{0:T(128)} %get-tuple-element.69.refs_1_), custom_call_target="tpu_custom_call" | custom-call | tf_op jit(solution)/shard_map/pallas_call | solution.py:795
  26.9 0.0 collective-permute-done.1.x_high
  26.9 0.0 collective-permute-done.x_low
  27.0 0.1 shard_map.74
  27.1 0.4 collective-permute-start.2
  27.5 2.3 %collective-permute-start.3 = (f32[40,256]{1,0:T(8,128)S(1)}, f32[40,256]{1,0:T(8,128)S(1)}, u32[]{:S(2)}, u32[]{:S(2)}) collective-permute-start(f32[40,256]{1,0:T(8,128)S(1)} %get-tuple-element.78), channel_id=1, source_target_pairs={{1,0},{2,1},{3,2},{4,3},{5,4},{6,5},{7,6},{0,7},{9,8},{10,9},{11,1... | collective-permute-start | bytes 122888 | tf_op jit(solution)/shard_map/ppermute | solution.py:720
  29.8 0.0 copy-done.1
  29.8 0.0 copy-done.2
  29.8 0.0 copy-done.3
  29.8 0.0 copy-done.4
  29.8 0.8 %while.12 = (s32[]{:T(128)}, f32[480,512]{1,0:T(8,128)}, f32[480,512]{1,0:T(8,128)}, s32[]{:T(128)}, s32[8,128]{1,0:T(8,128)S(1)}, /*index=5*/s32[3,2,512]{2,1,0...) while((s32[]{:T(128)}, f32[480,512]{1,0:T(8,128)}, f32[480,512]{1,0:T(8,128)}, ...), condition=%wide.region_1.0_spmd, body=%wide.region_0.0_spmd.sunk | while | flops 2 | bytes 4325501 | solution.py:824
  30.6 0.0 copy-start
  30.6 4.1 %shard_map.72.refs_0_ = f32[19,4,40,384]{3,2,1,0:T(8,128)S(1)} custom-call(f32[19,4,32,384]{3,2,1,0:T(8,128)} %f_in.5, f32[112,384]{1,0:T(8,128)S(1)} %collective-permute-done.x_low, f32[112,384]{1,0:T(8,128)S(1)} %collective-permute-done.1.x_high, f32[480,512]{1,0:T(8,128)} %get-tuple-element.72.force_ref.refs_3_), custom_call_target="tpu_custom_call" | custom-call | tf_op jit(solution)/shard_map/pallas_call | solution.py:711
  34.7 0.0 collective-permute-done.2.refs_1_
  34.8 0.0 collective-permute-done.3.refs_2_
  34.8 0.0 copy-done
  34.8 10.2 %shard_map.75 = (f32[19,4,32,384]{3,2,1,0:T(8,128)}, f32[32,2,128]{2,1,0:T(2,128)S(1)}) custom-call(f32[19,4,40,384]{3,2,1,0:T(8,128)S(1)} %shard_map.72.refs_0_, f32[40,256]{1,0:T(8,128)S(1)} %collective-permute-done.2.refs_1_, f32[40,256]{1,0:T(8,128)S(1)} %collective-permute-done.3.refs_2_, f32[480,512]{1,0:T(8,128)S(1)} %copy-done, ...), custom_call_target="tpu_custom_call" | custom-call | tf_op jit(solution)/shard_map/pallas_call | solution.py:837
  45.0 11.4 %all_to_all.16.refs_0_ = f32[32,2,128]{2,1,0:T(2,128)S(1)} all-to-all(f32[32,2,128]{2,1,0:T(2,128)S(1)} %get-tuple-element.81), channel_id=1, replica_groups=mesh['gx'=4,'gy'=8] {'gx','gy'}, dimensions={0} | all-to-all | bytes 65536 | tf_op jit(solution)/shard_map/all_to_all | solution.py:743
  56.4 1.2 %shard_map.76 = f32[3,2,512]{2,1,0:T(2,128)} custom-call(f32[32,2,128]{2,1,0:T(2,128)S(1)} %all_to_all.16.refs_0_, s32[2,512]{1,0:T(2,128)S(1)} %get-tuple-element.64.after_ref.refs_1_), custom_call_target="tpu_custom_call" | custom-call | tf_op jit(solution)/shard_map/pallas_call | solution.py:857
Async XLA Ops:
  4.1 15.5 %all-to-all-start.1 = ((f32[32,8,128]{2,1,0:T(8,128)}), f32[32,8,128]{2,1,0:T(8,128)S(1)}, u32[]{:S(2)}, u32[]{:S(2)}) async-start(f32[32,8,128]{2,1,0:T(8,128)} %get-tuple-element.67), calls=%async_computation.1 | async-start | bytes 262144 | tf_op jit(solution)/shard_map/all_to_all | solution.py:743
  11.4 18.3 %copy-start.1 = (s32[2,3,512]{2,0,1:T(2,128)S(1)}, s32[2,3,512]{2,0,1:T(2,128)}, u32[]{:S(2)}) copy-start(s32[2,3,512]{2,0,1:T(2,128)} %param.10) | copy-start | bytes 36868
  11.5 18.3 %copy-start.2 = (f32[2,3,512]{2,0,1:T(2,128)S(1)}, f32[2,3,512]{2,0,1:T(2,128)}, u32[]{:S(2)}) copy-start(f32[2,3,512]{2,0,1:T(2,128)} %param.9) | copy-start | bytes 36868
  11.5 18.3 %copy-start.3 = (f32[2,3,512]{2,0,1:T(2,128)S(1)}, f32[2,3,512]{2,0,1:T(2,128)}, u32[]{:S(2)}) copy-start(f32[2,3,512]{2,0,1:T(2,128)} %param.8) | copy-start | bytes 36868
  11.5 18.3 %copy-start.4 = (s32[2,512,1]{1,2,0:T(1,128)S(1)}, s32[2,512,1]{1,2,0:T(1,128)}, u32[]{:S(2)}) copy-start(s32[2,512,1]{1,2,0:T(1,128)} %param.11) | copy-start | bytes 12292
  13.1 13.8 %collective-permute-start.1 = (f32[112,384]{1,0:T(8,128)S(1)}, f32[112,384]{1,0:T(8,128)S(1)}, u32[]{:S(2)}, u32[]{:S(2)}) collective-permute-start(f32[112,384]{1,0:T(8,128)S(1)} %get-tuple-element.66), channel_id=1, source_target_pairs={{8,0},{16,8},{24,16},{0,24},{9,1},{17,9},{25,17},{1,25},{10,2},{18... | collective-permute-start | bytes 516104 | tf_op jit(solution)/shard_map/ppermute | solution.py:720
  16.8 10.2 %collective-permute-start = (f32[112,384]{1,0:T(8,128)S(1)}, f32[112,384]{1,0:T(8,128)S(1)}, u32[]{:S(2)}, u32[]{:S(2)}) collective-permute-start(f32[112,384]{1,0:T(8,128)S(1)} %get-tuple-element.65.after_ref), channel_id=1, source_target_pairs={{0,8},{8,16},{16,24},{24,0},{1,9},{9,17},{17,25},{25,1},{2,10},{10... | collective-permute-start | bytes 516104 | tf_op jit(solution)/shard_map/ppermute | solution.py:720
  27.1 7.7 %collective-permute-start.2 = (f32[40,256]{1,0:T(8,128)S(1)}, f32[40,256]{1,0:T(8,128)S(1)}, u32[]{:S(2)}, u32[]{:S(2)}) collective-permute-start(f32[40,256]{1,0:T(8,128)S(1)} %get-tuple-element.77), channel_id=1, source_target_pairs={{0,1},{1,2},{2,3},{3,4},{4,5},{5,6},{6,7},{7,0},{8,9},{9,10},{10,1... | collective-permute-start | bytes 122888 | tf_op jit(solution)/shard_map/ppermute | solution.py:720
  27.5 7.3 %collective-permute-start.3 = (f32[40,256]{1,0:T(8,128)S(1)}, f32[40,256]{1,0:T(8,128)S(1)}, u32[]{:S(2)}, u32[]{:S(2)}) collective-permute-start(f32[40,256]{1,0:T(8,128)S(1)} %get-tuple-element.78), channel_id=1, source_target_pairs={{1,0},{2,1},{3,2},{4,3},{5,4},{6,5},{7,6},{0,7},{9,8},{10,9},{11,1... | collective-permute-start | bytes 122888 | tf_op jit(solution)/shard_map/ppermute | solution.py:720
  30.6 4.2 %copy-start = (f32[480,512]{1,0:T(8,128)S(1)}, f32[480,512]{1,0:T(8,128)}, u32[]{:S(2)}) copy-start(f32[480,512]{1,0:T(8,128)} %get-tuple-element.72.force_ref.refs_3_) | copy-start | bytes 2949124

commit v5 on v4

--- a/solution.py
+++ b/solution.py
@@ -366,18 +366,21 @@
         force_ref[at : at + width_x, width_y:] = part_side
 
 
-def spread_kernel(cap, step, planes, width_x, width_y, recv_ref, *refs):
-    force_ref, own_ref, turns_ref = refs[-3:]
-    start, half = 2 * step * cap, cap // 2
-    first = gather(recv_ref, start, cap)
-    own_ref[...] = first
-    second = gather(recv_ref, start + cap, cap)
-    spread_own(first, second, planes, width_x, width_y, force_ref)
-    first = gather(recv_ref, start + cap, half)
-    second = gather(recv_ref, start + cap + half, half)
-    spread_ghosts(first, second, planes, width_x, width_y, force_ref, False)
-    turns = (jnp.max(second[3:4]).astype(jnp.int32) + half - 1) // half
-    turns_ref[0] = jnp.maximum(turns, refs[0][0]) if step else turns
+def spread_kernel(cap, steps, planes, width_x, width_y, recv_ref, *refs):
+    forces, owns, turns_ref = refs[:steps], refs[steps : 2 * steps], refs[2 * steps]
+    half = cap // 2
+    most = jnp.zeros((1, recv_ref.shape[0] * half), F32)
+    for step in range(steps):
+        start = 2 * step * cap
+        first = gather(recv_ref, start, cap)
+        owns[step][...] = first
+        second = gather(recv_ref, start + cap, cap)
+        spread_own(first, second, planes, width_x, width_y, forces[step])
+        first = gather(recv_ref, start + cap, half)
+        second = gather(recv_ref, start + cap + half, half)
+        spread_ghosts(first, second, planes, width_x, width_y, forces[step], False)
+        most = jnp.maximum(most, second[3:4])
+    turns_ref[0] = (jnp.max(most).astype(jnp.int32) + half - 1) // half
 
 
 def more_kernel(cap, steps, planes, width_x, width_y, recv_ref, *refs):
@@ -720,7 +723,7 @@
     return lax.ppermute(up, axis, forward), lax.ppermute(down, axis, backward)
 
 
-def local(populations_in, marker_force, marker_frac, marker_cell, marker_tile):
+def run(rounds, populations_in, marker_force, marker_frac, marker_cell, marker_tile):
     count_gx, count_gy = lax.axis_size("gx"), lax.axis_size("gy")
     devices = count_gx * count_gy
     steps, owned = marker_force.shape[0], marker_force.shape[2]
@@ -784,16 +787,13 @@
 
     x_low, x_high = pair(x_up, x_down, "gx")
     field = ((3 * planes * tall, wide), F32)
-    parts = []
-    for step in range(steps):
-
-        def spread_markers(*refs, step=step):
-            spread_kernel(cap, step, planes, width_x, width_y, *refs)
-
-        outs = [field, ((8, slots), F32), ((1,), jnp.int32)]
-        scalars = (False, None)[: step + 1]
-        parts.append(call(spread_markers, outs, fetched=scalars)(arrived, *[part[2] for part in parts[-1:]]))
-    (force_0, own_0, _), (force_1, own_1, turns) = parts
+
+    def spread_markers(*refs):
+        spread_kernel(cap, steps, planes, width_x, width_y, *refs)
+
+    force_0, force_1, own_0, own_1, turns = call(
+        spread_markers, [field] * steps + [((8, slots), F32)] * steps + [((1,), jnp.int32)]
+    )(arrived)
     turns = turns.reshape(())
 
     y_up, y_down = call(corner_kernel, [((width_x + 8, packed), F32)] * 2)(y_up, y_down, x_low, x_high, own_0, own_1)
@@ -821,7 +821,8 @@
         )(turn.reshape(1), *markers)
         return (turn + 1, *call(add_markers, [field] * steps)(send(outgoing), *forces))
 
-    _, force_0, force_1 = lax.while_loop(again, more, (jnp.int32(1), force_0, force_1))
+    if rounds:
+        _, force_0, force_1 = lax.while_loop(again, more, (jnp.int32(1), force_0, force_1))
 
     (before,) = call(
         first_kernel,
@@ -855,7 +856,19 @@
         unpack_kernel(cap, steps, *refs)
 
     (velocity,) = call(unpack, [((3, steps, owned), F32)])(returned, slot)
-    return fields, by_comp(velocity)
+    return fields, by_comp(velocity), turns
+
+
+def local(*inputs):
+    def again(state):
+        return state[2] > 1
+
+    def whole(state):
+        fields, velocity, _ = run(True, *inputs)
+        return fields, velocity, jnp.int32(0)
+
+    fields, velocity, _ = lax.while_loop(again, whole, run(False, *inputs))
+    return fields, velocity
 
 
 def solution(mesh):

time: 58.1 us -> 53.2 us (0.916)
  blocking collectives: 11.4 us -> 0 us
  waiting for transfers between devices: 0.79 us -> 8.76 us
  Pallas kernels: 30.2 us -> 25.5 us
  starting transfers between devices: 13.7 us -> 17 us
    all_to_all x1 -> x0, blocking collectives: 11.4 us -> none  [send(): lax.all_to_all(outgoing, ('gx', 'gy'), split_axis=0, concat_axis=0, tiled...]
    all_to_all x1 -> x2, waiting for transfers between devices: 0.78 us -> 7.84 us  [send(): lax.all_to_all(outgoing, ('gx', 'gy'), split_axis=0, concat_axis=0, tiled...]
    pallas_call x5 -> x4, Pallas kernels: 18.8 us -> 15.4 us  [the longest x1 9.65 us: run(): call(main, [(populations_in.shape, F32), ((devices, steps, LANES), F32)],...]
    all_to_all x1 -> x2, starting transfers between devices: 7.3 us -> 10.4 us  [send(): lax.all_to_all(outgoing, ('gx', 'gy'), split_axis=0, concat_axis=0, tiled...]
    pallas_call x4, Pallas kernels: 11.4 us -> 10.1 us  [call(): made(*[pltpu.with_memory_space_constraint(x, pltpu.HBM) if own else x for...]
    ppermute x4, waiting for transfers between devices: 0.01 us -> 0.92 us  [pair(): return (lax.ppermute(up, axis, forward), lax.ppermute(down, axis, backward))]
  transfers between devices with their start and end apart: 5 -> 6, of which waited for: 1 -> 3; matrix products, arithmetic and copies ran while one was open for 0% -> 0% of each run, Pallas kernels for 26% -> 21%
where the time goes in v5:
time: 53.2 us; the launch traced here: 52.8 us
  Pallas kernels  25.5 us (48%)
  starting transfers between devices  17 us (32%)
  waiting for transfers between devices  8.76 us (16%)
  between operations  0.94 us (2%)
  loops' own time  0.64 us (1%)
    all_to_all x2, starting transfers between devices, send(): lax.all_to_all(outgoing, ('gx', 'gy'), split_axis=0, concat_axis=0, tiled...  10.4 us
    pallas_call x4, Pallas kernels, call(): made(*[pltpu.with_memory_space_constraint(x, pltpu.HBM) if own else x for...  10.1 us
    pallas_call x1, Pallas kernels, run(): call(main, [(populations_in.shape, F32), ((devices, steps, LANES), F32)],...  9.65 us
    all_to_all x2, waiting for transfers between devices, send(): lax.all_to_all(outgoing, ('gx', 'gy'), split_axis=0, concat_axis=0, tiled...  7.84 us
    ppermute x4, starting transfers between devices, pair(): return (lax.ppermute(up, axis, forward), lax.ppermute(down, axis, backward))  6.57 us
    pallas_call x1, Pallas kernels, run(): call(spread_markers, [field] * steps + [((8, slots), F32)] * steps + [((1...  4.43 us
    pallas_call x1, Pallas kernels, run(): velocity, = call(unpack, [((3, steps, owned), F32)])(returned, slot)  1.24 us
  transfers between devices with their start and end apart: 6, of which 3 were waited for; matrix products, arithmetic and copies ran while one was open for 0% of the time, Pallas kernels for 21%

profile of v5, /device:TPU:0, one launch (start us, length us, event | category | flops | bytes accessed | tf_op | source)
XLA Modules:
  0.0 52.8 jit_solution(6219351233155949101)
XLA Ops:
  0.6 3.5 %shard_map.68 = (f32[32,8,128]{2,1,0:T(8,128)}, s32[2,512]{1,0:T(2,128)S(1)}) custom-call(s32[8,128]{1,0:T(8,128)} %bitcast.28, s32[3,2,512]{2,1,0:T(2,128)} %bitcast.16, f32[3,2,512]{2,1,0:T(2,128)} %bitcast.20, f32[3,2,512]{2,1,0:T(2,128)} %bitcast.24), custom_call_target="tpu_custom_call" | custom-call | tf_op jit(solution)/shard_map/pallas_call | solution.py:714
  4.1 7.3 %all-to-all-start.3 = ((f32[32,8,128]{2,1,0:T(8,128)}), f32[32,8,128]{2,1,0:T(8,128)S(1)}, u32[]{:S(2)}, u32[]{:S(2)}) async-start(f32[32,8,128]{2,1,0:T(8,128)} %get-tuple-element.121), calls=%async_computation.3 | async-start | bytes 262144 | tf_op jit(solution)/shard_map/all_to_all | solution.py:746
  11.4 1.6 %shard_map.69 = (f32[112,384]{1,0:T(8,128)S(1)}, f32[112,384]{1,0:T(8,128)S(1)}) custom-call(f32[19,4,32,384]{3,2,1,0:T(8,128)} %f_in.5, s32[2,512]{1,0:T(2,128)S(1)} %get-tuple-element.118.after_ref.refs_1_), custom_call_target="tpu_custom_call" | custom-call | tf_op jit(solution)/shard_map/pallas_call | solution.py:714
  13.1 1.8 %collective-permute-start.4 = (f32[112,384]{1,0:T(8,128)S(1)}, f32[112,384]{1,0:T(8,128)S(1)}, u32[]{:S(2)}, u32[]{:S(2)}) collective-permute-start(f32[112,384]{1,0:T(8,128)S(1)} %get-tuple-element.119.after_ref), channel_id=1, source_target_pairs={{0,8},{8,16},{16,24},{24,0},{1,9},{9,17},{17,25},{25,1},{2,10},{10... | collective-permute-start | bytes 516104 | tf_op jit(solution)/shard_map/ppermute | solution.py:723
  14.9 2.1 %collective-permute-start.5 = (f32[112,384]{1,0:T(8,128)S(1)}, f32[112,384]{1,0:T(8,128)S(1)}, u32[]{:S(2)}, u32[]{:S(2)}) collective-permute-start(f32[112,384]{1,0:T(8,128)S(1)} %get-tuple-element.120), channel_id=1, source_target_pairs={{8,0},{16,8},{24,16},{0,24},{9,1},{17,9},{25,17},{1,25},{10,2},{18... | collective-permute-start | bytes 516104 | tf_op jit(solution)/shard_map/ppermute | solution.py:723
  16.9 2.1 %shard_map.72 = (f32[32,256]{1,0:T(8,128)S(1)}, f32[32,256]{1,0:T(8,128)S(1)}) custom-call(f32[19,4,32,384]{3,2,1,0:T(8,128)} %f_in.5, f32[112,384]{1,0:T(8,128)S(1)} %get-tuple-element.119.after_ref), custom_call_target="tpu_custom_call" | custom-call | tf_op jit(solution)/shard_map/pallas_call | solution.py:714
  19.0 0.6 %all-to-all-done.3.refs_0_ = f32[32,8,128]{2,1,0:T(8,128)S(1)} async-done(((f32[32,8,128]{2,1,0:T(8,128)}), f32[32,8,128]{2,1,0:T(8,128)S(1)}, u32[]{:S(2)}, u32[]{:S(2)}) %all-to-all-start.3) | async-done | bytes 131104 | tf_op jit(solution)/shard_map/all_to_all | solution.py:746
  19.7 4.4 %shard_map.70 = (f32[480,512]{1,0:T(8,128)S(1)}, f32[480,512]{1,0:T(8,128)S(1)}, f32[8,1024]{1,0:T(8,128)S(1)}, f32[8,1024]{1,0:T(8,128)S(1)}, s32[1]{0:T(128)}) custom-call(f32[32,8,128]{2,1,0:T(8,128)S(1)} %all-to-all-done.3.refs_0_), custom_call_target="tpu_custom_call" | custom-call | tf_op jit(solution)/shard_map/pallas_call | solution.py:794
  24.1 0.0 collective-permute-done.4.x_low
  24.1 0.9 %collective-permute-done.5.x_high = f32[112,384]{1,0:T(8,128)S(1)} collective-permute-done((f32[112,384]{1,0:T(8,128)S(1)}, f32[112,384]{1,0:T(8,128)S(1)}, u32[]{:S(2)}, u32[]{:S(2)}) %collective-permute-start.5) | collective-permute-done | bytes 172064 | tf_op jit(solution)/shard_map/ppermute | solution.py:723
  25.0 0.1 shard_map.73
  25.1 0.1 collective-permute-start.6
  25.2 2.6 %collective-permute-start.7 = (f32[40,256]{1,0:T(8,128)S(1)}, f32[40,256]{1,0:T(8,128)S(1)}, u32[]{:S(2)}, u32[]{:S(2)}) collective-permute-start(f32[40,256]{1,0:T(8,128)S(1)} %get-tuple-element.128), channel_id=1, source_target_pairs={{1,0},{2,1},{3,2},{4,3},{5,4},{6,5},{7,6},{0,7},{9,8},{10,9},{11,1... | collective-permute-start | bytes 122888 | tf_op jit(solution)/shard_map/ppermute | solution.py:723
  27.8 2.8 %shard_map.71.refs_0_ = f32[19,4,40,384]{3,2,1,0:T(8,128)S(1)} custom-call(f32[19,4,32,384]{3,2,1,0:T(8,128)} %f_in.5, f32[112,384]{1,0:T(8,128)S(1)} %collective-permute-done.4.x_low, f32[112,384]{1,0:T(8,128)S(1)} %collective-permute-done.5.x_high, f32[480,512]{1,0:T(8,128)S(1)} %get-tuple-element.122.force_ref.refs_3_), custom_call_target="tpu_custom_call" | custom-call | tf_op jit(solution)/shard_map/pallas_call | solution.py:714
  30.7 0.0 copy-start.8
  30.7 0.0 copy-start.1
  30.7 0.0 copy-start.3
  30.7 0.0 copy-start.5
  30.7 0.0 collective-permute-done.6.refs_1_
  30.8 0.0 collective-permute-done.7.refs_2_
  30.8 9.6 %shard_map.74 = (f32[19,4,32,384]{3,2,1,0:T(8,128)}, f32[32,2,128]{2,1,0:T(2,128)}) custom-call(f32[19,4,40,384]{3,2,1,0:T(8,128)S(1)} %shard_map.71.refs_0_, f32[40,256]{1,0:T(8,128)S(1)} %collective-permute-done.6.refs_1_, f32[40,256]{1,0:T(8,128)S(1)} %collective-permute-done.7.refs_2_, f32[480,512]{1,0:T(8,128)S(1)} %get-tuple-element.122.force_ref.refs_3_, ...), custom_call_target="tpu_custom_call" | custom-call | tf_op jit(solution)/shard_map/pallas_call | solution.py:838
  40.4 3.1 %all-to-all-start.4 = ((f32[32,2,128]{2,1,0:T(2,128)}), f32[32,2,128]{2,1,0:T(2,128)S(1)}, u32[]{:S(2)}, u32[]{:S(2)}) async-start(f32[32,2,128]{2,1,0:T(2,128)} %get-tuple-element.131), calls=%async_computation.4 | async-start | bytes 65536 | tf_op jit(solution)/shard_map/all_to_all | solution.py:746
  43.6 0.0 copy-done.8
  43.6 7.2 %all-to-all-done.4.refs_0_ = f32[32,2,128]{2,1,0:T(2,128)S(1)} async-done(((f32[32,2,128]{2,1,0:T(2,128)}), f32[32,2,128]{2,1,0:T(2,128)S(1)}, u32[]{:S(2)}, u32[]{:S(2)}) %all-to-all-start.4) | async-done | bytes 32800 | tf_op jit(solution)/shard_map/all_to_all | solution.py:746
  50.8 1.2 %shard_map.75 = f32[3,2,512]{2,1,0:T(2,128)} custom-call(f32[32,2,128]{2,1,0:T(2,128)S(1)} %all-to-all-done.4.refs_0_, s32[2,512]{1,0:T(2,128)S(1)} %get-tuple-element.118.after_ref.refs_1_), custom_call_target="tpu_custom_call" | custom-call | tf_op jit(solution)/shard_map/pallas_call | solution.py:858
  52.0 0.0 copy-done.1
  52.0 0.0 copy-done.3
  52.0 0.0 copy-done.5
  52.0 0.6 %while.22 = (f32[19,4,32,384]{3,2,1,0:T(8,128)}, f32[2,3,512]{2,0,1:T(2,128)}, s32[]{:T(128)}, s32[2,512,1]{1,0,2:T(2,128)S(1)}, s32[2,3,512]{2,0,1:T(2,128)S(1)...) while((f32[19,4,32,384]{3,2,1,0:T(8,128)}, ...), condition=%region_3.0_spmd, body=%region_0.0_spmd | while | flops 3 | bytes 10625698 | solution.py:870
  (1 shorter events, 0.0 us)
Async XLA Ops:
  4.1 15.5 %all-to-all-start.3 = ((f32[32,8,128]{2,1,0:T(8,128)}), f32[32,8,128]{2,1,0:T(8,128)S(1)}, u32[]{:S(2)}, u32[]{:S(2)}) async-start(f32[32,8,128]{2,1,0:T(8,128)} %get-tuple-element.121), calls=%async_computation.3 | async-start | bytes 262144 | tf_op jit(solution)/shard_map/all_to_all | solution.py:746
  13.1 11.1 %collective-permute-start.4 = (f32[112,384]{1,0:T(8,128)S(1)}, f32[112,384]{1,0:T(8,128)S(1)}, u32[]{:S(2)}, u32[]{:S(2)}) collective-permute-start(f32[112,384]{1,0:T(8,128)S(1)} %get-tuple-element.119.after_ref), channel_id=1, source_target_pairs={{0,8},{8,16},{16,24},{24,0},{1,9},{9,17},{17,25},{25,1},{2,10},{10... | collective-permute-start | bytes 516104 | tf_op jit(solution)/shard_map/ppermute | solution.py:723
  14.9 10.2 %collective-permute-start.5 = (f32[112,384]{1,0:T(8,128)S(1)}, f32[112,384]{1,0:T(8,128)S(1)}, u32[]{:S(2)}, u32[]{:S(2)}) collective-permute-start(f32[112,384]{1,0:T(8,128)S(1)} %get-tuple-element.120), channel_id=1, source_target_pairs={{8,0},{16,8},{24,16},{0,24},{9,1},{17,9},{25,17},{1,25},{10,2},{18... | collective-permute-start | bytes 516104 | tf_op jit(solution)/shard_map/ppermute | solution.py:723
  25.1 5.6 %collective-permute-start.6 = (f32[40,256]{1,0:T(8,128)S(1)}, f32[40,256]{1,0:T(8,128)S(1)}, u32[]{:S(2)}, u32[]{:S(2)}) collective-permute-start(f32[40,256]{1,0:T(8,128)S(1)} %get-tuple-element.127), channel_id=1, source_target_pairs={{0,1},{1,2},{2,3},{3,4},{4,5},{5,6},{6,7},{7,0},{8,9},{9,10},{10,1... | collective-permute-start | bytes 122888 | tf_op jit(solution)/shard_map/ppermute | solution.py:723
  25.2 5.5 %collective-permute-start.7 = (f32[40,256]{1,0:T(8,128)S(1)}, f32[40,256]{1,0:T(8,128)S(1)}, u32[]{:S(2)}, u32[]{:S(2)}) collective-permute-start(f32[40,256]{1,0:T(8,128)S(1)} %get-tuple-element.128), channel_id=1, source_target_pairs={{1,0},{2,1},{3,2},{4,3},{5,4},{6,5},{7,6},{0,7},{9,8},{10,9},{11,1... | collective-permute-start | bytes 122888 | tf_op jit(solution)/shard_map/ppermute | solution.py:723
  30.7 12.9 %copy-start.8 = (s32[2,512,1]{1,2,0:T(1,128)S(1)}, s32[2,512,1]{1,2,0:T(1,128)}, u32[]{:S(2)}) copy-start(s32[2,512,1]{1,2,0:T(1,128)} %param.13) | copy-start | bytes 12292
  30.7 21.3 %copy-start.1 = (s32[2,3,512]{2,0,1:T(2,128)S(1)}, s32[2,3,512]{2,0,1:T(2,128)}, u32[]{:S(2)}) copy-start(s32[2,3,512]{2,0,1:T(2,128)} %param.12) | copy-start | bytes 36868
  30.7 21.3 %copy-start.3 = (f32[2,3,512]{2,0,1:T(2,128)S(1)}, f32[2,3,512]{2,0,1:T(2,128)}, u32[]{:S(2)}) copy-start(f32[2,3,512]{2,0,1:T(2,128)} %param.11) | copy-start | bytes 36868
  30.7 21.3 %copy-start.5 = (f32[2,3,512]{2,0,1:T(2,128)S(1)}, f32[2,3,512]{2,0,1:T(2,128)}, u32[]{:S(2)}) copy-start(f32[2,3,512]{2,0,1:T(2,128)} %param.10) | copy-start | bytes 36868
  40.4 10.4 %all-to-all-start.4 = ((f32[32,2,128]{2,1,0:T(2,128)}), f32[32,2,128]{2,1,0:T(2,128)S(1)}, u32[]{:S(2)}, u32[]{:S(2)}) async-start(f32[32,2,128]{2,1,0:T(2,128)} %get-tuple-element.131), calls=%async_computation.4 | async-start | bytes 65536 | tf_op jit(solution)/shard_map/all_to_all | solution.py:746

commit v6 on v5

--- a/solution.py
+++ b/solution.py
@@ -541,6 +541,7 @@
 
 X_UP = [i for i in range(19) if LATTICE[i][0] == 1]
 X_DOWN = [i for i in range(19) if LATTICE[i][0] == -1]
+RUNS = [(0, 1, 0, 0), (1, 2, 1, 0), (3, 2, 0, 1), (5, 2, 0, 0), (7, 4, 1, 1), (11, 4, 1, 0), (15, 4, 0, 1)]
 MOVED = [i for i in range(19) if LATTICE[i][0] or LATTICE[i][1]]
 
 
@@ -592,8 +593,8 @@
 
 
 def main_kernel(
-    cap, steps, before, y_low, y_high, force_0, force_1, own_0, own_1, out_hbm, back_ref,
-    side, after, ring_ref, probe_0, probe_1, rows, out_ref, sems,
+    cap, steps, before, y_low, y_high, force_0, force_1, own_0, own_1, after_hbm, back_ref,
+    side, after, ring_ref, probe_0, probe_1, rows, sems,
 ):
     planes, tall, width_y = before.shape[1], before.shape[2], before.shape[3]
     width_x, wide = tall - RING, after.shape[3]
@@ -621,7 +622,7 @@
             if member in MOVED:
                 f.append(after[member, z, at, lanes])
                 continue
-            other = lax.rem(z - LATTICE[member][2] + planes, planes)
+            other = (z - LATTICE[member][2]) % planes
             f.append(before[member, other, at, lanes] if start < width_y else side[member, other, at, all_lanes])
         density, momenta = moments(f)
         if flat is not None:
@@ -634,45 +635,83 @@
         for member in kept:
             after[member, z, at, lanes] = values[member]
 
-    def second_body(z, row, flat):
-        for start in range(0, width_y, LANES):
-            second_block(z, row, start, flat)
-        second_block(z, row, width_y, kept=[i for i in range(19) if LATTICE[i][1]])
-
-    for_rows(planes, width_x, second_body)
-
-    @pl.loop(0, planes)
-    def _(z):
+    copies = []
+    for z in range(planes):
+
+        @pl.loop(0, width_x // 8)
+        def _(index):
+            row = pl.multiple_of(index * 8, 8)
+            for start in range(0, width_y, LANES):
+                second_block(z, row, start, pl.multiple_of(z * width_x + row, 8))
+            second_block(z, row, width_y, kept=[i for i in range(19) if LATTICE[i][1]])
+
         for start in range(0, wide, LANES):
             second_block(z, width_x, start, kept=[i for i in range(19) if LATTICE[i][0]])
+        for number, (first, count, along_x, along_y) in enumerate(RUNS):
+            part = (pl.ds(first, count), z, pl.ds(0, tall if along_x else width_x), pl.ds(0, wide if along_y else width_y))
+            copies.append(pltpu.make_async_copy(after.at[part], after_hbm.at[part], sems.at[len(RUNS) * z + number]))
+            copies[-1].start()
 
     def sample_step(step, own_ref, probe_ref):
         for number, row in enumerate(sample(own_ref[...], planes, width_x, width_y, probe_ref)):
             rows[steps * number + step : steps * number + step + 1, :] = row
 
     sample_step(0, own_0, probe_0)
-    copies = []
-    for member in range(19):
-        for z in range(planes):
-            to = (z + LATTICE[member][2]) % planes
-            out_ref[member, to] = shifted(after[member, z], member)[0:width_x, 0:width_y]
-        copies.append(pltpu.make_async_copy(out_ref.at[member], out_hbm.at[member], sems.at[member]))
-        copies[-1].start()
-
-    def last_body(z, row, flat):
-        for start in range(0, width_y, LANES):
-            lanes = pl.ds(start, LANES)
-            density, momenta = moments([out_ref[member, z, pl.ds(row, 8), lanes] for member in range(19)])
-            inverse = 1.0 / density
-            for number, force in enumerate(force_at(force_1, planes, tall, z, row, lanes)):
-                probe_1[pl.ds(pl.multiple_of(number * planes * width_x + flat, 8), 8), lanes] = (
-                    momenta[number] + 0.5 * force
-                ) * inverse
-
-    for_rows(planes, width_x, last_body)
+    for z in range(planes):
+
+        def streamed(along_x, along_y, weight):
+            total = None
+            rows_used = tall if along_x else width_x
+            lanes_used = wide if along_y else width_y
+            for member in range(19):
+                if LATTICE[member][:2] != (along_x, along_y) or weight(LATTICE[member][2]) == 0:
+                    continue
+                value = after[member, (z - LATTICE[member][2]) % planes, 0:rows_used, 0:lanes_used]
+                value = value if weight(LATTICE[member][2]) > 0 else -value
+                total = value if total is None else total + value
+            if along_x:
+                total = pltpu.roll(total, along_x % rows_used, 0)
+            if along_y:
+                total = pltpu.roll(total, along_y % lanes_used, 1)
+            return total[0:width_x, 0:width_y]
+
+        here = {(x, y): streamed(x, y, lambda cz: 1) for x in (-1, 0, 1) for y in (-1, 0, 1)}
+        density = sum(here.values())
+        momenta = [
+            sum(here[1, y] - here[-1, y] for y in (-1, 0, 1)),
+            sum(here[x, 1] - here[x, -1] for x in (-1, 0, 1)),
+            sum(streamed(x, y, lambda cz: cz) for x, y in ((0, 0), (1, 0), (-1, 0), (0, 1), (0, -1))),
+        ]
+        inverse = 1.0 / density
+        for number in range(3):
+            at, to = (number * planes + z) * tall, (number * planes + z) * width_x
+            probe_1[to : to + width_x, :] = (
+                momenta[number] + 0.5 * force_1[at : at + width_x, 0:width_y]
+            ) * inverse
 
     sample_step(1, own_1, probe_1)
     send_back(cap, rows, back_ref)
+    for copy in copies:
+        copy.wait()
+
+
+def store_kernel(after_hbm, out_hbm, after, out_ref, sems, out_sems):
+    planes, width_x, width_y = out_ref.shape[1], out_ref.shape[2], out_ref.shape[3]
+    tall, wide = after.shape[2], after.shape[3]
+    parts = [
+        (pl.ds(first, count), slice(None), pl.ds(0, tall if along_x else width_x), pl.ds(0, wide if along_y else width_y))
+        for first, count, along_x, along_y in RUNS
+    ]
+    arriving = fetch([(after_hbm.at[part], after.at[part]) for part in parts], sems)
+    copies = []
+    for copy, (first, count, along_x, along_y) in zip(arriving, RUNS):
+        copy.wait()
+        for member in range(first, first + count):
+            for z in range(planes):
+                block = after[member, z, 0 : tall if along_x else width_x, 0 : wide if along_y else width_y]
+                out_ref[member, (z + LATTICE[member][2]) % planes] = shifted(block, member)[0:width_x, 0:width_y]
+            copies.append(pltpu.make_async_copy(out_ref.at[member], out_hbm.at[member], out_sems.at[member]))
+            copies[-1].start()
     for copy in copies:
         copy.wait()
 
@@ -697,6 +736,7 @@
     shapes = [jax.ShapeDtypeStruct(shape, kind) for shape, kind in outs]
     out_specs = [pl.BlockSpec(memory_space=pltpu.SMEM if len(shape) == 1 else pltpu.VMEM) for shape, _ in outs]
     if stored:
+        shapes = [pltpu.HBM(*out) if own else shape for out, shape, own in zip(outs, shapes, stored)]
         out_specs = [pl.BlockSpec(memory_space=pltpu.HBM if own else pltpu.VMEM) for own in stored]
     places = {True: pltpu.HBM, False: pltpu.VMEM, None: pltpu.SMEM}
     specs = [pl.BlockSpec(memory_space=places[own]) for own in fetched]
@@ -835,9 +875,9 @@
         main_kernel(cap, steps, *refs)
 
     own_field = pltpu.VMEM((3 * planes * width_x, width_y), F32)
-    fields, back = call(
+    after, back = call(
         main,
-        [(populations_in.shape, F32), ((devices, steps, LANES), F32)],
+        [((19, planes, tall, wide), F32), ((devices, steps, LANES), F32)],
         [
             pltpu.VMEM((19, planes, tall, LANES), F32),
             pltpu.VMEM((19, planes, tall, wide), F32),
@@ -845,11 +885,22 @@
             own_field,
             own_field,
             pltpu.VMEM((8, slots), F32),
-            pltpu.VMEM(populations_in.shape, F32),
-            pltpu.SemaphoreType.DMA((19,)),
+            pltpu.SemaphoreType.DMA((len(RUNS) * planes,)),
         ],
         stored=(True, False),
     )(before, y_low, y_high, force_0, force_1, own_0, own_1)
+    (fields,) = call(
+        store_kernel,
+        [(populations_in.shape, F32)],
+        [
+            pltpu.VMEM((19, planes, tall, wide), F32),
+            pltpu.VMEM(populations_in.shape, F32),
+            pltpu.SemaphoreType.DMA((len(RUNS),)),
+            pltpu.SemaphoreType.DMA((19,)),
+        ],
+        fetched=(True,),
+        stored=(True,),
+    )(after)
     returned = send(back)
 
     def unpack(*refs):

time: 53.2 us -> 52.4 us (0.985)
  waiting for transfers between devices: 8.76 us -> 4.5 us
  Pallas kernels: 25.5 us -> 29 us
    all_to_all x2, waiting for transfers between devices: 7.84 us -> 3.58 us  [send(): lax.all_to_all(outgoing, ('gx', 'gy'), split_axis=0, concat_axis=0, tiled...]
    pallas_call x4 -> x5, Pallas kernels: 10.1 us -> 14.3 us  [call(): made(*[pltpu.with_memory_space_constraint(x, pltpu.HBM) if own else x for...]
    pallas_call x1, Pallas kernels: 9.65 us -> 8.97 us  [run(): call(main, [((19, planes, tall, wide), F32), ((devices, steps, LANES), F3...]
  transfers between devices with their start and end apart: 6 -> 6, of which waited for: 3 -> 3; matrix products, arithmetic and copies ran while one was open for 0% -> 0% of each run, Pallas kernels for 21% -> 29%
where the time goes in v6:
time: 52.4 us; the launch traced here: 52.1 us
  Pallas kernels  29 us (55%)
  starting transfers between devices  17 us (32%)
  waiting for transfers between devices  4.5 us (9%)
  between operations  0.95 us (2%)
  loops' own time  0.63 us (1%)
    pallas_call x5, Pallas kernels, call(): made(*[pltpu.with_memory_space_constraint(x, pltpu.HBM) if own else x for...  14.3 us
    all_to_all x2, starting transfers between devices, send(): lax.all_to_all(outgoing, ('gx', 'gy'), split_axis=0, concat_axis=0, tiled...  10.4 us
    pallas_call x1, Pallas kernels, run(): call(main, [((19, planes, tall, wide), F32), ((devices, steps, LANES), F3...  8.97 us
    ppermute x4, starting transfers between devices, pair(): return (lax.ppermute(up, axis, forward), lax.ppermute(down, axis, backward))  6.57 us
    pallas_call x1, Pallas kernels, run(): call(spread_markers, [field] * steps + [((8, slots), F32)] * steps + [((1...  4.43 us
    all_to_all x2, waiting for transfers between devices, send(): lax.all_to_all(outgoing, ('gx', 'gy'), split_axis=0, concat_axis=0, tiled...  3.58 us
    pallas_call x1, Pallas kernels, run(): velocity, = call(unpack, [((3, steps, owned), F32)])(returned, slot)  1.23 us
  transfers between devices with their start and end apart: 6, of which 3 were waited for; matrix products, arithmetic and copies ran while one was open for 0% of the time, Pallas kernels for 29%

profile of v6, /device:TPU:0, one launch (start us, length us, event | category | flops | bytes accessed | tf_op | source)
XLA Modules:
  0.0 52.1 jit_solution(2201024867818649704)
XLA Ops:
  0.6 3.5 %shard_map.68 = (f32[32,8,128]{2,1,0:T(8,128)}, s32[2,512]{1,0:T(2,128)S(1)}) custom-call(s32[8,128]{1,0:T(8,128)} %bitcast.28, s32[3,2,512]{2,1,0:T(2,128)} %bitcast.16, f32[3,2,512]{2,1,0:T(2,128)} %bitcast.20, f32[3,2,512]{2,1,0:T(2,128)} %bitcast.24), custom_call_target="tpu_custom_call" | custom-call | tf_op jit(solution)/shard_map/pallas_call | solution.py:754
  4.1 7.3 %all-to-all-start.3 = ((f32[32,8,128]{2,1,0:T(8,128)}), f32[32,8,128]{2,1,0:T(8,128)S(1)}, u32[]{:S(2)}, u32[]{:S(2)}) async-start(f32[32,8,128]{2,1,0:T(8,128)} %get-tuple-element.121), calls=%async_computation.3 | async-start | bytes 262144 | tf_op jit(solution)/shard_map/all_to_all | solution.py:786
  11.4 1.6 %shard_map.69 = (f32[112,384]{1,0:T(8,128)S(1)}, f32[112,384]{1,0:T(8,128)S(1)}) custom-call(f32[19,4,32,384]{3,2,1,0:T(8,128)} %f_in.5, s32[2,512]{1,0:T(2,128)S(1)} %get-tuple-element.118.after_ref.refs_1_), custom_call_target="tpu_custom_call" | custom-call | tf_op jit(solution)/shard_map/pallas_call | solution.py:754
  13.1 1.8 %collective-permute-start.4 = (f32[112,384]{1,0:T(8,128)S(1)}, f32[112,384]{1,0:T(8,128)S(1)}, u32[]{:S(2)}, u32[]{:S(2)}) collective-permute-start(f32[112,384]{1,0:T(8,128)S(1)} %get-tuple-element.119.after_ref), channel_id=1, source_target_pairs={{0,8},{8,16},{16,24},{24,0},{1,9},{9,17},{17,25},{25,1},{2,10},{10... | collective-permute-start | bytes 516104 | tf_op jit(solution)/shard_map/ppermute | solution.py:763
  14.9 2.1 %collective-permute-start.5 = (f32[112,384]{1,0:T(8,128)S(1)}, f32[112,384]{1,0:T(8,128)S(1)}, u32[]{:S(2)}, u32[]{:S(2)}) collective-permute-start(f32[112,384]{1,0:T(8,128)S(1)} %get-tuple-element.120), channel_id=1, source_target_pairs={{8,0},{16,8},{24,16},{0,24},{9,1},{17,9},{25,17},{1,25},{10,2},{18... | collective-permute-start | bytes 516104 | tf_op jit(solution)/shard_map/ppermute | solution.py:763
  16.9 2.1 %shard_map.72 = (f32[32,256]{1,0:T(8,128)S(1)}, f32[32,256]{1,0:T(8,128)S(1)}) custom-call(f32[19,4,32,384]{3,2,1,0:T(8,128)} %f_in.5, f32[112,384]{1,0:T(8,128)S(1)} %get-tuple-element.119.after_ref), custom_call_target="tpu_custom_call" | custom-call | tf_op jit(solution)/shard_map/pallas_call | solution.py:754
  19.0 0.6 %all-to-all-done.3.refs_0_ = f32[32,8,128]{2,1,0:T(8,128)S(1)} async-done(((f32[32,8,128]{2,1,0:T(8,128)}), f32[32,8,128]{2,1,0:T(8,128)S(1)}, u32[]{:S(2)}, u32[]{:S(2)}) %all-to-all-start.3) | async-done | bytes 131104 | tf_op jit(solution)/shard_map/all_to_all | solution.py:786
  19.7 4.4 %shard_map.70 = (f32[480,512]{1,0:T(8,128)S(1)}, f32[480,512]{1,0:T(8,128)S(1)}, f32[8,1024]{1,0:T(8,128)S(1)}, f32[8,1024]{1,0:T(8,128)S(1)}, s32[1]{0:T(128)}) custom-call(f32[32,8,128]{2,1,0:T(8,128)S(1)} %all-to-all-done.3.refs_0_), custom_call_target="tpu_custom_call" | custom-call | tf_op jit(solution)/shard_map/pallas_call | solution.py:834
  24.1 0.0 collective-permute-done.4.x_low
  24.1 0.9 %collective-permute-done.5.x_high = f32[112,384]{1,0:T(8,128)S(1)} collective-permute-done((f32[112,384]{1,0:T(8,128)S(1)}, f32[112,384]{1,0:T(8,128)S(1)}, u32[]{:S(2)}, u32[]{:S(2)}) %collective-permute-start.5) | collective-permute-done | bytes 172064 | tf_op jit(solution)/shard_map/ppermute | solution.py:763
  25.0 0.1 shard_map.73
  25.1 0.1 collective-permute-start.6
  25.2 2.6 %collective-permute-start.7 = (f32[40,256]{1,0:T(8,128)S(1)}, f32[40,256]{1,0:T(8,128)S(1)}, u32[]{:S(2)}, u32[]{:S(2)}) collective-permute-start(f32[40,256]{1,0:T(8,128)S(1)} %get-tuple-element.128), channel_id=1, source_target_pairs={{1,0},{2,1},{3,2},{4,3},{5,4},{6,5},{7,6},{0,7},{9,8},{10,9},{11,1... | collective-permute-start | bytes 122888 | tf_op jit(solution)/shard_map/ppermute | solution.py:763
  27.8 2.8 %shard_map.71.refs_0_ = f32[19,4,40,384]{3,2,1,0:T(8,128)S(1)} custom-call(f32[19,4,32,384]{3,2,1,0:T(8,128)} %f_in.5, f32[112,384]{1,0:T(8,128)S(1)} %collective-permute-done.4.x_low, f32[112,384]{1,0:T(8,128)S(1)} %collective-permute-done.5.x_high, f32[480,512]{1,0:T(8,128)S(1)} %get-tuple-element.122.force_ref.refs_3_), custom_call_target="tpu_custom_call" | custom-call | tf_op jit(solution)/shard_map/pallas_call | solution.py:754
  30.7 0.0 copy-start.8
  30.7 0.0 collective-permute-done.6.refs_1_
  30.7 0.0 collective-permute-done.7.refs_2_
  30.7 9.0 %shard_map.74 = (f32[19,4,40,512]{3,2,1,0:T(8,128)}, f32[32,2,128]{2,1,0:T(2,128)}) custom-call(f32[19,4,40,384]{3,2,1,0:T(8,128)S(1)} %shard_map.71.refs_0_, f32[40,256]{1,0:T(8,128)S(1)} %collective-permute-done.6.refs_1_, f32[40,256]{1,0:T(8,128)S(1)} %collective-permute-done.7.refs_2_, f32[480,512]{1,0:T(8,128)S(1)} %get-tuple-element.122.force_ref.refs_3_, ...), custom_call_target="tpu_custom_call" | custom-call | tf_op jit(solution)/shard_map/pallas_call | solution.py:878
  39.7 3.1 %all-to-all-start.4 = ((f32[32,2,128]{2,1,0:T(2,128)}), f32[32,2,128]{2,1,0:T(2,128)S(1)}, u32[]{:S(2)}, u32[]{:S(2)}) async-start(f32[32,2,128]{2,1,0:T(2,128)} %get-tuple-element.131), calls=%async_computation.4 | async-start | bytes 65536 | tf_op jit(solution)/shard_map/all_to_all | solution.py:786
  42.8 0.0 copy-done.8
  42.9 0.0 copy-start.1
  42.9 0.0 copy-start.3
  42.9 0.0 copy-start.5
  42.9 4.2 %shard_map.75 = f32[19,4,32,384]{3,2,1,0:T(8,128)} custom-call(f32[19,4,40,512]{3,2,1,0:T(8,128)} %get-tuple-element.130.after_hbm), custom_call_target="tpu_custom_call" | custom-call | tf_op jit(solution)/shard_map/pallas_call | solution.py:754
  47.1 2.9 %all-to-all-done.4.refs_0_ = f32[32,2,128]{2,1,0:T(2,128)S(1)} async-done(((f32[32,2,128]{2,1,0:T(2,128)}), f32[32,2,128]{2,1,0:T(2,128)S(1)}, u32[]{:S(2)}, u32[]{:S(2)}) %all-to-all-start.4) | async-done | bytes 32800 | tf_op jit(solution)/shard_map/all_to_all | solution.py:786
  50.1 1.2 %shard_map.76 = f32[3,2,512]{2,1,0:T(2,128)} custom-call(f32[32,2,128]{2,1,0:T(2,128)S(1)} %all-to-all-done.4.refs_0_, s32[2,512]{1,0:T(2,128)S(1)} %get-tuple-element.118.after_ref.refs_1_), custom_call_target="tpu_custom_call" | custom-call | tf_op jit(solution)/shard_map/pallas_call | solution.py:909
  51.3 0.0 copy-done.1
  51.3 0.0 copy-done.3
  51.3 0.0 copy-done.5
  51.3 0.6 %while.22 = (f32[19,4,32,384]{3,2,1,0:T(8,128)}, f32[2,3,512]{2,0,1:T(2,128)}, s32[]{:T(128)}, s32[2,512,1]{1,0,2:T(2,128)S(1)}, s32[2,3,512]{2,0,1:T(2,128)S(1)...) while((f32[19,4,32,384]{3,2,1,0:T(8,128)}, ...), condition=%region_3.0_spmd, body=%region_0.0_spmd | while | flops 3 | bytes 10625698 | solution.py:921
  (1 shorter events, 0.0 us)
Async XLA Ops:
  4.1 15.5 %all-to-all-start.3 = ((f32[32,8,128]{2,1,0:T(8,128)}), f32[32,8,128]{2,1,0:T(8,128)S(1)}, u32[]{:S(2)}, u32[]{:S(2)}) async-start(f32[32,8,128]{2,1,0:T(8,128)} %get-tuple-element.121), calls=%async_computation.3 | async-start | bytes 262144 | tf_op jit(solution)/shard_map/all_to_all | solution.py:786
  13.1 11.1 %collective-permute-start.4 = (f32[112,384]{1,0:T(8,128)S(1)}, f32[112,384]{1,0:T(8,128)S(1)}, u32[]{:S(2)}, u32[]{:S(2)}) collective-permute-start(f32[112,384]{1,0:T(8,128)S(1)} %get-tuple-element.119.after_ref), channel_id=1, source_target_pairs={{0,8},{8,16},{16,24},{24,0},{1,9},{9,17},{17,25},{25,1},{2,10},{10... | collective-permute-start | bytes 516104 | tf_op jit(solution)/shard_map/ppermute | solution.py:763
  14.9 10.2 %collective-permute-start.5 = (f32[112,384]{1,0:T(8,128)S(1)}, f32[112,384]{1,0:T(8,128)S(1)}, u32[]{:S(2)}, u32[]{:S(2)}) collective-permute-start(f32[112,384]{1,0:T(8,128)S(1)} %get-tuple-element.120), channel_id=1, source_target_pairs={{8,0},{16,8},{24,16},{0,24},{9,1},{17,9},{25,17},{1,25},{10,2},{18... | collective-permute-start | bytes 516104 | tf_op jit(solution)/shard_map/ppermute | solution.py:763
  25.1 5.6 %collective-permute-start.6 = (f32[40,256]{1,0:T(8,128)S(1)}, f32[40,256]{1,0:T(8,128)S(1)}, u32[]{:S(2)}, u32[]{:S(2)}) collective-permute-start(f32[40,256]{1,0:T(8,128)S(1)} %get-tuple-element.127), channel_id=1, source_target_pairs={{0,1},{1,2},{2,3},{3,4},{4,5},{5,6},{6,7},{7,0},{8,9},{9,10},{10,1... | collective-permute-start | bytes 122888 | tf_op jit(solution)/shard_map/ppermute | solution.py:763
  25.2 5.5 %collective-permute-start.7 = (f32[40,256]{1,0:T(8,128)S(1)}, f32[40,256]{1,0:T(8,128)S(1)}, u32[]{:S(2)}, u32[]{:S(2)}) collective-permute-start(f32[40,256]{1,0:T(8,128)S(1)} %get-tuple-element.128), channel_id=1, source_target_pairs={{1,0},{2,1},{3,2},{4,3},{5,4},{6,5},{7,6},{0,7},{9,8},{10,9},{11,1... | collective-permute-start | bytes 122888 | tf_op jit(solution)/shard_map/ppermute | solution.py:763
  30.7 12.1 %copy-start.8 = (s32[2,512,1]{1,2,0:T(1,128)S(1)}, s32[2,512,1]{1,2,0:T(1,128)}, u32[]{:S(2)}) copy-start(s32[2,512,1]{1,2,0:T(1,128)} %param.13) | copy-start | bytes 12292
  39.7 10.4 %all-to-all-start.4 = ((f32[32,2,128]{2,1,0:T(2,128)}), f32[32,2,128]{2,1,0:T(2,128)S(1)}, u32[]{:S(2)}, u32[]{:S(2)}) async-start(f32[32,2,128]{2,1,0:T(2,128)} %get-tuple-element.131), calls=%async_computation.4 | async-start | bytes 65536 | tf_op jit(solution)/shard_map/all_to_all | solution.py:786
  42.9 8.5 %copy-start.1 = (s32[2,3,512]{2,0,1:T(2,128)S(1)}, s32[2,3,512]{2,0,1:T(2,128)}, u32[]{:S(2)}) copy-start(s32[2,3,512]{2,0,1:T(2,128)} %param.12) | copy-start | bytes 36868
  42.9 8.4 %copy-start.3 = (f32[2,3,512]{2,0,1:T(2,128)S(1)}, f32[2,3,512]{2,0,1:T(2,128)}, u32[]{:S(2)}) copy-start(f32[2,3,512]{2,0,1:T(2,128)} %param.11) | copy-start | bytes 36868
  42.9 8.4 %copy-start.5 = (f32[2,3,512]{2,0,1:T(2,128)S(1)}, f32[2,3,512]{2,0,1:T(2,128)}, u32[]{:S(2)}) copy-start(f32[2,3,512]{2,0,1:T(2,128)} %param.10) | copy-start | bytes 36868

commit v7 on v6

--- a/solution.py
+++ b/solution.py
@@ -42,14 +42,6 @@
     return high, low
 
 
-def split3(x):
-    high = x.astype(BF)
-    rest = x - high.astype(F32)
-    middle = rest.astype(BF)
-    low = (rest - middle.astype(F32)).astype(BF)
-    return high, middle, low
-
-
 def nt(a, b):
     return lax.dot_general(a, b, (((1,), (1,)), ((), ())), preferred_element_type=F32)
 
@@ -66,9 +58,15 @@
 SIDE = LANES
 
 
-def slot_table(slot, slots):
-    owned = slot.shape[1]
-    return jnp.where(iota((slots, owned), 0) == slot, 1.0, 0.0).astype(BF)
+def gather_lanes(rows, index):
+    index = jnp.broadcast_to(index, (8, LANES))
+    line, lane = index // LANES, index % LANES
+    found = jnp.zeros((8, LANES), F32)
+    for number in range(rows.shape[1] // LANES):
+        piece = rows[:, number * LANES : (number + 1) * LANES]
+        piece = jnp.take_along_axis(piece, lane, axis=1, mode="promise_in_bounds")
+        found = jnp.where(line == number, piece, found)
+    return found
 
 
 def fetch(pairs, sems):
@@ -99,11 +97,32 @@
     ]
 
 
+def filled(rows, members, ranks, devices, width):
+    owned = rows.shape[1]
+    number = iota((1, owned), 1) + 1
+    digits = [(number % 256).astype(F32), (number // 256).astype(F32)]
+    left = jnp.concatenate([jnp.concatenate([m * digit for m in members], axis=1) for digit in digits], axis=0)
+    place = (iota((LANES, owned), 0) % width).astype(F32)
+    right = jnp.concatenate([jnp.where(place == rank, 1.0, 0.0) for rank in ranks], axis=1)
+    found = nt(left.astype(BF), right.astype(BF))
+    marker = (found[0:devices] + 256.0 * found[devices:]).astype(jnp.int32) - 1
+    per = LANES // width
+    group = iota((1, LANES), 1) // width
+    halves = ([], [])
+    for line in range(devices // per):
+        index = marker[line * per : line * per + 1]
+        for other in range(1, per):
+            index = jnp.where(group == other, marker[line * per + other : line * per + other + 1], index)
+        for half, source in zip(halves, (rows[0:8, :], rows[8:16, :])):
+            half.append(gather_lanes(source, index))
+    return [jnp.concatenate(half, axis=1) for half in halves]
+
+
 def pack(grid, steps, cap, step_rows, out_ref, slot_ref, rows, turn=None):
     count_gx, count_gy, width_x, width_y = grid
     devices, half = count_gx * count_gy, cap // 2
     owned = rows.shape[1]
-    slots, spare = devices * cap, devices * half
+    spare = devices * half
     earlier = jnp.where(iota((owned, owned), 0) < iota((owned, owned), 1), 1.0, 0.0).astype(BF)
     column = iota((devices, owned), 0).astype(F32)
     octets, extras, most = [], [], []
@@ -122,26 +141,18 @@
             rows[...] = jnp.zeros_like(rows)
             for number, value in enumerate(values):
                 rows[number : number + 1, :] = value
-            packed = nt(jnp.concatenate(split3(rows[...]), axis=0), slot_table(slot, slots))
-            packed = packed[0:16] + packed[16:32] + packed[32:48]
-            octets.append((packed[0:8], packed[8:16]))
+            octets.append(filled(rows, [member[step][0]], [rank], devices, cap))
         taken = [jnp.zeros((devices, 1), F32)]
-        places = []
+        ranks = []
         for number in range(1, 4):
             here = member[step][number]
             rank = jnp.sum((before[4 * step + number] + taken[-1]) * here, axis=0, keepdims=True)
             taken.append(taken[-1] + jnp.sum(here, axis=1, keepdims=True))
-            if turn is not None:
-                rank = rank - turn * half
-            tile = asked[step][number]
-            places.append(jnp.where((tile >= 0) & (rank >= 0) & (rank < half), tile * half + rank, -1.0).astype(jnp.int32))
-        grid_slots = iota((spare, owned), 0)
-        chosen = (grid_slots == places[0]) | (grid_slots == places[1]) | (grid_slots == places[2])
+            ranks.append(rank if turn is None else rank - turn * half)
         rows[...] = jnp.zeros_like(rows)
         for place, value in zip((1, 2, 3, 4, 5, 6, 7, 9, 10), values):
             rows[place : place + 1, :] = value
-        extra = nt(jnp.concatenate(split3(rows[...]), axis=0), jnp.where(chosen, 1.0, 0.0).astype(BF))
-        extra = extra[0:16] + extra[16:32] + extra[32:48]
+        extra, more_extra = filled(rows, member[step][1:], ranks, devices, half)
         lanes, sender = iota((devices, spare), 1), iota((devices, spare), 0)
         ends = [
             jnp.sum(jnp.where(lanes // half == sender, end, 0.0), axis=0, keepdims=True) for end in (taken[1], taken[2])
@@ -154,7 +165,7 @@
         first = []
         for cell, width, moved in ((extra[1:2], width_x, in_x), (extra[2:3], width_y, in_y)):
             first.append(cell + jnp.where(moved, jnp.where(cell * 2 < width, width * 1.0, -1.0 * width), 0.0))
-        extras.append((jnp.concatenate([extra[0:1]] + first + [extra[3:8]], axis=0), extra[8:16]))
+        extras.append((jnp.concatenate([extra[0:1]] + first + [extra[3:8]], axis=0), more_extra))
         most.append(jnp.max(taken[3], axis=0, keepdims=True))
     lane, row = iota((8, LANES), 1), iota((8, LANES), 0)
 
@@ -293,13 +304,12 @@
                 total = jnp.where(group == place, piece, total)
             pieces.append(total)
         comps.append(jnp.concatenate(pieces, axis=1))
-    slots = devices * cap
     for step in range(steps):
-        rows = jnp.concatenate([comp[step : step + 1] for comp in comps] + [jnp.zeros((13, slots), F32)], axis=0)
-        found = nn(jnp.concatenate(split3(rows), axis=0), slot_table(slot_ref[step : step + 1, :], slots))
-        found = found[0:8] + found[16:24] + found[32:40]
-        for number in range(3):
-            out_ref[number, step : step + 1, :] = found[number : number + 1]
+        rows = jnp.concatenate([comp[step : step + 1] for comp in comps] + [jnp.zeros((5, devices * cap), F32)], axis=0)
+        for start in range(0, slot_ref.shape[1], LANES):
+            found = gather_lanes(rows, slot_ref[step : step + 1, start : start + LANES])
+            for number in range(3):
+                out_ref[number, step : step + 1, start : start + LANES] = found[number : number + 1]
 
 
 def line_weights(cell, frac, extent):

time: 52.4 us -> 51.3 us (0.979)
  Pallas kernels: 29 us -> 27.8 us
    pallas_call x5, Pallas kernels: 14.3 us -> 13.4 us  [call(): made(*[pltpu.with_memory_space_constraint(x, pltpu.HBM) if own else x for...]
  transfers between devices with their start and end apart: 6 -> 6, of which waited for: 3 -> 3; matrix products, arithmetic and copies ran while one was open for 0% -> 0% of each run, Pallas kernels for 29% -> 30%
where the time goes in v7:
time: 51.3 us; the launch traced here: 51 us
  Pallas kernels  27.8 us (54%)
  starting transfers between devices  17 us (33%)
  waiting for transfers between devices  4.51 us (9%)
  between operations  0.95 us (2%)
  loops' own time  0.63 us (1%)
    pallas_call x5, Pallas kernels, call(): made(*[pltpu.with_memory_space_constraint(x, pltpu.HBM) if own else x for...  13.4 us
    all_to_all x2, starting transfers between devices, send(): lax.all_to_all(outgoing, ('gx', 'gy'), split_axis=0, concat_axis=0, tiled...  10.4 us
    pallas_call x1, Pallas kernels, run(): call(main, [((19, planes, tall, wide), F32), ((devices, steps, LANES), F3...  8.97 us
    ppermute x4, starting transfers between devices, pair(): return (lax.ppermute(up, axis, forward), lax.ppermute(down, axis, backward))  6.57 us
    pallas_call x1, Pallas kernels, run(): call(spread_markers, [field] * steps + [((8, slots), F32)] * steps + [((1...  4.42 us
    all_to_all x2, waiting for transfers between devices, send(): lax.all_to_all(outgoing, ('gx', 'gy'), split_axis=0, concat_axis=0, tiled...  3.58 us
  transfers between devices with their start and end apart: 6, of which 3 were waited for; matrix products, arithmetic and copies ran while one was open for 0% of the time, Pallas kernels for 30%

profile of v7, /device:TPU:0, one launch (start us, length us, event | category | flops | bytes accessed | tf_op | source)
XLA Modules:
  0.0 51.0 jit_solution(15923590875197770974)
XLA Ops:
  0.6 2.7 %shard_map.68 = (f32[32,8,128]{2,1,0:T(8,128)}, s32[2,512]{1,0:T(2,128)S(1)}) custom-call(s32[8,128]{1,0:T(8,128)} %bitcast.28, s32[3,2,512]{2,1,0:T(2,128)} %bitcast.16, f32[3,2,512]{2,1,0:T(2,128)} %bitcast.20, f32[3,2,512]{2,1,0:T(2,128)} %bitcast.24), custom_call_target="tpu_custom_call" | custom-call | tf_op jit(solution)/shard_map/pallas_call | solution.py:764
  3.3 7.3 %all-to-all-start.3 = ((f32[32,8,128]{2,1,0:T(8,128)}), f32[32,8,128]{2,1,0:T(8,128)S(1)}, u32[]{:S(2)}, u32[]{:S(2)}) async-start(f32[32,8,128]{2,1,0:T(8,128)} %get-tuple-element.121), calls=%async_computation.3 | async-start | bytes 262144 | tf_op jit(solution)/shard_map/all_to_all | solution.py:796
  10.6 1.6 %shard_map.69 = (f32[112,384]{1,0:T(8,128)S(1)}, f32[112,384]{1,0:T(8,128)S(1)}) custom-call(f32[19,4,32,384]{3,2,1,0:T(8,128)} %f_in.5, s32[2,512]{1,0:T(2,128)S(1)} %get-tuple-element.118.after_ref.refs_1_), custom_call_target="tpu_custom_call" | custom-call | tf_op jit(solution)/shard_map/pallas_call | solution.py:764
  12.2 1.8 %collective-permute-start.4 = (f32[112,384]{1,0:T(8,128)S(1)}, f32[112,384]{1,0:T(8,128)S(1)}, u32[]{:S(2)}, u32[]{:S(2)}) collective-permute-start(f32[112,384]{1,0:T(8,128)S(1)} %get-tuple-element.119.after_ref), channel_id=1, source_target_pairs={{0,8},{8,16},{16,24},{24,0},{1,9},{9,17},{17,25},{25,1},{2,10},{10... | collective-permute-start | bytes 516104 | tf_op jit(solution)/shard_map/ppermute | solution.py:773
  14.1 2.1 %collective-permute-start.5 = (f32[112,384]{1,0:T(8,128)S(1)}, f32[112,384]{1,0:T(8,128)S(1)}, u32[]{:S(2)}, u32[]{:S(2)}) collective-permute-start(f32[112,384]{1,0:T(8,128)S(1)} %get-tuple-element.120), channel_id=1, source_target_pairs={{8,0},{16,8},{24,16},{0,24},{9,1},{17,9},{25,17},{1,25},{10,2},{18... | collective-permute-start | bytes 516104 | tf_op jit(solution)/shard_map/ppermute | solution.py:773
  16.1 2.1 %shard_map.72 = (f32[32,256]{1,0:T(8,128)S(1)}, f32[32,256]{1,0:T(8,128)S(1)}) custom-call(f32[19,4,32,384]{3,2,1,0:T(8,128)} %f_in.5, f32[112,384]{1,0:T(8,128)S(1)} %get-tuple-element.119.after_ref), custom_call_target="tpu_custom_call" | custom-call | tf_op jit(solution)/shard_map/pallas_call | solution.py:764
  18.2 0.6 %all-to-all-done.3.refs_0_ = f32[32,8,128]{2,1,0:T(8,128)S(1)} async-done(((f32[32,8,128]{2,1,0:T(8,128)}), f32[32,8,128]{2,1,0:T(8,128)S(1)}, u32[]{:S(2)}, u32[]{:S(2)}) %all-to-all-start.3) | async-done | bytes 131104 | tf_op jit(solution)/shard_map/all_to_all | solution.py:796
  18.8 4.4 %shard_map.70 = (f32[480,512]{1,0:T(8,128)S(1)}, f32[480,512]{1,0:T(8,128)S(1)}, f32[8,1024]{1,0:T(8,128)S(1)}, f32[8,1024]{1,0:T(8,128)S(1)}, s32[1]{0:T(128)}) custom-call(f32[32,8,128]{2,1,0:T(8,128)S(1)} %all-to-all-done.3.refs_0_), custom_call_target="tpu_custom_call" | custom-call | tf_op jit(solution)/shard_map/pallas_call | solution.py:844
  23.3 0.0 collective-permute-done.4.x_low
  23.3 0.9 %collective-permute-done.5.x_high = f32[112,384]{1,0:T(8,128)S(1)} collective-permute-done((f32[112,384]{1,0:T(8,128)S(1)}, f32[112,384]{1,0:T(8,128)S(1)}, u32[]{:S(2)}, u32[]{:S(2)}) %collective-permute-start.5) | collective-permute-done | bytes 172064 | tf_op jit(solution)/shard_map/ppermute | solution.py:773
  24.2 0.1 shard_map.73
  24.3 0.1 collective-permute-start.6
  24.4 2.6 %collective-permute-start.7 = (f32[40,256]{1,0:T(8,128)S(1)}, f32[40,256]{1,0:T(8,128)S(1)}, u32[]{:S(2)}, u32[]{:S(2)}) collective-permute-start(f32[40,256]{1,0:T(8,128)S(1)} %get-tuple-element.128), channel_id=1, source_target_pairs={{1,0},{2,1},{3,2},{4,3},{5,4},{6,5},{7,6},{0,7},{9,8},{10,9},{11,1... | collective-permute-start | bytes 122888 | tf_op jit(solution)/shard_map/ppermute | solution.py:773
  27.0 2.8 %shard_map.71.refs_0_ = f32[19,4,40,384]{3,2,1,0:T(8,128)S(1)} custom-call(f32[19,4,32,384]{3,2,1,0:T(8,128)} %f_in.5, f32[112,384]{1,0:T(8,128)S(1)} %collective-permute-done.4.x_low, f32[112,384]{1,0:T(8,128)S(1)} %collective-permute-done.5.x_high, f32[480,512]{1,0:T(8,128)S(1)} %get-tuple-element.122.force_ref.refs_3_), custom_call_target="tpu_custom_call" | custom-call | tf_op jit(solution)/shard_map/pallas_call | solution.py:764
  29.9 0.0 copy-start.8
  29.9 0.0 collective-permute-done.6.refs_1_
  29.9 0.0 collective-permute-done.7.refs_2_
  29.9 9.0 %shard_map.74 = (f32[19,4,40,512]{3,2,1,0:T(8,128)}, f32[32,2,128]{2,1,0:T(2,128)}) custom-call(f32[19,4,40,384]{3,2,1,0:T(8,128)S(1)} %shard_map.71.refs_0_, f32[40,256]{1,0:T(8,128)S(1)} %collective-permute-done.6.refs_1_, f32[40,256]{1,0:T(8,128)S(1)} %collective-permute-done.7.refs_2_, f32[480,512]{1,0:T(8,128)S(1)} %get-tuple-element.122.force_ref.refs_3_, ...), custom_call_target="tpu_custom_call" | custom-call | tf_op jit(solution)/shard_map/pallas_call | solution.py:888
  38.9 3.1 %all-to-all-start.4 = ((f32[32,2,128]{2,1,0:T(2,128)}), f32[32,2,128]{2,1,0:T(2,128)S(1)}, u32[]{:S(2)}, u32[]{:S(2)}) async-start(f32[32,2,128]{2,1,0:T(2,128)} %get-tuple-element.131), calls=%async_computation.4 | async-start | bytes 65536 | tf_op jit(solution)/shard_map/all_to_all | solution.py:796
  42.0 0.0 copy-done.8
  42.0 0.0 copy-start.1
  42.0 0.0 copy-start.3
  42.0 0.0 copy-start.5
  42.1 4.2 %shard_map.75 = f32[19,4,32,384]{3,2,1,0:T(8,128)} custom-call(f32[19,4,40,512]{3,2,1,0:T(8,128)} %get-tuple-element.130.after_hbm), custom_call_target="tpu_custom_call" | custom-call | tf_op jit(solution)/shard_map/pallas_call | solution.py:764
  46.3 2.9 %all-to-all-done.4.refs_0_ = f32[32,2,128]{2,1,0:T(2,128)S(1)} async-done(((f32[32,2,128]{2,1,0:T(2,128)}), f32[32,2,128]{2,1,0:T(2,128)S(1)}, u32[]{:S(2)}, u32[]{:S(2)}) %all-to-all-start.4) | async-done | bytes 32800 | tf_op jit(solution)/shard_map/all_to_all | solution.py:796
  49.2 0.9 %shard_map.76 = f32[3,2,512]{2,1,0:T(2,128)} custom-call(f32[32,2,128]{2,1,0:T(2,128)S(1)} %all-to-all-done.4.refs_0_, s32[2,512]{1,0:T(2,128)S(1)} %get-tuple-element.118.after_ref.refs_1_), custom_call_target="tpu_custom_call" | custom-call | tf_op jit(solution)/shard_map/pallas_call | solution.py:919
  50.2 0.0 copy-done.1
  50.2 0.0 copy-done.3
  50.2 0.0 copy-done.5
  50.2 0.6 %while.22 = (f32[19,4,32,384]{3,2,1,0:T(8,128)}, f32[2,3,512]{2,0,1:T(2,128)}, s32[]{:T(128)}, s32[2,512,1]{1,0,2:T(2,128)S(1)}, s32[2,3,512]{2,0,1:T(2,128)S(1)...) while((f32[19,4,32,384]{3,2,1,0:T(8,128)}, ...), condition=%region_3.0_spmd, body=%region_0.0_spmd | while | flops 3 | bytes 10625698 | solution.py:931
  (1 shorter events, 0.0 us)
Async XLA Ops:
  3.3 15.5 %all-to-all-start.3 = ((f32[32,8,128]{2,1,0:T(8,128)}), f32[32,8,128]{2,1,0:T(8,128)S(1)}, u32[]{:S(2)}, u32[]{:S(2)}) async-start(f32[32,8,128]{2,1,0:T(8,128)} %get-tuple-element.121), calls=%async_computation.3 | async-start | bytes 262144 | tf_op jit(solution)/shard_map/all_to_all | solution.py:796
  12.2 11.1 %collective-permute-start.4 = (f32[112,384]{1,0:T(8,128)S(1)}, f32[112,384]{1,0:T(8,128)S(1)}, u32[]{:S(2)}, u32[]{:S(2)}) collective-permute-start(f32[112,384]{1,0:T(8,128)S(1)} %get-tuple-element.119.after_ref), channel_id=1, source_target_pairs={{0,8},{8,16},{16,24},{24,0},{1,9},{9,17},{17,25},{25,1},{2,10},{10... | collective-permute-start | bytes 516104 | tf_op jit(solution)/shard_map/ppermute | solution.py:773
  14.1 10.2 %collective-permute-start.5 = (f32[112,384]{1,0:T(8,128)S(1)}, f32[112,384]{1,0:T(8,128)S(1)}, u32[]{:S(2)}, u32[]{:S(2)}) collective-permute-start(f32[112,384]{1,0:T(8,128)S(1)} %get-tuple-element.120), channel_id=1, source_target_pairs={{8,0},{16,8},{24,16},{0,24},{9,1},{17,9},{25,17},{1,25},{10,2},{18... | collective-permute-start | bytes 516104 | tf_op jit(solution)/shard_map/ppermute | solution.py:773
  24.3 5.6 %collective-permute-start.6 = (f32[40,256]{1,0:T(8,128)S(1)}, f32[40,256]{1,0:T(8,128)S(1)}, u32[]{:S(2)}, u32[]{:S(2)}) collective-permute-start(f32[40,256]{1,0:T(8,128)S(1)} %get-tuple-element.127), channel_id=1, source_target_pairs={{0,1},{1,2},{2,3},{3,4},{4,5},{5,6},{6,7},{7,0},{8,9},{9,10},{10,1... | collective-permute-start | bytes 122888 | tf_op jit(solution)/shard_map/ppermute | solution.py:773
  24.4 5.5 %collective-permute-start.7 = (f32[40,256]{1,0:T(8,128)S(1)}, f32[40,256]{1,0:T(8,128)S(1)}, u32[]{:S(2)}, u32[]{:S(2)}) collective-permute-start(f32[40,256]{1,0:T(8,128)S(1)} %get-tuple-element.128), channel_id=1, source_target_pairs={{1,0},{2,1},{3,2},{4,3},{5,4},{6,5},{7,6},{0,7},{9,8},{10,9},{11,1... | collective-permute-start | bytes 122888 | tf_op jit(solution)/shard_map/ppermute | solution.py:773
  29.9 12.1 %copy-start.8 = (s32[2,512,1]{1,2,0:T(1,128)S(1)}, s32[2,512,1]{1,2,0:T(1,128)}, u32[]{:S(2)}) copy-start(s32[2,512,1]{1,2,0:T(1,128)} %param.13) | copy-start | bytes 12292
  38.9 10.4 %all-to-all-start.4 = ((f32[32,2,128]{2,1,0:T(2,128)}), f32[32,2,128]{2,1,0:T(2,128)S(1)}, u32[]{:S(2)}, u32[]{:S(2)}) async-start(f32[32,2,128]{2,1,0:T(2,128)} %get-tuple-element.131), calls=%async_computation.4 | async-start | bytes 65536 | tf_op jit(solution)/shard_map/all_to_all | solution.py:796
  42.0 8.1 %copy-start.1 = (s32[2,3,512]{2,0,1:T(2,128)S(1)}, s32[2,3,512]{2,0,1:T(2,128)}, u32[]{:S(2)}) copy-start(s32[2,3,512]{2,0,1:T(2,128)} %param.12) | copy-start | bytes 36868
  42.0 8.1 %copy-start.3 = (f32[2,3,512]{2,0,1:T(2,128)S(1)}, f32[2,3,512]{2,0,1:T(2,128)}, u32[]{:S(2)}) copy-start(f32[2,3,512]{2,0,1:T(2,128)} %param.11) | copy-start | bytes 36868
  42.0 8.1 %copy-start.5 = (f32[2,3,512]{2,0,1:T(2,128)S(1)}, f32[2,3,512]{2,0,1:T(2,128)}, u32[]{:S(2)}) copy-start(f32[2,3,512]{2,0,1:T(2,128)} %param.10) | copy-start | bytes 36868

commit v8 on v7

--- a/solution.py
+++ b/solution.py
@@ -611,13 +611,10 @@
     side_cells(y_low, y_high, side, ring_ref)
     far, all_lanes = pl.ds(width_y, LANES), pl.ds(0, LANES)
 
-    def side_body(z, row, flat):
-        collide_block(side, None, force_0, z, row, all_lanes, far)
-
-    for_rows(planes, width_x, side_body)
-
     @pl.loop(0, planes)
     def _(z):
+        for row in range(0, width_x, 8):
+            collide_block(side, None, force_0, z, row, all_lanes, far)
         collide_block(side, ring_ref, force_0, z, width_x, all_lanes, far)
 
     for member in MOVED:

time: 51.3 us -> 51 us (level)
  no operation moved by 1% of the time
where the time goes in v8:
time: 51 us; the launch traced here: 50.7 us
  Pallas kernels  27.6 us (54%)
  starting transfers between devices  17 us (33%)
  waiting for transfers between devices  4.51 us (9%)
  between operations  0.95 us (2%)
  loops' own time  0.63 us (1%)
    pallas_call x5, Pallas kernels, call(): made(*[pltpu.with_memory_space_constraint(x, pltpu.HBM) if own else x for...  13.4 us
    all_to_all x2, starting transfers between devices, send(): lax.all_to_all(outgoing, ('gx', 'gy'), split_axis=0, concat_axis=0, tiled...  10.4 us
    pallas_call x1, Pallas kernels, run(): call(main, [((19, planes, tall, wide), F32), ((devices, steps, LANES), F3...  8.72 us
    ppermute x4, starting transfers between devices, pair(): return (lax.ppermute(up, axis, forward), lax.ppermute(down, axis, backward))  6.57 us
    pallas_call x1, Pallas kernels, run(): call(spread_markers, [field] * steps + [((8, slots), F32)] * steps + [((1...  4.42 us
    all_to_all x2, waiting for transfers between devices, send(): lax.all_to_all(outgoing, ('gx', 'gy'), split_axis=0, concat_axis=0, tiled...  3.58 us
  transfers between devices with their start and end apart: 6, of which 3 were waited for; matrix products, arithmetic and copies ran while one was open for 0% of the time, Pallas kernels for 30%

profile of v8, /device:TPU:0, one launch (start us, length us, event | category | flops | bytes accessed | tf_op | source)
XLA Modules:
  0.0 50.7 jit_solution(15090524873798973098)
XLA Ops:
  0.6 2.7 %shard_map.68 = (f32[32,8,128]{2,1,0:T(8,128)}, s32[2,512]{1,0:T(2,128)S(1)}) custom-call(s32[8,128]{1,0:T(8,128)} %bitcast.28, s32[3,2,512]{2,1,0:T(2,128)} %bitcast.16, f32[3,2,512]{2,1,0:T(2,128)} %bitcast.20, f32[3,2,512]{2,1,0:T(2,128)} %bitcast.24), custom_call_target="tpu_custom_call" | custom-call | tf_op jit(solution)/shard_map/pallas_call | solution.py:761
  3.3 7.3 %all-to-all-start.3 = ((f32[32,8,128]{2,1,0:T(8,128)}), f32[32,8,128]{2,1,0:T(8,128)S(1)}, u32[]{:S(2)}, u32[]{:S(2)}) async-start(f32[32,8,128]{2,1,0:T(8,128)} %get-tuple-element.121), calls=%async_computation.3 | async-start | bytes 262144 | tf_op jit(solution)/shard_map/all_to_all | solution.py:793
  10.6 1.6 %shard_map.69 = (f32[112,384]{1,0:T(8,128)S(1)}, f32[112,384]{1,0:T(8,128)S(1)}) custom-call(f32[19,4,32,384]{3,2,1,0:T(8,128)} %f_in.5, s32[2,512]{1,0:T(2,128)S(1)} %get-tuple-element.118.after_ref.refs_1_), custom_call_target="tpu_custom_call" | custom-call | tf_op jit(solution)/shard_map/pallas_call | solution.py:761
  12.2 1.8 %collective-permute-start.4 = (f32[112,384]{1,0:T(8,128)S(1)}, f32[112,384]{1,0:T(8,128)S(1)}, u32[]{:S(2)}, u32[]{:S(2)}) collective-permute-start(f32[112,384]{1,0:T(8,128)S(1)} %get-tuple-element.119.after_ref), channel_id=1, source_target_pairs={{0,8},{8,16},{16,24},{24,0},{1,9},{9,17},{17,25},{25,1},{2,10},{10... | collective-permute-start | bytes 516104 | tf_op jit(solution)/shard_map/ppermute | solution.py:770
  14.1 2.1 %collective-permute-start.5 = (f32[112,384]{1,0:T(8,128)S(1)}, f32[112,384]{1,0:T(8,128)S(1)}, u32[]{:S(2)}, u32[]{:S(2)}) collective-permute-start(f32[112,384]{1,0:T(8,128)S(1)} %get-tuple-element.120), channel_id=1, source_target_pairs={{8,0},{16,8},{24,16},{0,24},{9,1},{17,9},{25,17},{1,25},{10,2},{18... | collective-permute-start | bytes 516104 | tf_op jit(solution)/shard_map/ppermute | solution.py:770
  16.1 2.1 %shard_map.72 = (f32[32,256]{1,0:T(8,128)S(1)}, f32[32,256]{1,0:T(8,128)S(1)}) custom-call(f32[19,4,32,384]{3,2,1,0:T(8,128)} %f_in.5, f32[112,384]{1,0:T(8,128)S(1)} %get-tuple-element.119.after_ref), custom_call_target="tpu_custom_call" | custom-call | tf_op jit(solution)/shard_map/pallas_call | solution.py:761
  18.2 0.6 %all-to-all-done.3.refs_0_ = f32[32,8,128]{2,1,0:T(8,128)S(1)} async-done(((f32[32,8,128]{2,1,0:T(8,128)}), f32[32,8,128]{2,1,0:T(8,128)S(1)}, u32[]{:S(2)}, u32[]{:S(2)}) %all-to-all-start.3) | async-done | bytes 131104 | tf_op jit(solution)/shard_map/all_to_all | solution.py:793
  18.8 4.4 %shard_map.70 = (f32[480,512]{1,0:T(8,128)S(1)}, f32[480,512]{1,0:T(8,128)S(1)}, f32[8,1024]{1,0:T(8,128)S(1)}, f32[8,1024]{1,0:T(8,128)S(1)}, s32[1]{0:T(128)}) custom-call(f32[32,8,128]{2,1,0:T(8,128)S(1)} %all-to-all-done.3.refs_0_), custom_call_target="tpu_custom_call" | custom-call | tf_op jit(solution)/shard_map/pallas_call | solution.py:841
  23.3 0.0 collective-permute-done.4.x_low
  23.3 0.9 %collective-permute-done.5.x_high = f32[112,384]{1,0:T(8,128)S(1)} collective-permute-done((f32[112,384]{1,0:T(8,128)S(1)}, f32[112,384]{1,0:T(8,128)S(1)}, u32[]{:S(2)}, u32[]{:S(2)}) %collective-permute-start.5) | collective-permute-done | bytes 172064 | tf_op jit(solution)/shard_map/ppermute | solution.py:770
  24.2 0.1 shard_map.73
  24.3 0.1 collective-permute-start.6
  24.4 2.6 %collective-permute-start.7 = (f32[40,256]{1,0:T(8,128)S(1)}, f32[40,256]{1,0:T(8,128)S(1)}, u32[]{:S(2)}, u32[]{:S(2)}) collective-permute-start(f32[40,256]{1,0:T(8,128)S(1)} %get-tuple-element.128), channel_id=1, source_target_pairs={{1,0},{2,1},{3,2},{4,3},{5,4},{6,5},{7,6},{0,7},{9,8},{10,9},{11,1... | collective-permute-start | bytes 122888 | tf_op jit(solution)/shard_map/ppermute | solution.py:770
  27.0 2.8 %shard_map.71.refs_0_ = f32[19,4,40,384]{3,2,1,0:T(8,128)S(1)} custom-call(f32[19,4,32,384]{3,2,1,0:T(8,128)} %f_in.5, f32[112,384]{1,0:T(8,128)S(1)} %collective-permute-done.4.x_low, f32[112,384]{1,0:T(8,128)S(1)} %collective-permute-done.5.x_high, f32[480,512]{1,0:T(8,128)S(1)} %get-tuple-element.122.force_ref.refs_3_), custom_call_target="tpu_custom_call" | custom-call | tf_op jit(solution)/shard_map/pallas_call | solution.py:761
  29.9 0.0 copy-start.8
  29.9 0.0 collective-permute-done.6.refs_1_
  29.9 0.0 collective-permute-done.7.refs_2_
  29.9 8.7 %shard_map.74 = (f32[19,4,40,512]{3,2,1,0:T(8,128)}, f32[32,2,128]{2,1,0:T(2,128)}) custom-call(f32[19,4,40,384]{3,2,1,0:T(8,128)S(1)} %shard_map.71.refs_0_, f32[40,256]{1,0:T(8,128)S(1)} %collective-permute-done.6.refs_1_, f32[40,256]{1,0:T(8,128)S(1)} %collective-permute-done.7.refs_2_, f32[480,512]{1,0:T(8,128)S(1)} %get-tuple-element.122.force_ref.refs_3_, ...), custom_call_target="tpu_custom_call" | custom-call | tf_op jit(solution)/shard_map/pallas_call | solution.py:885
  38.6 3.1 %all-to-all-start.4 = ((f32[32,2,128]{2,1,0:T(2,128)}), f32[32,2,128]{2,1,0:T(2,128)S(1)}, u32[]{:S(2)}, u32[]{:S(2)}) async-start(f32[32,2,128]{2,1,0:T(2,128)} %get-tuple-element.131), calls=%async_computation.4 | async-start | bytes 65536 | tf_op jit(solution)/shard_map/all_to_all | solution.py:793
  41.8 0.0 copy-done.8
  41.8 0.0 copy-start.1
  41.8 0.0 copy-start.3
  41.8 0.0 copy-start.5
  41.8 4.2 %shard_map.75 = f32[19,4,32,384]{3,2,1,0:T(8,128)} custom-call(f32[19,4,40,512]{3,2,1,0:T(8,128)} %get-tuple-element.130.after_hbm), custom_call_target="tpu_custom_call" | custom-call | tf_op jit(solution)/shard_map/pallas_call | solution.py:761
  46.0 2.9 %all-to-all-done.4.refs_0_ = f32[32,2,128]{2,1,0:T(2,128)S(1)} async-done(((f32[32,2,128]{2,1,0:T(2,128)}), f32[32,2,128]{2,1,0:T(2,128)S(1)}, u32[]{:S(2)}, u32[]{:S(2)}) %all-to-all-start.4) | async-done | bytes 32800 | tf_op jit(solution)/shard_map/all_to_all | solution.py:793
  49.0 0.9 %shard_map.76 = f32[3,2,512]{2,1,0:T(2,128)} custom-call(f32[32,2,128]{2,1,0:T(2,128)S(1)} %all-to-all-done.4.refs_0_, s32[2,512]{1,0:T(2,128)S(1)} %get-tuple-element.118.after_ref.refs_1_), custom_call_target="tpu_custom_call" | custom-call | tf_op jit(solution)/shard_map/pallas_call | solution.py:916
  49.9 0.0 copy-done.1
  49.9 0.0 copy-done.3
  49.9 0.0 copy-done.5
  49.9 0.6 %while.22 = (f32[19,4,32,384]{3,2,1,0:T(8,128)}, f32[2,3,512]{2,0,1:T(2,128)}, s32[]{:T(128)}, s32[2,512,1]{1,0,2:T(2,128)S(1)}, s32[2,3,512]{2,0,1:T(2,128)S(1)...) while((f32[19,4,32,384]{3,2,1,0:T(8,128)}, ...), condition=%region_3.0_spmd, body=%region_0.0_spmd | while | flops 3 | bytes 10625698 | solution.py:928
  (1 shorter events, 0.0 us)
Async XLA Ops:
  3.3 15.5 %all-to-all-start.3 = ((f32[32,8,128]{2,1,0:T(8,128)}), f32[32,8,128]{2,1,0:T(8,128)S(1)}, u32[]{:S(2)}, u32[]{:S(2)}) async-start(f32[32,8,128]{2,1,0:T(8,128)} %get-tuple-element.121), calls=%async_computation.3 | async-start | bytes 262144 | tf_op jit(solution)/shard_map/all_to_all | solution.py:793
  12.2 11.1 %collective-permute-start.4 = (f32[112,384]{1,0:T(8,128)S(1)}, f32[112,384]{1,0:T(8,128)S(1)}, u32[]{:S(2)}, u32[]{:S(2)}) collective-permute-start(f32[112,384]{1,0:T(8,128)S(1)} %get-tuple-element.119.after_ref), channel_id=1, source_target_pairs={{0,8},{8,16},{16,24},{24,0},{1,9},{9,17},{17,25},{25,1},{2,10},{10... | collective-permute-start | bytes 516104 | tf_op jit(solution)/shard_map/ppermute | solution.py:770
  14.1 10.2 %collective-permute-start.5 = (f32[112,384]{1,0:T(8,128)S(1)}, f32[112,384]{1,0:T(8,128)S(1)}, u32[]{:S(2)}, u32[]{:S(2)}) collective-permute-start(f32[112,384]{1,0:T(8,128)S(1)} %get-tuple-element.120), channel_id=1, source_target_pairs={{8,0},{16,8},{24,16},{0,24},{9,1},{17,9},{25,17},{1,25},{10,2},{18... | collective-permute-start | bytes 516104 | tf_op jit(solution)/shard_map/ppermute | solution.py:770
  24.3 5.6 %collective-permute-start.6 = (f32[40,256]{1,0:T(8,128)S(1)}, f32[40,256]{1,0:T(8,128)S(1)}, u32[]{:S(2)}, u32[]{:S(2)}) collective-permute-start(f32[40,256]{1,0:T(8,128)S(1)} %get-tuple-element.127), channel_id=1, source_target_pairs={{0,1},{1,2},{2,3},{3,4},{4,5},{5,6},{6,7},{7,0},{8,9},{9,10},{10,1... | collective-permute-start | bytes 122888 | tf_op jit(solution)/shard_map/ppermute | solution.py:770
  24.4 5.5 %collective-permute-start.7 = (f32[40,256]{1,0:T(8,128)S(1)}, f32[40,256]{1,0:T(8,128)S(1)}, u32[]{:S(2)}, u32[]{:S(2)}) collective-permute-start(f32[40,256]{1,0:T(8,128)S(1)} %get-tuple-element.128), channel_id=1, source_target_pairs={{1,0},{2,1},{3,2},{4,3},{5,4},{6,5},{7,6},{0,7},{9,8},{10,9},{11,1... | collective-permute-start | bytes 122888 | tf_op jit(solution)/shard_map/ppermute | solution.py:770
  29.9 11.9 %copy-start.8 = (s32[2,512,1]{1,2,0:T(1,128)S(1)}, s32[2,512,1]{1,2,0:T(1,128)}, u32[]{:S(2)}) copy-start(s32[2,512,1]{1,2,0:T(1,128)} %param.13) | copy-start | bytes 12292
  38.6 10.4 %all-to-all-start.4 = ((f32[32,2,128]{2,1,0:T(2,128)}), f32[32,2,128]{2,1,0:T(2,128)S(1)}, u32[]{:S(2)}, u32[]{:S(2)}) async-start(f32[32,2,128]{2,1,0:T(2,128)} %get-tuple-element.131), calls=%async_computation.4 | async-start | bytes 65536 | tf_op jit(solution)/shard_map/all_to_all | solution.py:793
  41.8 8.1 %copy-start.1 = (s32[2,3,512]{2,0,1:T(2,128)S(1)}, s32[2,3,512]{2,0,1:T(2,128)}, u32[]{:S(2)}) copy-start(s32[2,3,512]{2,0,1:T(2,128)} %param.12) | copy-start | bytes 36868
  41.8 8.1 %copy-start.3 = (f32[2,3,512]{2,0,1:T(2,128)S(1)}, f32[2,3,512]{2,0,1:T(2,128)}, u32[]{:S(2)}) copy-start(f32[2,3,512]{2,0,1:T(2,128)} %param.11) | copy-start | bytes 36868
  41.8 8.1 %copy-start.5 = (f32[2,3,512]{2,0,1:T(2,128)S(1)}, f32[2,3,512]{2,0,1:T(2,128)}, u32[]{:S(2)}) copy-start(f32[2,3,512]{2,0,1:T(2,128)} %param.10) | copy-start | bytes 36868
